TPU v7x, 32 devices: a whole 2x2x4 slice. The times are simulated.
32 devices in a mesh: ctx: 2 (over y), tp: 4 (over x, core), section: 4 (over z).
Axes of the slice: x: 2, y: 2, z: 4, core: 2. Of those that a mesh axis runs over, the one named last changes fastest.
Arguments:
- queries: bfloat16 [2, 1024, 8192], P(None, ('ctx', 'section'), 'tp'), may hold values from -15 to 15
- self_kv: bfloat16 [2, 1024, 2048], P(None, ('ctx', 'section')), may hold values from -6 to 6
- image_kv: bfloat16 [32, 2048], P(('ctx', 'tp', 'section')), may hold values from -6 to 6
- cross_gate: float32 [64], P('tp'), may hold values from 0.3 to 2
- lengths: int32 [2], replicated, may hold values from 256 to 1024, as said below
Outputs:
- attended: bfloat16 [2, 1024, 8192], P(None, ('ctx', 'section'), 'tp')
Inputs may be any that keep to these rules, and one draw needn't show every extreme that they name: `lengths`: one of the two sequences uses all 1024 positions, the other fewer.
All inputs are finite; a program needn't handle non-finite values.
Results may differ from a plain program's by a relative error of at most 0.004.
Values may be sent and summed in bfloat16 or wider, within the bound.
No kernel may reach another device: no remote copies, remote signals or barrier semaphores. Data moves between devices by JAX's collectives and lax.ppermute only.
A program may use at most 128 MiB of HBM per device.

v0:
```python
import math

import jax
import jax.numpy as jnp
from jax import lax
from jax.sharding import PartitionSpec as P

HQ = 64
KVH = 8
HEAD_SIZE = 128


neg_large = -1e30


def fold_block(carry_state, query_grid, key_matrix, value_matrix, allowed, score_form, value_form):
    row_best, row_total, weighted = carry_state
    logit_scores = jnp.einsum(
        score_form, query_grid, key_matrix, preferred_element_type=jnp.float32
    ) * (1.0 / math.sqrt(HEAD_SIZE))
    masked = jnp.where(allowed, logit_scores, neg_large)
    new_best = jnp.maximum(row_best, jnp.max(masked, axis=-1))
    weights = jnp.where(allowed, jnp.exp(masked - new_best[..., None]), 0.0)
    shrink = jnp.exp(row_best - new_best)
    row_total = row_total * shrink + jnp.sum(weights, axis=-1)
    weighted = weighted * shrink[..., None] + jnp.einsum(
        value_form, weights.astype(jnp.bfloat16), value_matrix, preferred_element_type=jnp.float32
    )
    return (new_best, row_total, weighted)


def finish(carry_state):
    return jnp.transpose(carry_state[2] / carry_state[1][..., None], (0, 3, 1, 2, 4))


def per_device(queries, self_kv, image_kv, cross_gate, lengths):
    tp_count = lax.axis_size("tp")
    heads_local = HQ // tp_count
    kv_local = max(1, KVH // tp_count)
    replicas = max(1, tp_count // KVH)
    heads_per_kv = heads_local // kv_local
    seq_rows = queries.shape[1]
    kv_cols = kv_local * 2 * HEAD_SIZE
    tp_rank = lax.axis_index("tp")
    own_pairs = lax.dynamic_slice_in_dim(self_kv, tp_rank // replicas * kv_cols, kv_cols, 2)
    query_grid = queries.reshape(2, seq_rows, kv_local, heads_per_kv, HEAD_SIZE)
    block_rank = lax.axis_index(("ctx", "section"))
    query_pos = block_rank * seq_rows + jnp.arange(seq_rows, dtype=jnp.int32)
    last_needed = jnp.minimum(block_rank * seq_rows + seq_rows - 1, jnp.max(lengths) - 1)
    start_state = (
        jnp.full((2, kv_local, heads_per_kv, seq_rows), neg_large, jnp.float32),
        jnp.zeros((2, kv_local, heads_per_kv, seq_rows), jnp.float32),
        jnp.zeros((2, kv_local, heads_per_kv, seq_rows, HEAD_SIZE), jnp.float32),
    )
    carry_state = start_state
    kv_piece = lax.all_gather(own_pairs, ("ctx", "section"), axis=1, tiled=True)
    row_count = kv_piece.shape[1]
    block_rows = math.gcd(row_count, 512)
    blocks = jnp.moveaxis(
        kv_piece.reshape(2, row_count // block_rows, block_rows, kv_local, 2, HEAD_SIZE), 1, 0
    )

    def self_one_block(inner_state, scan_item):
        block_number, block_pairs = scan_item
        block_first = block_number * block_rows
        key_pos = block_first + jnp.arange(block_rows, dtype=jnp.int32)
        allowed = (key_pos[None, None, :] <= query_pos[None, :, None]) & (
            key_pos[None, None, :] < lengths[:, None, None]
        )

        def compute_block(state_in):
            return fold_block(
                state_in,
                query_grid,
                block_pairs[:, :, :, 0],
                block_pairs[:, :, :, 1],
                allowed[:, None, None],
                "bsgrd,bpgd->bgrsp",
                "bgrsp,bpgd->bgrsd",
            )

        def keep_state(state_in):
            return state_in

        return (lax.cond(block_first > last_needed, keep_state, compute_block, inner_state), None)

    carry_state, _ = lax.scan(
        self_one_block, carry_state, (jnp.arange(row_count // block_rows, dtype=jnp.int32), blocks)
    )
    image_rows = image_kv.shape[0]
    copies = jnp.repeat(image_kv.reshape(image_rows, KVH // kv_local, kv_cols), replicas, axis=1)
    image_own = lax.all_to_all(
        copies.reshape(image_rows, tp_count * kv_cols),
        "tp",
        split_axis=1,
        concat_axis=0,
        tiled=True,
    )
    image_carry_state = start_state
    kv_piece = lax.all_gather(image_own, ("ctx", "section"), axis=0, tiled=True)
    row_count = kv_piece.shape[0]
    image_block_rows = math.gcd(row_count, 512)
    blocks = kv_piece.reshape(
        row_count // image_block_rows, image_block_rows, kv_local, 2, HEAD_SIZE
    )
    everywhere = jnp.ones((), jnp.bool_)

    def image_one_block(inner_state, block_pairs):
        return (
            fold_block(
                inner_state,
                query_grid,
                block_pairs[:, :, 0],
                block_pairs[:, :, 1],
                everywhere,
                "bsgrd,pgd->bgrsp",
                "bgrsp,pgd->bgrsd",
            ),
            None,
        )

    image_carry_state, _ = lax.scan(image_one_block, image_carry_state, blocks)
    gate_factor = jnp.tanh(cross_gate).reshape(1, 1, kv_local, heads_per_kv, 1)
    attended = finish(carry_state) + gate_factor * finish(image_carry_state)
    return attended.reshape(2, seq_rows, heads_local * HEAD_SIZE).astype(jnp.bfloat16)


def solution(mesh):
    placed = (
        P(None, ("ctx", "section"), "tp"),
        P(None, ("ctx", "section"), None),
        P(("ctx", "tp", "section"), None),
        P("tp"),
        P(),
    )
    return jax.shard_map(
        per_device,
        mesh=mesh,
        in_specs=placed,
        out_specs=P(None, ("ctx", "section"), "tp"),
        check_vma=False,
    )
```

profile of v0, /device:TPU:14, one launch (start us, length us, event | category | flops | bytes accessed | tf_op | source)
XLA Modules:
  0.0 104.2 jit_solution(13466147795451038210)
XLA Ops:
  6.5 1.2 %copy-done = bf16[2,128,2048]{2,1,0:T(8,128)(2,1)S(1)} copy-done((bf16[2,128,2048]{2,1,0:T(8,128)(2,1)S(1)}, bf16[2,128,2048]{2,1,0:T(8,128)(2,1)}, u32[]{:S(2)}) %copy-start) | copy-done | bytes 1048600
  7.8 0.7 constant_dynamic-slice_fusion
  8.5 0.0 all-gather.3.cloned.1.call-update
  8.5 0.5 broadcast.114
  9.0 1.4 %reduce.1 = bf16[4,512]{1,0:T(4,128)(2,1)S(1)} reduce(bf16[4,1,512]{2,1,0:T(2,128)(2,1)} %bitcast.82, bf16[]{:T(256)} %broadcast.114), dimensions={1}, to_apply=%bitcast.68.reduce_sub_computation | reduce | bytes 8194
  10.4 0.6 reshape.110
  11.0 3.8 %all-to-all-start = ((bf16[4,2,256]{2,1,0:T(2,128)(2,1)}), bf16[4,2,256]{2,1,0:T(2,128)(2,1)S(1)}, u32[]{:S(2)}, u32[]{:S(2)}) async-start(bf16[4,2,256]{2,1,0:T(2,128)(2,1)} %reshape.110), calls=%async_computation | async-start | bytes 8192 | tf_op jit(solution)/shard_map/all_to_all | solution.py:92
  14.8 0.7 tanh.3
  15.4 0.1 mul.81
  15.5 1.6 %copy.28 = bf16[2,128,2048]{1,2,0:T(8,128)(2,1)S(1)} copy(bf16[2,128,2048]{2,1,0:T(8,128)(2,1)} %param.9) | data formatting | bytes 2097152 | tf_op args[0]
  17.2 0.7 copy.32
  17.8 0.7 reduce_max.29
  19.2 30.0 %all-gather = bf16[1,32,512]{2,0,1:T(2,128)(2,1)S(1)} all-gather(bf16[1,4,512]{2,0,1:T(2,128)(2,1)S(1)} %bitcast.81), channel_id=2, replica_groups=mesh['ctx'=2,'tp'=4,'section'=4] {'ctx','section'}, dimensions={1}, use_global_device_ids=true | all-gather | bytes 36864 | tf_op jit(solution)/shard_map/all_gather | solution.py:100
  49.1 0.2 reduce
  49.3 0.1 fusion.24
  49.4 0.3 fusion.25
  49.7 0.8 copy-done.3
  50.5 0.1 fusion.20
  50.6 9.1 %all-gather.3.cloned.1.call-done = bf16[2,1024,512]{2,1,0:T(8,128)(2,1)} async-done(((bf16[2,128,512]{2,1,0:T(8,128)(2,1)}), bf16[2,1024,512]{2,1,0:T(8,128)(2,1)}) %all-gather.3.cloned.1.call-update) | async-done | bytes 2097168 | tf_op jit(solution)/shard_map/all_gather | solution.py:56
  59.7 4.0 %reshape.101 = bf16[2,2,512,2,2,128]{5,4,3,2,1,0:T(2,128)(2,1)} reshape(bf16[2,1024,512]{2,1,0:T(8,128)(2,1)} %all-gather.3.cloned.1.call-done) | data formatting | bytes 4194304 | tf_op jit(solution)/shard_map/reshape | solution.py:60
  63.7 3.3 %copy.31 = bf16[2,2,512,2,2,128]{5,2,3,1,4,0:T(8,128)(2,1)} copy(bf16[2,2,512,2,2,128]{5,4,3,2,0,1:T(2,128)(2,1)} %bitcast.79) | data formatting | bytes 4194304
  67.1 1.5 %broadcast_in_dim.50 = f32[2,2,8,128,128]{4,3,2,1,0:T(8,128)} broadcast(f32[]{:T(128)} %constant.74.clone.1), dimensions={} | broadcast | bytes 2097156 | tf_op jit(solution)/shard_map/broadcast_in_dim | solution.py:53
  68.6 22.1 %while.3 = (s32[]{:T(128)}, f32[2,2,8,128]{3,2,1,0:T(8,128)S(1)}, f32[2,2,8,128]{3,2,1,0:T(8,128)S(1)}, f32[2,2,8,128,128]{4,3,2,1,0:T(8,128)}, s32[2]{0:T(128)S...) while((s32[]{:T(128)}, f32[2,2,8,128]{3,2,1,0:T(8,128)S(1)}, ...), condition=%wide.region_6.7_spmd.clone, body=%wide.region_1.6_spmd.clone.sunk | while | flops 1102259840 | bytes 51263864 | solution.py:87
  68.6 0.6 dynamic_slice.21
  70.0 9.7 %conditional.3 = (f32[2,2,8,128]{3,2,1,0:T(8,128)S(1)}, f32[2,2,8,128]{3,2,1,0:T(8,128)S(1)}, f32[2,2,8,128,128]{4,3,2,1,0:T(8,128)}) conditional(s32[]{:T(128)} %convert_element_type.29, (s32[]{:T(128)}, s32[512]{0:T(512)S(1)}, s32[]{:T(128)}, s32[2]{0:T(128)S(1)}, bf16[2,2,512,2,2,128]{5,2,3,1,4,0:T(8,128)(2,1)}, /*index=5*/s32[]{:T(128)}, ...), branch_computations={%region_2.4_spmd, %region_5.5_spmd} | conditional | flops 1102259840 | bytes 51228260 | solution.py:85
  70.0 0.1 broadcast_compare_fusion.1
  70.1 0.1 broadcast_compare_fusion
  70.2 0.2 broadcast_and_fusion
  70.4 1.3 %dynamic-slice_bitcast_fusion = bf16[2,512,2,2,128]{4,1,2,0,3:T(8,128)(2,1)S(1)} fusion(bf16[2,2,512,2,2,128]{5,2,3,1,4,0:T(8,128)(2,1)} %get-tuple-element.131, s32[]{:T(128)} %get-tuple-element.132), kind=kLoop, calls=%fused_computation.9 | loop fusion | bytes 2097156 | tf_op jit(solution)/shard_map/while/body/jit(dynamic_index_in_dim)/squeeze | solution.py:87
  71.7 1.3 %fusion.2 = (f32[2,2,8,128]{3,2,1,0:T(8,128)S(1)}, f32[2,2,512,128,8]{3,2,4,1,0:T(8,128)S(1)}) fusion(pred[2,128,512]{1,2,0:T(8,128)(4,1)S(1)} %broadcast_and_fusion, bf16[2,128,2,8,128]{4,1,3,2,0:T(8,128)(2,1)S(1)} %get-tuple-element.133, bf16[2,512,2,2,128]{4,1,2,0,3:T(8,128)(2,1)S(1)} %dynamic-slice_bitcast_fusion), kind=kOutput, calls=%fused_computation.3 | convolution fusion | flops 543158272 | bytes 10108928 | tf_op jit(solution)/shard_map/while/body/eval_jaxpr/cond/branch_0_fun/bsgrd,bpgd->bgrsp/dot_general | solution.py:18
  73.1 0.0 copy-start.1
  73.1 2.0 %fusion.4 = f32[2,2,8,128]{3,2,1,0:T(8,128)S(1)} fusion(f32[2,2,512,128,8]{3,2,4,1,0:T(8,128)S(1)} %get-tuple-element.226, f32[2,2,8,128]{3,2,1,0:T(8,128)S(1)} %max.19, pred[2,128,512]{1,2,0:T(8,128)(4,1)S(1)} %broadcast_and_fusion), kind=kLoop, calls=%fused_computation.5 | loop fusion | flops 10481664 | bytes 8552448 | tf_op jit(solution)/shard_map/while/body/eval_jaxpr/cond/branch_0_fun/reduce_sum | solution.py:25
  75.1 3.2 %multiply_add_fusion = f32[2,2,8,128,128]{4,3,2,1,0:T(8,128)S(1)} fusion(f32[2,2,8,128,128]{4,3,2,1,0:T(8,128)S(1)} %copy-done.1, f32[2,2,512,128,8]{3,2,4,1,0:T(8,128)S(1)} %get-tuple-element.226, f32[2,2,8,128]{3,2,1,0:T(8,128)S(1)} %max.19, pred[2,128,512]{1,2,0:T(8,128)(4,1)S(1)} %broadcast_and_fusion, f32[2,2,8,128]{3,2,1,0:T(8,128)S(1)} %get-tuple-element.224, ...), kind=kOutput, calls=%fused_computation.8 | convolution fusion | flops 548405248 | bytes 13271040 | tf_op jit(solution)/shard_map/while/body/eval_jaxpr/cond/branch_0_fun/bgrsp,bpgd->bgrsd/dot_general | solution.py:26
  78.3 1.3 %copy-done.2 = f32[2,2,8,128,128]{4,3,2,1,0:T(8,128)} copy-done((f32[2,2,8,128,128]{4,3,2,1,0:T(8,128)}, f32[2,2,8,128,128]{4,3,2,1,0:T(8,128)S(1)}, u32[]{:S(2)}) %copy-start.2) | copy-done | bytes 2097176 | tf_op jit(solution)/shard_map/while/body/eval_jaxpr/cond
  79.6 0.6 dynamic_slice.21
  81.0 9.7 %conditional.3 = (f32[2,2,8,128]{3,2,1,0:T(8,128)S(1)}, f32[2,2,8,128]{3,2,1,0:T(8,128)S(1)}, f32[2,2,8,128,128]{4,3,2,1,0:T(8,128)}) conditional(s32[]{:T(128)} %convert_element_type.29, (s32[]{:T(128)}, s32[512]{0:T(512)S(1)}, s32[]{:T(128)}, s32[2]{0:T(128)S(1)}, bf16[2,2,512,2,2,128]{5,2,3,1,4,0:T(8,128)(2,1)}, /*index=5*/s32[]{:T(128)}, ...), branch_computations={%region_2.4_spmd, %region_5.5_spmd} | conditional | flops 1102259840 | bytes 51228260 | solution.py:85
  81.0 0.1 broadcast_compare_fusion.1
  81.1 0.1 broadcast_compare_fusion
  81.2 0.2 broadcast_and_fusion
  81.5 1.3 %dynamic-slice_bitcast_fusion = bf16[2,512,2,2,128]{4,1,2,0,3:T(8,128)(2,1)S(1)} fusion(bf16[2,2,512,2,2,128]{5,2,3,1,4,0:T(8,128)(2,1)} %get-tuple-element.131, s32[]{:T(128)} %get-tuple-element.132), kind=kLoop, calls=%fused_computation.9 | loop fusion | bytes 2097156 | tf_op jit(solution)/shard_map/while/body/jit(dynamic_index_in_dim)/squeeze | solution.py:87
  82.8 1.3 %fusion.2 = (f32[2,2,8,128]{3,2,1,0:T(8,128)S(1)}, f32[2,2,512,128,8]{3,2,4,1,0:T(8,128)S(1)}) fusion(pred[2,128,512]{1,2,0:T(8,128)(4,1)S(1)} %broadcast_and_fusion, bf16[2,128,2,8,128]{4,1,3,2,0:T(8,128)(2,1)S(1)} %get-tuple-element.133, bf16[2,512,2,2,128]{4,1,2,0,3:T(8,128)(2,1)S(1)} %dynamic-slice_bitcast_fusion), kind=kOutput, calls=%fused_computation.3 | convolution fusion | flops 543158272 | bytes 10108928 | tf_op jit(solution)/shard_map/while/body/eval_jaxpr/cond/branch_0_fun/bsgrd,bpgd->bgrsp/dot_general | solution.py:18
  84.1 2.0 %fusion.4 = f32[2,2,8,128]{3,2,1,0:T(8,128)S(1)} fusion(f32[2,2,512,128,8]{3,2,4,1,0:T(8,128)S(1)} %get-tuple-element.226, f32[2,2,8,128]{3,2,1,0:T(8,128)S(1)} %max.19, pred[2,128,512]{1,2,0:T(8,128)(4,1)S(1)} %broadcast_and_fusion), kind=kLoop, calls=%fused_computation.5 | loop fusion | flops 10481664 | bytes 8552448 | tf_op jit(solution)/shard_map/while/body/eval_jaxpr/cond/branch_0_fun/reduce_sum | solution.py:25
  86.2 3.2 %multiply_add_fusion = f32[2,2,8,128,128]{4,3,2,1,0:T(8,128)S(1)} fusion(f32[2,2,8,128,128]{4,3,2,1,0:T(8,128)S(1)} %copy-done.1, f32[2,2,512,128,8]{3,2,4,1,0:T(8,128)S(1)} %get-tuple-element.226, f32[2,2,8,128]{3,2,1,0:T(8,128)S(1)} %max.19, pred[2,128,512]{1,2,0:T(8,128)(4,1)S(1)} %broadcast_and_fusion, f32[2,2,8,128]{3,2,1,0:T(8,128)S(1)} %get-tuple-element.224, ...), kind=kOutput, calls=%fused_computation.8 | convolution fusion | flops 548405248 | bytes 13271040 | tf_op jit(solution)/shard_map/while/body/eval_jaxpr/cond/branch_0_fun/bgrsp,bpgd->bgrsd/dot_general | solution.py:26
  89.4 1.3 %copy-done.2 = f32[2,2,8,128,128]{4,3,2,1,0:T(8,128)} copy-done((f32[2,2,8,128,128]{4,3,2,1,0:T(8,128)}, f32[2,2,8,128,128]{4,3,2,1,0:T(8,128)S(1)}, u32[]{:S(2)}) %copy-start.2) | copy-done | bytes 2097176 | tf_op jit(solution)/shard_map/while/body/eval_jaxpr/cond
  90.7 3.0 %copy.34 = f32[2,2,8,128,128]{3,4,2,0,1:T(8,128)} copy(f32[2,2,8,128,128]{4,3,2,1,0:T(8,128)} %get-tuple-element.152) | data formatting | bytes 4194304 | tf_op jit(solution)/shard_map/while | solution.py:87
  93.7 2.3 %fusion.17 = bf16[2,128,2,8,128]{1,4,3,0,2:T(8,128)(2,1)S(1)} fusion(f32[2,2,8,128,128]{3,4,2,0,1:T(8,128)} %copy.34, f32[2,128,2,8]{1,3,0,2:T(8,128)S(1)} %bitcast_add_fusion.1, f32[2,128,2,8]{1,3,0,2:T(8,128)S(1)} %get-tuple-element.229, f32[2,8]{1,0:T(2,128)S(1)} %mul.81, f32[2,2,8,128,32]{3,4,2,0,1:T(8,128)S(1)} %copy-done.4, ...), kind=kOutput, calls=%fused_computation.27 | convolution fusion | flops 36962304 | bytes 3752000 | tf_op jit(solution)/shard_map/while/body/eval_jaxpr/bgrsp,pgd->bgrsd/dot_general | solution.py:26
  96.0 0.1 copy.38
  96.0 1.3 %copy.39 = bf16[2,128,2048]{2,1,0:T(8,128)(2,1)} copy(bf16[2,128,2048]{1,2,0:T(8,128)(2,1)S(1)} %bitcast.80) | data formatting | bytes 2097152 | tf_op jit(solution)/shard_map/convert_element_type | solution.py:125
  (34 shorter events, 0.2 us)
Async XLA Ops:
  6.5 1.2 %copy-start = (bf16[2,128,2048]{2,1,0:T(8,128)(2,1)S(1)}, bf16[2,128,2048]{2,1,0:T(8,128)(2,1)}, u32[]{:S(2)}) copy-start(bf16[2,128,2048]{2,1,0:T(8,128)(2,1)} %param.10) | copy-start | bytes 3145732
  6.5 53.2 %all-gather.3.cloned.1.call-start = ((), (), s32[]{:S(2)}) async-start(), calls=%async_computation.1 | async-start | bytes 2359296 | tf_op jit(solution)/shard_map/all_gather | solution.py:56
  11.0 8.1 %all-to-all-start = ((bf16[4,2,256]{2,1,0:T(2,128)(2,1)}), bf16[4,2,256]{2,1,0:T(2,128)(2,1)S(1)}, u32[]{:S(2)}, u32[]{:S(2)}) async-start(bf16[4,2,256]{2,1,0:T(2,128)(2,1)} %reshape.110), calls=%async_computation | async-start | bytes 8192 | tf_op jit(solution)/shard_map/all_to_all | solution.py:92
  15.5 2.3 %copy-start.5 = (s32[2]{0:T(128)S(1)}, s32[2]{0:T(128)}, u32[]{:S(2)}) copy-start(s32[2]{0:T(128)} %param.13) | copy-start | bytes 28
  49.7 0.8 copy-start.3
  73.1 2.1 %copy-start.1 = (f32[2,2,8,128,128]{4,3,2,1,0:T(8,128)S(1)}, f32[2,2,8,128,128]{4,3,2,1,0:T(8,128)}, u32[]{:S(2)}) copy-start(f32[2,2,8,128,128]{4,3,2,1,0:T(8,128)} %get-tuple-element.135) | copy-start | bytes 6291460 | tf_op jit(solution)/shard_map/while/body/eval_jaxpr/cond
  78.3 1.3 %copy-start.2 = (f32[2,2,8,128,128]{4,3,2,1,0:T(8,128)}, f32[2,2,8,128,128]{4,3,2,1,0:T(8,128)S(1)}, u32[]{:S(2)}) copy-start(f32[2,2,8,128,128]{4,3,2,1,0:T(8,128)S(1)} %multiply_add_fusion) | copy-start | bytes 6291460 | tf_op jit(solution)/shard_map/while/body/eval_jaxpr/cond
  84.1 2.1 %copy-start.1 = (f32[2,2,8,128,128]{4,3,2,1,0:T(8,128)S(1)}, f32[2,2,8,128,128]{4,3,2,1,0:T(8,128)}, u32[]{:S(2)}) copy-start(f32[2,2,8,128,128]{4,3,2,1,0:T(8,128)} %get-tuple-element.135) | copy-start | bytes 6291460 | tf_op jit(solution)/shard_map/while/body/eval_jaxpr/cond
  89.4 1.3 %copy-start.2 = (f32[2,2,8,128,128]{4,3,2,1,0:T(8,128)}, f32[2,2,8,128,128]{4,3,2,1,0:T(8,128)S(1)}, u32[]{:S(2)}) copy-start(f32[2,2,8,128,128]{4,3,2,1,0:T(8,128)S(1)} %multiply_add_fusion) | copy-start | bytes 6291460 | tf_op jit(solution)/shard_map/while/body/eval_jaxpr/cond
  90.7 3.0 %copy-start.4 = (f32[2,2,8,128,32]{3,4,2,0,1:T(8,128)S(1)}, f32[2,2,8,128,32]{3,4,2,0,1:T(8,128)}, u32[]{:S(2)}) copy-start(f32[2,2,8,128,32]{3,4,2,0,1:T(8,128)} %copy-done.3) | copy-start | bytes 1572868
Sparse Core Ops, SparseCore 0:
  9.5 50.1 all-gather.2
where the time goes:
time: 105 us; the launch traced here: 104 us
  blocking collectives  30 us (29%)
  local copies, waits for them, and re-layouts  26.7 us (25%)
  between operations  14.1 us (13%)
  matrix products  11.6 us (11%)
  waiting for transfers between devices  9.15 us (9%)
  other arithmetic  7.28 us (7%)
  starting transfers between devices  3.75 us (4%)
  loops' own time  1.64 us (2%)
    all_gather x1, blocking collectives, per_device(): kv_piece = lax.all_gather(image_own, ('ctx', 'section'), axis=0, tiled=True)  30 us
    all_gather x1, waiting for transfers between devices, per_device(): kv_piece = lax.all_gather(own_pairs, ('ctx', 'section'), axis=1, tiled=True)  9.13 us
    unnamed x14, local copies, waits for them, and re-layouts  8.77 us
    dot_general x3, matrix products, fold_block(): jnp.einsum(value_form, weights.astype(jnp.bfloat16), value_matrix, prefer...  8.66 us
    reduce_sum x3, other arithmetic, fold_block(): row_total = row_total * shrink + jnp.sum(weights, axis=-1)  4.16 us
    reshape x1, local copies, waits for them, and re-layouts, per_device(): kv_piece.reshape(2, row_count // block_rows, block_rows, kv_local, 2, HEA...  3.98 us
    all_to_all x1, starting transfers between devices, per_device(): lax.all_to_all(copies.reshape(image_rows, tp_count * kv_cols), 'tp', spli...  3.75 us
    while x1, local copies, waits for them, and re-layouts, per_device(): lax.scan(self_one_block, carry_state, (jnp.arange(row_count // block_rows...  3.01 us
  transfers between devices with their start and end apart: 2, of which 1 were waited for; matrix products, arithmetic and copies ran while one was open for 7% of the time, Pallas kernels for 0%

commit v1 on v0

--- a/solution.py
+++ b/solution.py
@@ -1,8 +1,11 @@
+import functools
 import math
 
 import jax
 import jax.numpy as jnp
 from jax import lax
+from jax.experimental import pallas as pl
+from jax.experimental.pallas import tpu as pltpu
 from jax.sharding import PartitionSpec as P
 
 HQ = 64
@@ -33,7 +36,7 @@
     return jnp.transpose(carry_state[2] / carry_state[1][..., None], (0, 3, 1, 2, 4))
 
 
-def per_device(queries, self_kv, image_kv, cross_gate, lengths):
+def scan_device(queries, self_kv, image_kv, cross_gate, lengths):
     tp_count = lax.axis_size("tp")
     heads_local = HQ // tp_count
     kv_local = max(1, KVH // tp_count)
@@ -125,6 +128,112 @@
     return attended.reshape(2, seq_rows, heads_local * HEAD_SIZE).astype(jnp.bfloat16)
 
 
+NEG=-1e30
+C2=math.log2(math.e)/math.sqrt(HEAD_SIZE)
+
+def nt(a,b): return lax.dot_general(a,b,(((1,),(1,)),((),())),preferred_element_type=jnp.float32)
+def nn(a,b): return lax.dot_general(a,b,(((1,),(0,)),((),())),preferred_element_type=jnp.float32)
+
+def full_kernel(nblk, heads, rows, chunk, meta, gate, *refs):
+    q_ref=refs[0]; blocks=refs[1:1+nblk]; img_ref=refs[1+nblk]; out_ref=refs[2+nblk]
+    b=pl.program_id(0); g=pl.program_id(1)
+    limit=meta[nblk+b]
+    ki=lax.broadcasted_iota(jnp.int32,(1,rows),1)
+    bias=[jnp.where(meta[i]+ki<limit,0.0,NEG) for i in range(nblk)]
+    tri=lax.broadcasted_iota(jnp.int32,(rows,rows),1)<=lax.broadcasted_iota(jnp.int32,(rows,rows),0)
+    own_bias=jnp.where(tri,bias[0],NEG)
+    keys=jnp.concatenate([r[0,:,:HEAD_SIZE] for r in blocks],0)
+    ones=jnp.ones((rows*nblk,HEAD_SIZE),jnp.bfloat16)
+    vals=jnp.concatenate([jnp.concatenate([r[0,:,HEAD_SIZE:] for r in blocks],0),ones],1)
+    n_img=img_ref.shape[0]
+    ik=img_ref[:,:HEAD_SIZE]; iv=jnp.concatenate([img_ref[:,HEAD_SIZE:],jnp.ones((n_img,HEAD_SIZE),jnp.bfloat16)],1)
+    for h0 in range(0,heads,chunk):
+        qs=jnp.concatenate([q_ref[0,:,(h0+j)*HEAD_SIZE:(h0+j+1)*HEAD_SIZE] for j in range(chunk)],0)
+        s=nt(qs,keys)
+        si=nt(qs,ik)
+        cols=[]
+        for i in range(nblk):
+            si_=s[:,i*rows:(i+1)*rows]
+            if i==0: cols.append((si_.reshape(chunk,rows,rows)+own_bias[None]).reshape(chunk*rows,rows))
+            else: cols.append(si_+bias[i])
+        m=functools.reduce(jnp.maximum,cols)
+        m=jnp.max(m,axis=1,keepdims=True)
+        p=jnp.concatenate([jnp.exp2((c-m)*C2).astype(jnp.bfloat16) for c in cols],1)
+        o=nn(p,vals)
+        pi=jnp.exp2((si-jnp.max(si,axis=1,keepdims=True))*C2).astype(jnp.bfloat16)
+        oi=nn(pi,iv)
+        so=o[:,:HEAD_SIZE]/o[:,HEAD_SIZE:]
+        co=oi[:,:HEAD_SIZE]/oi[:,HEAD_SIZE:]
+        for j in range(chunk):
+            gf=jnp.tanh(jnp.full((1,HEAD_SIZE),gate[g*heads+h0+j],jnp.float32))
+            out_ref[0,:,(h0+j)*HEAD_SIZE:(h0+j+1)*HEAD_SIZE]=(so[j*rows:(j+1)*rows]+gf*co[j*rows:(j+1)*rows]).astype(jnp.bfloat16)
+
+def attend_all(meta, gate, q, blocks, img, chunk=2):
+    nb,rows,qc=q.shape
+    kvl=blocks[0].shape[2]//(2*HEAD_SIZE)
+    heads=qc//HEAD_SIZE//kvl
+    nblk=len(blocks)
+    blk=pl.BlockSpec((1,rows,2*HEAD_SIZE),lambda b,g,m,t: (b,0,g))
+    qspec=pl.BlockSpec((1,rows,heads*HEAD_SIZE),lambda b,g,m,t:(b,0,g))
+    grid_spec=pltpu.PrefetchScalarGridSpec(num_scalar_prefetch=2,grid=(nb,kvl),
+        in_specs=[qspec]+[blk]*nblk+[pl.BlockSpec((img.shape[0],2*HEAD_SIZE),lambda b,g,m,t:(0,m[nblk+nb]*kvl+g))],
+        out_specs=qspec)
+    return pl.pallas_call(functools.partial(full_kernel,nblk,heads,rows,chunk),grid_spec=grid_spec,
+        out_shape=jax.ShapeDtypeStruct(q.shape,jnp.bfloat16),
+        compiler_params=pltpu.CompilerParams(vmem_limit_bytes=48<<20,dimension_semantics=("arbitrary","arbitrary")),
+        name="attend")(meta,gate,q,*blocks,img)
+
+def section_shift(block, step):
+    count = lax.axis_size("section")
+    return lax.ppermute(block, "section", [(z, (z + step) % count) for z in range(count)])
+
+
+def ctx_swap(block):
+    return lax.ppermute(block, "ctx", [(0, 1), (1, 0)])
+
+
+def after(block, *others):
+    return lax.optimization_barrier((block,) + others)[0]
+
+
+def gather_rows(rows):
+    for name in ("ctx", "section", "tp"):
+        count = lax.axis_size(name)
+        step = 1
+        while step < count:
+            other = lax.ppermute(rows, name, [(i, i ^ step) for i in range(count)])
+            rows = jnp.concatenate([rows, other], 0)
+            step *= 2
+    return rows
+
+
+def ring_device(queries, self_kv, image_kv, cross_gate, lengths):
+    tp_count = lax.axis_size("tp")
+    kv_local = KVH // tp_count
+    seq_rows = queries.shape[1]
+    kv_cols = kv_local * 2 * HEAD_SIZE
+    tp_rank = lax.axis_index("tp")
+    ctx = lax.axis_index("ctx")
+    section = lax.axis_index("section")
+    own = lax.dynamic_slice_in_dim(self_kv, tp_rank * kv_cols, kv_cols, 2)
+    image = gather_rows(image_kv)
+    r1 = section_shift(own, 1)
+    y0 = ctx_swap(own)
+    r3 = section_shift(after(own, r1), 3)
+    y1 = ctx_swap(after(r1, y0))
+    r2 = section_shift(after(r1, r3), 1)
+    y3 = ctx_swap(after(r3, y1))
+    y2 = ctx_swap(after(r2, y3))
+    never = jnp.int32(1 << 30)
+    firsts = [(ctx * 4 + section) * seq_rows]
+    for k in (1, 2, 3):
+        firsts.append(jnp.where(section >= k, (ctx * 4 + section - k) * seq_rows, never))
+    for k in (0, 1, 2, 3):
+        firsts.append(jnp.where(ctx == 1, (section - k) % 4 * seq_rows, never))
+    meta = jnp.concatenate([jnp.stack(firsts), lengths, tp_rank[None]]).astype(jnp.int32)
+    return attend_all(meta, cross_gate, queries, [own, r1, r2, r3, y0, y1, y2, y3], image, chunk=4)
+
+
 def solution(mesh):
     placed = (
         P(None, ("ctx", "section"), "tp"),
@@ -133,8 +242,9 @@
         P("tp"),
         P(),
     )
+    few = mesh.shape["ctx"] == 2 and mesh.shape["section"] == 4 and mesh.shape["tp"] == 4
     return jax.shard_map(
-        per_device,
+        ring_device if few else scan_device,
         mesh=mesh,
         in_specs=placed,
         out_specs=P(None, ("ctx", "section"), "tp"),

time: 105 us -> 54.6 us (0.52)
  the two profiles are of different devices: /device:TPU:14 before, /device:TPU:0 now
where the time goes in v1:
time: 54.6 us; the launch traced here: 54.2 us
  waiting for transfers between devices  21.9 us (40%)
  starting transfers between devices  13.7 us (25%)
  Pallas kernels  11 us (20%)
  local copies, waits for them, and re-layouts  6.64 us (12%)
  other arithmetic  0.8 us (1%)
    pallas_call x1, Pallas kernels, attend_all(): pl.pallas_call(functools.partial(full_kernel, nblk, heads, rows, chunk),...  11 us
    ppermute x3, waiting for transfers between devices, section_shift(): lax.ppermute(block, 'section', [(z, (z + step) % count) for z in range(co...  10.5 us
    ppermute x5, waiting for transfers between devices, gather_rows(): other = lax.ppermute(rows, name, [(i, i ^ step) for i in range(count)])  10.1 us
    ppermute x3, starting transfers between devices, section_shift(): lax.ppermute(block, 'section', [(z, (z + step) % count) for z in range(co...  4.82 us
    ppermute x4, starting transfers between devices, ctx_swap(): return lax.ppermute(block, 'ctx', [(0, 1), (1, 0)])  4.57 us
    ppermute x5, starting transfers between devices, gather_rows(): other = lax.ppermute(rows, name, [(i, i ^ step) for i in range(count)])  4.33 us
    unnamed x20, local copies, waits for them, and re-layouts  3.42 us
    concatenate x2, local copies, waits for them, and re-layouts, gather_rows(): rows = jnp.concatenate([rows, other], 0)  2.46 us
  transfers between devices with their start and end apart: 12, of which 7 were waited for; matrix products, arithmetic and copies ran while one was open for 7% of the time, Pallas kernels for 0%

profile of v1, /device:TPU:0, one launch (start us, length us, event | category | flops | bytes accessed | tf_op | source)
XLA Modules:
  0.0 54.2 jit_solution(18210679425085624363)
XLA Ops:
  0.0 0.0 copy-start
  0.0 0.0 copy-start.5
  0.0 0.0 copy-start.1
  0.0 1.2 %copy-done = bf16[2,128,2048]{2,1,0:T(8,128)(2,1)S(1)} copy-done((bf16[2,128,2048]{2,1,0:T(8,128)(2,1)S(1)}, bf16[2,128,2048]{2,1,0:T(8,128)(2,1)}, u32[]{:S(2)}) %copy-start) | copy-done | bytes 1048600
  1.2 3.1 %collective-permute-start = (bf16[2,128,512]{2,1,0:T(8,128)(2,1)S(1)}, bf16[2,128,512]{2,1,0:T(8,128)(2,1)S(1)}, u32[]{:S(2)}, u32[]{:S(2)}) collective-permute-start(bf16[2,128,512]{2,1,0:T(8,128)(2,1)S(1)} %constant_dynamic-slice_fusion.refs_1_), channel_id=1, source_target_pairs={{0,1},{1,2},{2,3},{3,0},{4,5},{5,6},{6,7},{7,4},{8,9},{9,10},{10,1... | collective-permute-start | bytes 786440 | tf_op jit(solution)/shard_map/ppermute | solution.py:188
  4.3 1.5 %collective-permute-start.3 = (bf16[2,128,512]{2,1,0:T(8,128)(2,1)S(1)}, bf16[2,128,512]{2,1,0:T(8,128)(2,1)S(1)}, u32[]{:S(2)}, u32[]{:S(2)}) collective-permute-start(bf16[2,128,512]{2,1,0:T(8,128)(2,1)S(1)} %constant_dynamic-slice_fusion.refs_1_), channel_id=1, source_target_pairs={{0,16},{16,0},{1,17},{17,1},{2,18},{18,2},{3,19},{19,3},{4,20},{20... | collective-permute-start | bytes 786440 | tf_op jit(solution)/shard_map/ppermute | solution.py:192
  5.8 6.8 %collective-permute-done.refs_2_ = bf16[2,128,512]{2,1,0:T(8,128)(2,1)S(1)} collective-permute-done((bf16[2,128,512]{2,1,0:T(8,128)(2,1)S(1)}, bf16[2,128,512]{2,1,0:T(8,128)(2,1)S(1)}, u32[]{:S(2)}, u32[]{:S(2)}) %collective-permute-start) | collective-permute-done | bytes 262176 | tf_op jit(solution)/shard_map/ppermute | solution.py:188
  12.7 1.7 %collective-permute-start.1 = (bf16[2,128,512]{2,1,0:T(8,128)(2,1)S(1)}, bf16[2,128,512]{2,1,0:T(8,128)(2,1)S(1)}, u32[]{:S(2)}, u32[]{:S(2)}) collective-permute-start(bf16[2,128,512]{2,1,0:T(8,128)(2,1)S(1)} %constant_dynamic-slice_fusion.refs_1_), channel_id=1, source_target_pairs={{0,3},{1,0},{2,1},{3,2},{4,7},{5,4},{6,5},{7,6},{8,11},{9,8},{10,9... | collective-permute-start | bytes 786440 | tf_op jit(solution)/shard_map/ppermute | solution.py:188
  14.4 0.0 collective-permute-done.3.refs_5_
  14.4 1.5 %collective-permute-start.4 = (bf16[2,128,512]{2,1,0:T(8,128)(2,1)S(1)}, bf16[2,128,512]{2,1,0:T(8,128)(2,1)S(1)}, u32[]{:S(2)}, u32[]{:S(2)}) collective-permute-start(bf16[2,128,512]{2,1,0:T(8,128)(2,1)S(1)} %collective-permute-done.refs_2_), channel_id=1, source_target_pairs={{0,16},{16,0},{1,17},{17,1},{2,18},{18,2},{3,19},{19,3},{4,20},{20... | collective-permute-start | bytes 786440 | tf_op jit(solution)/shard_map/ppermute | solution.py:192
  15.9 0.5 collective-permute-start.7
  16.4 3.7 %collective-permute-done.1.refs_4_ = bf16[2,128,512]{2,1,0:T(8,128)(2,1)S(1)} collective-permute-done((bf16[2,128,512]{2,1,0:T(8,128)(2,1)S(1)}, bf16[2,128,512]{2,1,0:T(8,128)(2,1)S(1)}, u32[]{:S(2)}, u32[]{:S(2)}) %collective-permute-start.1) | collective-permute-done | bytes 262176 | tf_op jit(solution)/shard_map/ppermute | solution.py:188
  20.1 0.0 collective-permute-start.2
  20.2 1.2 %collective-permute-done.4.refs_6_ = bf16[2,128,512]{2,1,0:T(8,128)(2,1)S(1)} collective-permute-done((bf16[2,128,512]{2,1,0:T(8,128)(2,1)S(1)}, bf16[2,128,512]{2,1,0:T(8,128)(2,1)S(1)}, u32[]{:S(2)}, u32[]{:S(2)}) %collective-permute-start.4) | collective-permute-done | bytes 262176 | tf_op jit(solution)/shard_map/ppermute | solution.py:192
  21.4 1.5 %collective-permute-start.5 = (bf16[2,128,512]{2,1,0:T(8,128)(2,1)S(1)}, bf16[2,128,512]{2,1,0:T(8,128)(2,1)S(1)}, u32[]{:S(2)}, u32[]{:S(2)}) collective-permute-start(bf16[2,128,512]{2,1,0:T(8,128)(2,1)S(1)} %collective-permute-done.1.refs_4_), channel_id=1, source_target_pairs={{0,16},{16,0},{1,17},{17,1},{2,18},{18,2},{3,19},{19,3},{4,20},{20... | collective-permute-start | bytes 786440 | tf_op jit(solution)/shard_map/ppermute | solution.py:192
  22.9 0.0 collective-permute-done.7
  22.9 0.0 copy-start.6
  22.9 0.7 %pad_maximum_fusion.2 = bf16[2,2048]{1,0:T(2,128)(2,1)S(1)} fusion(bf16[1,2048]{1,0:T(2,128)(2,1)S(1)} %collective-permute-done.7, bf16[1,2048]{1,0:T(2,128)(2,1)} %param.7), kind=kLoop, calls=%fused_computation.2 | loop fusion | flops 16384 | bytes 16384 | tf_op jit(solution)/shard_map/concatenate | solution.py:205
  23.6 0.4 collective-permute-start.8
  24.1 4.6 %collective-permute-done.8 = bf16[2,2048]{1,0:T(2,128)(2,1)S(1)} collective-permute-done((bf16[2,2048]{1,0:T(2,128)(2,1)S(1)}, bf16[2,2048]{1,0:T(2,128)(2,1)S(1)}, u32[]{:S(2)}, u32[]{:S(2)}) %collective-permute-start.8) | collective-permute-done | bytes 8224 | tf_op jit(solution)/shard_map/ppermute | solution.py:204
  28.7 0.0 copy-done.5
  28.7 0.0 copy-start.9
  28.8 1.9 %collective-permute-start.9 = (bf16[4,2048]{1,0:T(4,128)(2,1)S(1)}, bf16[4,2048]{1,0:T(4,128)(2,1)S(1)}, u32[]{:S(2)}, u32[]{:S(2)}) collective-permute-start(bf16[4,2048]{1,0:T(4,128)(2,1)S(1)} %pad_maximum_fusion.1), channel_id=1, source_target_pairs={{0,2},{1,3},{2,0},{3,1},{4,6},{5,7},{6,4},{7,5},{8,10},{9,11},{10,... | collective-permute-start | bytes 49160 | tf_op jit(solution)/shard_map/ppermute | solution.py:204
  30.6 0.0 collective-permute-done.2.refs_3_
  30.6 0.0 collective-permute-done.5.refs_8_
  30.6 0.0 copy-start.2
  30.6 0.7 %copy-done.2 = bf16[2,128,512]{2,1,0:T(8,128)(2,1)} copy-done((bf16[2,128,512]{2,1,0:T(8,128)(2,1)}, bf16[2,128,512]{2,1,0:T(8,128)(2,1)S(1)}, u32[]{:S(2)}) %copy-start.2) | copy-done | bytes 262168
  31.3 0.0 collective-permute-start.6
  31.4 2.1 %collective-permute-done.9 = bf16[4,2048]{1,0:T(4,128)(2,1)S(1)} collective-permute-done((bf16[4,2048]{1,0:T(4,128)(2,1)S(1)}, bf16[4,2048]{1,0:T(4,128)(2,1)S(1)}, u32[]{:S(2)}, u32[]{:S(2)}) %collective-permute-start.9) | collective-permute-done | bytes 16416 | tf_op jit(solution)/shard_map/ppermute | solution.py:204
  33.5 0.0 copy-start.7
  33.5 0.1 collective-permute-start.10
  33.6 1.2 %collective-permute-done.10 = bf16[8,2048]{1,0:T(8,128)(2,1)S(1)} collective-permute-done((bf16[8,2048]{1,0:T(8,128)(2,1)S(1)}, bf16[8,2048]{1,0:T(8,128)(2,1)S(1)}, u32[]{:S(2)}, u32[]{:S(2)}) %collective-permute-start.10) | collective-permute-done | bytes 32800 | tf_op jit(solution)/shard_map/ppermute | solution.py:204
  34.8 0.0 copy-done.6
  34.8 0.0 copy-done.9
  34.8 0.0 copy-done.7
  34.8 0.0 copy-start.8
  34.8 0.1 concatenate.26
  34.9 0.5 copy-done.8
  35.4 1.5 %collective-permute-start.11 = (bf16[16,2048]{1,0:T(8,128)(2,1)S(1)}, bf16[16,2048]{1,0:T(8,128)(2,1)}, u32[]{:S(2)}, u32[]{:S(2)}) collective-permute-start(bf16[16,2048]{1,0:T(8,128)(2,1)S(1)} %concatenate.26), channel_id=1, source_target_pairs={{0,8},{4,12},{8,0},{12,4},{1,9},{5,13},{9,1},{13,5},{2,10},{6,14},... | collective-permute-start | bytes 196616 | tf_op jit(solution)/shard_map/ppermute | solution.py:204
  36.8 0.7 %concatenate.22.meta = s32[11]{0:T(128)S(1)} concatenate(s32[1]{0:T(128)} %bitcast, s32[1]{0:T(128)} %bitcast.1, s32[1]{0:T(128)} %bitcast.2, s32[1]{0:T(128)} %bitcast.3, s32[1]{0:T(128)} %bitcast.4, s32[1]{0:T(128)} %bitcast.5, s32[1]{0:T(128)} %bitcast.6, s32[1]{0:T(128)} %bitcast.7, s32[2]{0:T(128)} %param.9, s32[1]{0:T(128)} %bitcast.8), dimensions={0} | concatenate | bytes 88 | tf_op jit(solution)/shard_map/concatenate | solution.py:233
  37.6 2.2 %collective-permute-done.11 = bf16[16,2048]{1,0:T(8,128)(2,1)} collective-permute-done((bf16[16,2048]{1,0:T(8,128)(2,1)S(1)}, bf16[16,2048]{1,0:T(8,128)(2,1)}, u32[]{:S(2)}, u32[]{:S(2)}) %collective-permute-start.11) | collective-permute-done | bytes 65568 | tf_op jit(solution)/shard_map/ppermute | solution.py:204
  39.8 2.4 %concatenate.27.refs_9_ = bf16[32,2048]{1,0:T(8,128)(2,1)S(1)} concatenate(bf16[1,2048]{1,0:T(2,128)(2,1)S(1)} %copy-done.5, bf16[1,2048]{1,0:T(2,128)(2,1)} %copy-done.6, bf16[2,2048]{1,0:T(2,128)(2,1)} %copy-done.9, bf16[4,2048]{1,0:T(4,128)(2,1)} %copy-done.7, bf16[8,2048]{1,0:T(8,128)(2,1)} %copy-done.8, bf16[16,2048]{1,0:T(8,128)(2,1)} %collective-permute-done.11), dimensions={0} | concatenate | bytes 262144 | tf_op jit(solution)/shard_map/concatenate | solution.py:205
  42.2 0.0 collective-permute-done.6.refs_7_
  42.2 0.0 copy-done.1
  42.2 0.0 copy-done.4
  42.2 0.0 copy-start.3
  42.2 0.9 %copy-done.3 = bf16[2,128,512]{2,1,0:T(8,128)(2,1)S(1)} copy-done((bf16[2,128,512]{2,1,0:T(8,128)(2,1)S(1)}, bf16[2,128,512]{2,1,0:T(8,128)(2,1)}, u32[]{:S(2)}) %copy-start.3) | copy-done | bytes 262168
  43.1 11.0 %attend.1 = bf16[2,128,2048]{2,1,0:T(8,128)(2,1)} custom-call(s32[11]{0:T(128)S(1)} %concatenate.22.meta, f32[16]{0:T(128)S(1)} %copy-done.4, bf16[2,128,2048]{2,1,0:T(8,128)(2,1)S(1)} %copy-done.1, bf16[2,128,512]{2,1,0:T(8,128)(2,1)S(1)} %constant_dynamic-slice_fusion.refs_1_, bf16[2,128,512]{2,1,0:T(8,128)(2,1)S(1)} %collective-permute-done.refs_2_, ...), custom_call_target="tpu_custom_call" | custom-call | tf_op jit(solution)/shard_map/attend/pallas_call | solution.py:181
  (4 shorter events, 0.1 us)
Async XLA Ops:
  0.0 1.2 %copy-start = (bf16[2,128,2048]{2,1,0:T(8,128)(2,1)S(1)}, bf16[2,128,2048]{2,1,0:T(8,128)(2,1)}, u32[]{:S(2)}) copy-start(bf16[2,128,2048]{2,1,0:T(8,128)(2,1)} %param.6) | copy-start | bytes 3145732
  0.0 28.7 %copy-start.5 = (bf16[1,2048]{1,0:T(2,128)(2,1)S(1)}, bf16[1,2048]{1,0:T(2,128)(2,1)}, u32[]{:S(2)}) copy-start(bf16[1,2048]{1,0:T(2,128)(2,1)} %param.7) | copy-start | bytes 12292
  0.0 42.2 %copy-start.1 = (bf16[2,128,2048]{2,1,0:T(8,128)(2,1)S(1)}, bf16[2,128,2048]{2,1,0:T(8,128)(2,1)}, u32[]{:S(2)}) copy-start(bf16[2,128,2048]{2,1,0:T(8,128)(2,1)} %refs_0_.1) | copy-start | bytes 3145732
  1.2 11.4 %collective-permute-start = (bf16[2,128,512]{2,1,0:T(8,128)(2,1)S(1)}, bf16[2,128,512]{2,1,0:T(8,128)(2,1)S(1)}, u32[]{:S(2)}, u32[]{:S(2)}) collective-permute-start(bf16[2,128,512]{2,1,0:T(8,128)(2,1)S(1)} %constant_dynamic-slice_fusion.refs_1_), channel_id=1, source_target_pairs={{0,1},{1,2},{2,3},{3,0},{4,5},{5,6},{6,7},{7,4},{8,9},{9,10},{10,1... | collective-permute-start | bytes 786440 | tf_op jit(solution)/shard_map/ppermute | solution.py:188
  4.3 10.1 %collective-permute-start.3 = (bf16[2,128,512]{2,1,0:T(8,128)(2,1)S(1)}, bf16[2,128,512]{2,1,0:T(8,128)(2,1)S(1)}, u32[]{:S(2)}, u32[]{:S(2)}) collective-permute-start(bf16[2,128,512]{2,1,0:T(8,128)(2,1)S(1)} %constant_dynamic-slice_fusion.refs_1_), channel_id=1, source_target_pairs={{0,16},{16,0},{1,17},{17,1},{2,18},{18,2},{3,19},{19,3},{4,20},{20... | collective-permute-start | bytes 786440 | tf_op jit(solution)/shard_map/ppermute | solution.py:192
  12.7 7.5 %collective-permute-start.1 = (bf16[2,128,512]{2,1,0:T(8,128)(2,1)S(1)}, bf16[2,128,512]{2,1,0:T(8,128)(2,1)S(1)}, u32[]{:S(2)}, u32[]{:S(2)}) collective-permute-start(bf16[2,128,512]{2,1,0:T(8,128)(2,1)S(1)} %constant_dynamic-slice_fusion.refs_1_), channel_id=1, source_target_pairs={{0,3},{1,0},{2,1},{3,2},{4,7},{5,4},{6,5},{7,6},{8,11},{9,8},{10,9... | collective-permute-start | bytes 786440 | tf_op jit(solution)/shard_map/ppermute | solution.py:188
  14.4 7.0 %collective-permute-start.4 = (bf16[2,128,512]{2,1,0:T(8,128)(2,1)S(1)}, bf16[2,128,512]{2,1,0:T(8,128)(2,1)S(1)}, u32[]{:S(2)}, u32[]{:S(2)}) collective-permute-start(bf16[2,128,512]{2,1,0:T(8,128)(2,1)S(1)} %collective-permute-done.refs_2_), channel_id=1, source_target_pairs={{0,16},{16,0},{1,17},{17,1},{2,18},{18,2},{3,19},{19,3},{4,20},{20... | collective-permute-start | bytes 786440 | tf_op jit(solution)/shard_map/ppermute | solution.py:192
  15.9 7.0 %collective-permute-start.7 = (bf16[1,2048]{1,0:T(2,128)(2,1)}, bf16[1,2048]{1,0:T(2,128)(2,1)S(1)}, u32[]{:S(2)}, u32[]{:S(2)}) collective-permute-start(bf16[1,2048]{1,0:T(2,128)(2,1)} %param.7), channel_id=1, source_target_pairs={{0,16},{16,0},{1,17},{17,1},{2,18},{18,2},{3,19},{19,3},{4,20},{20... | collective-permute-start | bytes 12296 | tf_op jit(solution)/shard_map/ppermute | solution.py:204
  20.1 10.5 %collective-permute-start.2 = (bf16[2,128,512]{2,1,0:T(8,128)(2,1)S(1)}, bf16[2,128,512]{2,1,0:T(8,128)(2,1)}, u32[]{:S(2)}, u32[]{:S(2)}) collective-permute-start(bf16[2,128,512]{2,1,0:T(8,128)(2,1)S(1)} %collective-permute-done.refs_2_), channel_id=1, source_target_pairs={{0,1},{1,2},{2,3},{3,0},{4,5},{5,6},{6,7},{7,4},{8,9},{9,10},{10,1... | collective-permute-start | bytes 786440 | tf_op jit(solution)/shard_map/ppermute | solution.py:188
  21.4 9.2 %collective-permute-start.5 = (bf16[2,128,512]{2,1,0:T(8,128)(2,1)S(1)}, bf16[2,128,512]{2,1,0:T(8,128)(2,1)S(1)}, u32[]{:S(2)}, u32[]{:S(2)}) collective-permute-start(bf16[2,128,512]{2,1,0:T(8,128)(2,1)S(1)} %collective-permute-done.1.refs_4_), channel_id=1, source_target_pairs={{0,16},{16,0},{1,17},{17,1},{2,18},{18,2},{3,19},{19,3},{4,20},{20... | collective-permute-start | bytes 786440 | tf_op jit(solution)/shard_map/ppermute | solution.py:192
  22.9 11.9 %copy-start.6 = (bf16[1,2048]{1,0:T(2,128)(2,1)}, bf16[1,2048]{1,0:T(2,128)(2,1)S(1)}, u32[]{:S(2)}) copy-start(bf16[1,2048]{1,0:T(2,128)(2,1)S(1)} %collective-permute-done.7) | copy-start | bytes 12292
  23.6 5.1 %collective-permute-start.8 = (bf16[2,2048]{1,0:T(2,128)(2,1)S(1)}, bf16[2,2048]{1,0:T(2,128)(2,1)S(1)}, u32[]{:S(2)}, u32[]{:S(2)}) collective-permute-start(bf16[2,2048]{1,0:T(2,128)(2,1)S(1)} %pad_maximum_fusion.2), channel_id=1, source_target_pairs={{0,1},{1,0},{2,3},{3,2},{4,5},{5,4},{6,7},{7,6},{8,9},{9,8},{10,11... | collective-permute-start | bytes 24584 | tf_op jit(solution)/shard_map/ppermute | solution.py:204
  28.7 6.1 %copy-start.9 = (bf16[2,2048]{1,0:T(2,128)(2,1)}, bf16[2,2048]{1,0:T(2,128)(2,1)S(1)}, u32[]{:S(2)}) copy-start(bf16[2,2048]{1,0:T(2,128)(2,1)S(1)} %collective-permute-done.8) | copy-start | bytes 24580
  28.8 4.7 %collective-permute-start.9 = (bf16[4,2048]{1,0:T(4,128)(2,1)S(1)}, bf16[4,2048]{1,0:T(4,128)(2,1)S(1)}, u32[]{:S(2)}, u32[]{:S(2)}) collective-permute-start(bf16[4,2048]{1,0:T(4,128)(2,1)S(1)} %pad_maximum_fusion.1), channel_id=1, source_target_pairs={{0,2},{1,3},{2,0},{3,1},{4,6},{5,7},{6,4},{7,5},{8,10},{9,11},{10,... | collective-permute-start | bytes 49160 | tf_op jit(solution)/shard_map/ppermute | solution.py:204
  30.6 0.7 %copy-start.2 = (bf16[2,128,512]{2,1,0:T(8,128)(2,1)}, bf16[2,128,512]{2,1,0:T(8,128)(2,1)S(1)}, u32[]{:S(2)}) copy-start(bf16[2,128,512]{2,1,0:T(8,128)(2,1)S(1)} %collective-permute-done.5.refs_8_) | copy-start | bytes 786436
  31.3 10.8 %collective-permute-start.6 = (bf16[2,128,512]{2,1,0:T(8,128)(2,1)}, bf16[2,128,512]{2,1,0:T(8,128)(2,1)}, u32[]{:S(2)}, u32[]{:S(2)}) collective-permute-start(bf16[2,128,512]{2,1,0:T(8,128)(2,1)} %collective-permute-done.2.refs_3_), channel_id=1, source_target_pairs={{0,16},{16,0},{1,17},{17,1},{2,18},{18,2},{3,19},{19,3},{4,20},{20... | collective-permute-start | bytes 786440 | tf_op jit(solution)/shard_map/ppermute | solution.py:192
  33.5 1.3 %copy-start.7 = (bf16[4,2048]{1,0:T(4,128)(2,1)}, bf16[4,2048]{1,0:T(4,128)(2,1)S(1)}, u32[]{:S(2)}) copy-start(bf16[4,2048]{1,0:T(4,128)(2,1)S(1)} %collective-permute-done.9) | copy-start | bytes 49156
  33.5 1.3 %collective-permute-start.10 = (bf16[8,2048]{1,0:T(8,128)(2,1)S(1)}, bf16[8,2048]{1,0:T(8,128)(2,1)S(1)}, u32[]{:S(2)}, u32[]{:S(2)}) collective-permute-start(bf16[8,2048]{1,0:T(8,128)(2,1)S(1)} %pad_maximum_fusion), channel_id=1, source_target_pairs={{0,4},{4,0},{8,12},{12,8},{1,5},{5,1},{9,13},{13,9},{2,6},{6,2},{1... | collective-permute-start | bytes 98312 | tf_op jit(solution)/shard_map/ppermute | solution.py:204
  34.8 0.6 %copy-start.8 = (bf16[8,2048]{1,0:T(8,128)(2,1)}, bf16[8,2048]{1,0:T(8,128)(2,1)S(1)}, u32[]{:S(2)}) copy-start(bf16[8,2048]{1,0:T(8,128)(2,1)S(1)} %collective-permute-done.10) | copy-start | bytes 98308
  35.4 4.4 %collective-permute-start.11 = (bf16[16,2048]{1,0:T(8,128)(2,1)S(1)}, bf16[16,2048]{1,0:T(8,128)(2,1)}, u32[]{:S(2)}, u32[]{:S(2)}) collective-permute-start(bf16[16,2048]{1,0:T(8,128)(2,1)S(1)} %concatenate.26), channel_id=1, source_target_pairs={{0,8},{4,12},{8,0},{12,4},{1,9},{5,13},{9,1},{13,5},{2,10},{6,14},... | collective-permute-start | bytes 196616 | tf_op jit(solution)/shard_map/ppermute | solution.py:204
  37.6 4.6 %copy-start.4 = (f32[16]{0:T(128)S(1)}, f32[16]{0:T(128)}, u32[]{:S(2)}) copy-start(f32[16]{0:T(128)} %gate.1) | copy-start | bytes 196
  42.2 1.0 %copy-start.3 = (bf16[2,128,512]{2,1,0:T(8,128)(2,1)S(1)}, bf16[2,128,512]{2,1,0:T(8,128)(2,1)}, u32[]{:S(2)}) copy-start(bf16[2,128,512]{2,1,0:T(8,128)(2,1)} %copy-done.2) | copy-start | bytes 786436

commit v2 on v0

--- a/solution.py
+++ b/solution.py
@@ -1,8 +1,11 @@
+import functools
 import math
 
 import jax
 import jax.numpy as jnp
 from jax import lax
+from jax.experimental import pallas as pl
+from jax.experimental.pallas import tpu as pltpu
 from jax.sharding import PartitionSpec as P
 
 HQ = 64
@@ -33,7 +36,7 @@
     return jnp.transpose(carry_state[2] / carry_state[1][..., None], (0, 3, 1, 2, 4))
 
 
-def per_device(queries, self_kv, image_kv, cross_gate, lengths):
+def scan_device(queries, self_kv, image_kv, cross_gate, lengths):
     tp_count = lax.axis_size("tp")
     heads_local = HQ // tp_count
     kv_local = max(1, KVH // tp_count)
@@ -125,6 +128,374 @@
     return attended.reshape(2, seq_rows, heads_local * HEAD_SIZE).astype(jnp.bfloat16)
 
 
+MASKED = -1e30
+EXP2_SCALE = math.log2(math.e) / math.sqrt(HEAD_SIZE)
+VMEM_SPEC = pl.BlockSpec(memory_space=pltpu.VMEM)
+ANY_SPEC = pl.BlockSpec(memory_space=pl.ANY)
+BLOCKS = 8
+CHUNK = 4
+KERNEL = pltpu.CompilerParams(vmem_limit_bytes=12 << 20)
+
+
+def in_vmem(*arrays):
+    return [pltpu.with_memory_space_constraint(array, pltpu.VMEM) for array in arrays]
+
+
+def rows_by_rows(left, right):
+    return lax.dot_general(left, right, (((1,), (1,)), ((), ())), preferred_element_type=jnp.float32)
+
+
+def columns_by_columns(left, right):
+    return lax.dot_general(left, right, (((0,), (0,)), ((), ())), preferred_element_type=jnp.float32)
+
+
+def block_of(place):
+    return jnp.where(place < BLOCKS // 2, place, 3 * BLOCKS // 2 - 1 - place)
+
+
+def ring_blocks(shifts):
+    ctx, section = lax.axis_index("ctx"), lax.axis_index("section")
+    place = jnp.where(ctx == 0, section, BLOCKS - 1 - section)
+    return [block_of((place + shift + BLOCKS) & (BLOCKS - 1)) for shift in shifts], ctx * (BLOCKS // 2) + section
+
+
+def position_bias(block, own, limit, rows, diagonal):
+    key = lax.broadcasted_iota(jnp.int32, (rows, rows), 0)
+    first = jnp.where(block <= own, block * rows, 1 << 30)
+    allowed = first + key < limit
+    if diagonal:
+        allowed &= key <= lax.broadcasted_iota(jnp.int32, (rows, rows), 1)
+    return jnp.where(allowed, 0.0, MASKED)
+
+
+def weigh(scores, biases, rows, old):
+    if biases:
+        scores = jnp.concatenate([scores[i * rows : (i + 1) * rows] + bias for i, bias in enumerate(biases)], 0)
+    best = jnp.max(scores, axis=0, keepdims=True)
+    if old is not None:
+        best = jnp.maximum(old, best)
+    weights = jnp.exp2((scores - best) * EXP2_SCALE)
+    return best, jnp.sum(weights, axis=0, keepdims=True), weights.astype(jnp.bfloat16)
+
+
+def weigh_heads(scores, biases, rows, heads, old):
+    parts = []
+    for h in range(heads):
+        part = slice(h * rows, (h + 1) * rows)
+        parts.append(weigh(scores[:, part], biases, rows, None if old is None else old[:, part]))
+    return [jnp.concatenate(x, 1) for x in zip(*parts)]
+
+
+def in_turn(units, score, weigh_unit, collect):
+    ahead = score(*units[0])
+    waiting = None
+    for i, unit in enumerate(units):
+        scores = ahead
+        if i + 1 < len(units):
+            ahead = score(*units[i + 1])
+        weighed = weigh_unit(*unit, scores)
+        if waiting is not None:
+            collect(*waiting)
+        waiting = (*unit, *weighed)
+    collect(*waiting)
+
+
+class Heads:
+    def __init__(self, q_ref, groups):
+        self.q_ref = q_ref
+        self.sequences, self.rows = q_ref.shape[:2]
+        self.heads = q_ref.shape[2] // HEAD_SIZE // groups
+        self.chunk = min(CHUNK, self.heads)
+        self.units = [
+            (sequence, group, h)
+            for group in range(groups)
+            for sequence in range(self.sequences)
+            for h in range(0, self.heads, self.chunk)
+        ]
+
+    def queries(self, sequence, group, h):
+        first = (group * self.heads + h) * HEAD_SIZE
+        columns = [slice(first + j * HEAD_SIZE, first + (j + 1) * HEAD_SIZE) for j in range(self.chunk)]
+        return jnp.concatenate([self.q_ref[sequence, :, c] for c in columns], 0)
+
+    def part(self, h):
+        return slice(h * self.rows, (h + self.chunk) * self.rows)
+
+
+def key_columns(group):
+    return slice(2 * group * HEAD_SIZE, (2 * group + 1) * HEAD_SIZE)
+
+
+def value_columns(group):
+    return slice((2 * group + 1) * HEAD_SIZE, (2 * group + 2) * HEAD_SIZE)
+
+
+def stack_rows(refs, sequence, columns):
+    rows = [r[sequence if r.shape[0] > 1 else 0, :, columns] for r in refs]
+    return jnp.concatenate(rows, 0) if len(rows) > 1 else rows[0]
+
+
+def fold(heads, length_ref, blocks, numbers, own, old_state, state):
+    stat_ref, sum_ref = state
+    rows = heads.rows
+    biases = [
+        [
+            position_bias(number, own, length_ref[i : i + 1], rows, old_state is None and j == 0)
+            for j, number in enumerate(numbers)
+        ]
+        for i in range(heads.sequences)
+    ]
+
+    def score(sequence, group, h):
+        return rows_by_rows(stack_rows(blocks, sequence, key_columns(group)), heads.queries(sequence, group, h))
+
+    def weigh_unit(sequence, group, h, scores):
+        part = heads.part(h)
+        old = None if old_state is None else stat_ref[sequence, group, 0:1, part]
+        best, total, weights = weigh_heads(scores, biases[sequence], rows, heads.chunk, old)
+        shrink = None
+        if old is not None:
+            shrink = jnp.exp2((old - best) * EXP2_SCALE)
+            total = stat_ref[sequence, group, 1:2, part] * shrink + total
+        stat_ref[sequence, group, 0:1, part] = best
+        stat_ref[sequence, group, 1:2, part] = total
+        return shrink, weights
+
+    def collect(sequence, group, h, shrink, weights):
+        part = heads.part(h)
+        added = columns_by_columns(stack_rows(blocks, sequence, value_columns(group)), weights)
+        if shrink is not None:
+            added = sum_ref[sequence, group, :, part] * shrink + added
+        sum_ref[sequence, group, :, part] = added
+
+    in_turn(heads.units, score, weigh_unit, collect)
+
+
+def fold_kernel(first, shifts, groups, length_ref, q_ref, *refs):
+    blocks = refs[: len(shifts)]
+    numbers, own = ring_blocks(shifts)
+    heads = Heads(q_ref, groups)
+    if first:
+        fold(heads, length_ref, blocks, numbers, own, None, refs[-2:])
+    else:
+        useful = functools.reduce(jnp.logical_or, [number < own for number in numbers])
+        pl.when(useful)(lambda: fold(heads, length_ref, blocks, numbers, own, refs[-4:-2], refs[-2:]))
+
+
+def state_shapes(q, groups):
+    sequences, rows, columns = q.shape
+    width = columns // HEAD_SIZE // groups * rows
+    return [
+        pltpu.VMEM((sequences, groups, 2, width), jnp.float32),
+        pltpu.VMEM((sequences, groups, HEAD_SIZE, width), jnp.float32),
+    ]
+
+
+def cost(q, keys):
+    work = q.shape[0] * q.shape[2] // HEAD_SIZE * q.shape[1] * keys
+    return pl.CostEstimate(flops=work * 4 * HEAD_SIZE, bytes_accessed=1 << 20, transcendentals=work)
+
+
+def fold_blocks(lengths, q, blocks, shifts, state):
+    groups = blocks[0].shape[2] // (2 * HEAD_SIZE)
+    first = state is None
+    state = () if first else tuple(state)
+    held = 2 + len(blocks)
+    return pl.pallas_call(
+        functools.partial(fold_kernel, first, shifts, groups),
+        in_specs=[VMEM_SPEC] * (held + len(state)),
+        out_specs=[VMEM_SPEC] * 2,
+        out_shape=state_shapes(q, groups),
+        input_output_aliases={} if first else {held + i: i for i in range(2)},
+        compiler_params=KERNEL,
+        cost_estimate=cost(q, q.shape[1] * len(blocks)),
+        name="fold_blocks",
+    )(*in_vmem(lengths, q, *blocks, *state))
+
+
+def cross_kernel(groups, factor_ref, q_ref, *refs):
+    images, cross_ref = refs[:-1], refs[-1]
+    heads = Heads(q_ref, groups)
+    rows = heads.rows
+    first = lax.axis_index("tp") * 2 * groups
+    columns = [pl.ds(pl.multiple_of((first + i) * HEAD_SIZE, HEAD_SIZE), HEAD_SIZE) for i in range(2 * groups)]
+    image = [jnp.concatenate([r[:, c] for r in images], 0) for c in columns]
+
+    def score(sequence, group, h):
+        return rows_by_rows(image[2 * group], heads.queries(sequence, group, h))
+
+    def weigh_unit(sequence, group, h, scores):
+        _, total, weights = weigh_heads(scores, [], rows, heads.chunk, None)
+        first = group * heads.heads + h
+        factors = jnp.concatenate([factor_ref[first + j : first + j + 1] for j in range(heads.chunk)], 1)
+        return factors / total, weights
+
+    def collect(sequence, group, h, factors, weights):
+        cross_ref[sequence, group, :, heads.part(h)] = columns_by_columns(image[2 * group + 1], weights) * factors
+
+    in_turn(heads.units, score, weigh_unit, collect)
+
+
+def cross_attend(factors, q, images, groups):
+    return pl.pallas_call(
+        functools.partial(cross_kernel, groups),
+        in_specs=[VMEM_SPEC] * (2 + len(images)),
+        out_specs=VMEM_SPEC,
+        out_shape=state_shapes(q, groups)[1],
+        compiler_params=KERNEL,
+        cost_estimate=cost(q, q.shape[1]),
+        name="cross_attend",
+    )(*in_vmem(factors, q, *images))
+
+
+def finish_kernel(shift, groups, length_ref, q_ref, block0, block1, cross_ref, stat_ref, sum_ref, out_ref):
+    heads = Heads(q_ref, groups)
+    rows = heads.rows
+    (number,), own = ring_blocks([shift])
+    blocks = (block0, block1)
+    biases = [[position_bias(number, own, length_ref[i : i + 1], rows, False)] for i in range(heads.sequences)]
+
+    def score(sequence, group, h):
+        return rows_by_rows(blocks[sequence][0, :, key_columns(group)], heads.queries(sequence, group, h))
+
+    def weigh_unit(sequence, group, h, scores):
+        part = heads.part(h)
+        old = stat_ref[sequence, group, 0:1, part]
+        best, total, weights = weigh_heads(scores, biases[sequence], rows, heads.chunk, old)
+        shrink = jnp.exp2((old - best) * EXP2_SCALE)
+        over = 1.0 / (stat_ref[sequence, group, 1:2, part] * shrink + total)
+        return shrink * over, over, weights
+
+    def collect(sequence, group, h, old_factor, factor, weights):
+        part = heads.part(h)
+        added = columns_by_columns(blocks[sequence][0, :, value_columns(group)], weights)
+        out = sum_ref[sequence, group, :, part] * old_factor + added * factor + cross_ref[sequence, group, :, part]
+        for j in range(heads.chunk):
+            first = (group * heads.heads + h + j) * HEAD_SIZE
+            out_ref[sequence, :, first : first + HEAD_SIZE] = out[:, j * rows : (j + 1) * rows].T.astype(jnp.bfloat16)
+
+    in_turn(heads.units, score, weigh_unit, collect)
+
+
+def finish_rows(lengths, q, shift, blocks, cross, state):
+    groups = blocks[0].shape[2] // (2 * HEAD_SIZE)
+    args = in_vmem(lengths, q, *blocks, cross, *state)
+    return pl.pallas_call(
+        functools.partial(finish_kernel, shift, groups),
+        in_specs=[VMEM_SPEC] * len(args),
+        out_specs=VMEM_SPEC,
+        out_shape=jax.ShapeDtypeStruct(q.shape, q.dtype),
+        compiler_params=KERNEL,
+        cost_estimate=cost(q, q.shape[1]),
+        name="finish_rows",
+    )(*args)
+
+
+def load_kernel(lengths, gate, q_ref, image_ref, limit_ref, factor_ref, q_out, image_out, counts, gates, sems):
+    pairs = ((lengths, counts), (gate, gates), (q_ref, q_out), (image_ref, image_out))
+    copies = [pltpu.make_async_copy(source, target, sems.at[i]) for i, (source, target) in enumerate(pairs)]
+    for copy in copies:
+        copy.start()
+    copies[0].wait()
+    for i in range(limit_ref.shape[0]):
+        limit_ref[i : i + 1] = jnp.full((1, limit_ref.shape[1]), counts[i], jnp.int32)
+    copies[1].wait()
+    for i in range(factor_ref.shape[0]):
+        factor_ref[i : i + 1] = jnp.full((1, factor_ref.shape[1]), gates[i], jnp.float32)
+    factor_ref[...] = jnp.tanh(factor_ref[...])
+    copies[2].wait()
+    copies[3].wait()
+
+
+def load_inputs(*arrays):
+    lengths, gate, q, image = arrays
+    rows = q.shape[1]
+    return pl.pallas_call(
+        load_kernel,
+        in_specs=[ANY_SPEC] * 4,
+        out_specs=[VMEM_SPEC] * 4,
+        out_shape=[
+            pltpu.VMEM((lengths.shape[0], rows), jnp.int32),
+            pltpu.VMEM((gate.shape[0], rows), jnp.float32),
+            pltpu.VMEM(q.shape, q.dtype),
+            pltpu.VMEM(image.shape, image.dtype),
+        ],
+        scratch_shapes=[
+            pltpu.SMEM(lengths.shape, lengths.dtype),
+            pltpu.SMEM(gate.shape, gate.dtype),
+            pltpu.SemaphoreType.DMA((4,)),
+        ],
+        compiler_params=KERNEL,
+        name="load_inputs",
+    )(*[pltpu.with_memory_space_constraint(array, pltpu.HBM) for array in arrays])
+
+
+def halve_kernel(forward_ref, backward_ref, first_ref, second_ref):
+    first_ref[...] = forward_ref[0:1]
+    second_ref[...] = backward_ref[1:2]
+
+
+def half_of_each(forward, backward):
+    shape = pltpu.VMEM((1,) + forward.shape[1:], forward.dtype)
+    return pl.pallas_call(
+        halve_kernel,
+        in_specs=[VMEM_SPEC] * 2,
+        out_specs=[VMEM_SPEC] * 2,
+        out_shape=[shape] * 2,
+        compiler_params=KERNEL,
+        name="half_of_each",
+    )(*in_vmem(forward, backward))
+
+
+RING = (0, 1, 2, 3, 7, 6, 5, 4)
+
+
+def ring_forward(block):
+    pairs = [(RING[i], RING[(i + 1) % BLOCKS]) for i in range(BLOCKS)]
+    return lax.ppermute(block, ("ctx", "section"), pairs)
+
+
+def ring_backward(block):
+    pairs = [(RING[(i + 1) % BLOCKS], RING[i]) for i in range(BLOCKS)]
+    return lax.ppermute(block, ("ctx", "section"), pairs)
+
+
+def after(block, *others):
+    return lax.optimization_barrier((block,) + others)[0]
+
+
+def swapped(rows, name, bits):
+    return lax.ppermute(rows, name, [(i, i ^ bits) for i in range(lax.axis_size(name))])
+
+
+def ring_device(queries, self_kv, image_kv, cross_gate, lengths):
+    tp_count = lax.axis_size("tp")
+    groups = KVH // tp_count
+    kv_cols = groups * 2 * HEAD_SIZE
+    own = lax.dynamic_slice_in_dim(self_kv, lax.axis_index("tp") * kv_cols, kv_cols, 2)
+    f1, b1 = ring_forward(own), ring_backward(own)
+    i1 = swapped(image_kv, "section", 2)
+    limits, factors, q, image1 = load_inputs(lengths, cross_gate, queries, image_kv)
+    image2 = jnp.concatenate([image1, i1], 0)
+    i2 = swapped(image2, "section", 1)
+
+    f2, b2 = ring_forward(after(f1, image2)), ring_backward(after(b1, image2))
+    image4 = jnp.concatenate([image2, i2], 0)
+    i3 = swapped(image4, "ctx", 1)
+    state = fold_blocks(limits, q, [own, f1, after(b1, image4)], (0, -1, 1), None)
+
+    f3, b3 = ring_forward(after(f2, state[0])), ring_backward(after(b2, state[0]))
+    image8 = jnp.concatenate([image4, i3], 0)
+    images = [image8] + [swapped(image8, "tp", bits) for bits in range(1, tp_count)]
+    state = fold_blocks(limits, q, [f2, after(b2, image8)], (-2, 2), state)
+
+    f4, b4 = half_of_each(after(f3, state[0], *images), b3)
+    f4, b4 = ring_forward(f4), ring_backward(b4)
+    cross = cross_attend(factors, q, images, groups)
+    state = fold_blocks(limits, q, [f3, b3], (-3, 3), state)
+    return finish_rows(limits, q, 4, [f4, b4], cross, state)
+
+
 def solution(mesh):
     placed = (
         P(None, ("ctx", "section"), "tp"),
@@ -133,8 +504,9 @@
         P("tp"),
         P(),
     )
+    ring = mesh.shape["ctx"] == 2 and mesh.shape["section"] == 4 and mesh.shape["tp"] == 4
     return jax.shard_map(
-        per_device,
+        ring_device if ring else scan_device,
         mesh=mesh,
         in_specs=placed,
         out_specs=P(None, ("ctx", "section"), "tp"),

time: 105 us -> 37.5 us (0.36)
  the two profiles are of different devices: /device:TPU:14 before, /device:TPU:0 now
where the time goes in v2:
time: 37.5 us; the launch traced here: 37.4 us
  starting transfers between devices  18.9 us (50%)
  waiting for transfers between devices  9.7 us (26%)
  Pallas kernels  7.34 us (20%)
  local copies, waits for them, and re-layouts  1.24 us (3%)
    ppermute x6, starting transfers between devices, swapped(): lax.ppermute(rows, name, [(i, i ^ bits) for i in range(lax.axis_size(name...  8.74 us
    ppermute x4, starting transfers between devices, ring_backward(): return lax.ppermute(block, ('ctx', 'section'), pairs)  7.89 us
    ppermute x6, waiting for transfers between devices, swapped(): lax.ppermute(rows, name, [(i, i ^ bits) for i in range(lax.axis_size(name...  5.62 us
    pallas_call x1, Pallas kernels, finish_rows(): pl.pallas_call(functools.partial(finish_kernel, shift, groups), in_specs=...  2.64 us
    pallas_call x3, Pallas kernels, fold_blocks(): pl.pallas_call(functools.partial(fold_kernel, first, shifts, groups), in_...  2.59 us
    ppermute x4, starting transfers between devices, ring_forward(): return lax.ppermute(block, ('ctx', 'section'), pairs)  2.28 us
    ppermute x4, waiting for transfers between devices, ring_forward(): return lax.ppermute(block, ('ctx', 'section'), pairs)  2.27 us
    ppermute x4, waiting for transfers between devices, ring_backward(): return lax.ppermute(block, ('ctx', 'section'), pairs)  1.81 us
  transfers between devices with their start and end apart: 14, of which 7 were waited for; matrix products, arithmetic and copies ran while one was open for 0% of the time, Pallas kernels for 13%

profile of v2, /device:TPU:0, one launch (start us, length us, event | category | flops | bytes accessed | tf_op | source)
XLA Modules:
  0.0 37.4 jit_solution(8096691178572855704)
XLA Ops:
  0.0 0.0 copy-start
  0.0 1.2 %copy-done = bf16[2,128,2048]{2,1,0:T(8,128)(2,1)S(1)} copy-done((bf16[2,128,2048]{2,1,0:T(8,128)(2,1)S(1)}, bf16[2,128,2048]{2,1,0:T(8,128)(2,1)}, u32[]{:S(2)}) %copy-start) | copy-done | bytes 1048600
  1.2 3.0 %collective-permute-start.3 = (bf16[2,128,512]{2,1,0:T(8,128)(2,1)S(1)}, bf16[2,128,512]{2,1,0:T(8,128)(2,1)S(1)}, u32[]{:S(2)}, u32[]{:S(2)}) collective-permute-start(bf16[2,128,512]{2,1,0:T(8,128)(2,1)S(1)} %constant_dynamic-slice_fusion.refs_0_), channel_id=1, source_target_pairs={{1,0},{2,1},{3,2},{19,3},{18,19},{17,18},{16,17},{0,16},{5,4},{6,5... | collective-permute-start | bytes 786440 | tf_op jit(solution)/shard_map/ppermute | solution.py:460
  4.3 0.1 collective-permute-start
  4.4 3.0 %collective-permute-start.1 = (bf16[1,2048]{1,0:T(2,128)(2,1)}, bf16[1,2048]{1,0:T(2,128)(2,1)S(1)}, u32[]{:S(2)}, u32[]{:S(2)}) collective-permute-start(bf16[1,2048]{1,0:T(2,128)(2,1)} %image_ref.1), channel_id=1, source_target_pairs={{0,2},{1,3},{2,0},{3,1},{4,6},{5,7},{6,4},{7,5},{8,10},{9,11},{10,... | collective-permute-start | bytes 12296 | tf_op jit(solution)/shard_map/ppermute | solution.py:468
  7.4 1.3 %load_inputs.1 = (s32[2,128]{1,0:T(2,128)S(1)}, f32[16,128]{1,0:T(8,128)S(1)}, bf16[2,128,2048]{2,1,0:T(8,128)(2,1)S(1)}, bf16[1,2048]{1,0:T(2,128)(2,1)S(1)}) custom-call(s32[2]{0:T(128)} %lengths.1, f32[16]{0:T(128)} %gate.1, bf16[2,128,2048]{2,1,0:T(8,128)(2,1)} %q_ref.1, bf16[1,2048]{1,0:T(2,128)(2,1)} %image_ref.1), custom_call_target="tpu_custom_call" | custom-call | tf_op jit(solution)/shard_map/load_inputs/pallas_call | solution.py:413
  8.6 3.4 %collective-permute-done.1 = bf16[1,2048]{1,0:T(2,128)(2,1)S(1)} collective-permute-done((bf16[1,2048]{1,0:T(2,128)(2,1)}, bf16[1,2048]{1,0:T(2,128)(2,1)S(1)}, u32[]{:S(2)}, u32[]{:S(2)}) %collective-permute-start.1) | collective-permute-done | bytes 4128 | tf_op jit(solution)/shard_map/ppermute | solution.py:468
  12.1 1.6 %collective-permute-start.4 = (bf16[2,2048]{1,0:T(2,128)(2,1)S(1)}, bf16[2,2048]{1,0:T(2,128)(2,1)S(1)}, u32[]{:S(2)}, u32[]{:S(2)}) collective-permute-start(bf16[2,2048]{1,0:T(2,128)(2,1)S(1)} %pad_maximum_fusion.2), channel_id=1, source_target_pairs={{0,1},{1,0},{2,3},{3,2},{4,5},{5,4},{6,7},{7,6},{8,9},{9,8},{10,11... | collective-permute-start | bytes 24584 | tf_op jit(solution)/shard_map/ppermute | solution.py:468
  13.7 0.0 collective-permute-done.3.refs_2_
  13.7 0.0 collective-permute-done.refs_1_
  13.7 0.5 %collective-permute-start.2 = (bf16[2,128,512]{2,1,0:T(8,128)(2,1)S(1)}, bf16[2,128,512]{2,1,0:T(8,128)(2,1)S(1)}, u32[]{:S(2)}, u32[]{:S(2)}) collective-permute-start(bf16[2,128,512]{2,1,0:T(8,128)(2,1)S(1)} %collective-permute-done.refs_1_), channel_id=1, source_target_pairs={{0,1},{1,2},{2,3},{3,19},{19,18},{18,17},{17,16},{16,0},{4,5},{5,6... | collective-permute-start | bytes 786440 | tf_op jit(solution)/shard_map/ppermute | solution.py:455
  14.2 2.3 %collective-permute-start.6 = (bf16[2,128,512]{2,1,0:T(8,128)(2,1)S(1)}, bf16[2,128,512]{2,1,0:T(8,128)(2,1)S(1)}, u32[]{:S(2)}, u32[]{:S(2)}) collective-permute-start(bf16[2,128,512]{2,1,0:T(8,128)(2,1)S(1)} %collective-permute-done.3.refs_2_), channel_id=1, source_target_pairs={{1,0},{2,1},{3,2},{19,3},{18,19},{17,18},{16,17},{0,16},{5,4},{6,5... | collective-permute-start | bytes 786440 | tf_op jit(solution)/shard_map/ppermute | solution.py:460
  16.5 0.0 collective-permute-done.4
  16.6 2.3 %collective-permute-start.7 = (bf16[4,2048]{1,0:T(4,128)(2,1)S(1)}, bf16[4,2048]{1,0:T(4,128)(2,1)S(1)}, u32[]{:S(2)}, u32[]{:S(2)}) collective-permute-start(bf16[4,2048]{1,0:T(4,128)(2,1)S(1)} %pad_maximum_fusion.1), channel_id=1, source_target_pairs={{0,16},{16,0},{1,17},{17,1},{2,18},{18,2},{3,19},{19,3},{4,20},{20... | collective-permute-start | bytes 49160 | tf_op jit(solution)/shard_map/ppermute | solution.py:468
  18.9 2.6 %fold_blocks.3 = (f32[2,2,2,1024]{3,2,1,0:T(2,128)S(1)}, f32[2,2,128,1024]{3,2,1,0:T(8,128)S(1)}) custom-call(s32[2,128]{1,0:T(2,128)S(1)} %get-tuple-element.24.length_ref, bf16[2,128,2048]{2,1,0:T(8,128)(2,1)S(1)} %get-tuple-element.25.q_ref, bf16[2,128,512]{2,1,0:T(8,128)(2,1)S(1)} %constant_dynamic-slice_fusion.refs_0_, ...), custom_call_target="tpu_custom_call" | custom-call | flops 805306368 | bytes 1048576 | tf_op jit(solution)/shard_map/fold_blocks/pallas_call | solution.py:304
  21.4 0.0 collective-permute-done.6.refs_1_
  21.5 0.0 collective-permute-done.2.refs_0_
  21.5 1.5 %collective-permute-start.5 = (bf16[2,128,512]{2,1,0:T(8,128)(2,1)S(1)}, bf16[2,128,512]{2,1,0:T(8,128)(2,1)S(1)}, u32[]{:S(2)}, u32[]{:S(2)}) collective-permute-start(bf16[2,128,512]{2,1,0:T(8,128)(2,1)S(1)} %collective-permute-done.2.refs_0_), channel_id=1, source_target_pairs={{0,1},{1,2},{2,3},{3,19},{19,18},{18,17},{17,16},{16,0},{4,5},{5,6... | collective-permute-start | bytes 786440 | tf_op jit(solution)/shard_map/ppermute | solution.py:455
  23.0 0.6 %collective-permute-start.11 = (bf16[2,128,512]{2,1,0:T(8,128)(2,1)S(1)}, bf16[2,128,512]{2,1,0:T(8,128)(2,1)S(1)}, u32[]{:S(2)}, u32[]{:S(2)}) collective-permute-start(bf16[2,128,512]{2,1,0:T(8,128)(2,1)S(1)} %collective-permute-done.6.refs_1_), channel_id=1, source_target_pairs={{1,0},{2,1},{3,2},{19,3},{18,19},{17,18},{16,17},{0,16},{5,4},{6,5... | collective-permute-start | bytes 786440 | tf_op jit(solution)/shard_map/ppermute | solution.py:460
  23.5 0.0 collective-permute-done.7
  23.6 0.1 collective-permute-start.10
  23.7 1.6 %collective-permute-start.9 = (bf16[8,2048]{1,0:T(8,128)(2,1)S(1)}, bf16[8,2048]{1,0:T(8,128)(2,1)S(1)}, u32[]{:S(2)}, u32[]{:S(2)}) collective-permute-start(bf16[8,2048]{1,0:T(8,128)(2,1)S(1)} %pad_maximum_fusion.refs_0_), channel_id=1, source_target_pairs={{0,8},{4,12},{8,0},{12,4},{1,9},{5,13},{9,1},{13,5},{2,10},{6,14},... | collective-permute-start | bytes 98312 | tf_op jit(solution)/shard_map/ppermute | solution.py:468
  25.2 0.3 collective-permute-start.8
  25.5 1.8 %collective-permute-done.10.refs_3_ = bf16[8,2048]{1,0:T(8,128)(2,1)S(1)} collective-permute-done((bf16[8,2048]{1,0:T(8,128)(2,1)S(1)}, bf16[8,2048]{1,0:T(8,128)(2,1)S(1)}, u32[]{:S(2)}, u32[]{:S(2)}) %collective-permute-start.10) | collective-permute-done | bytes 32800 | tf_op jit(solution)/shard_map/ppermute | solution.py:468
  27.3 0.4 %collective-permute-done.9.refs_2_ = bf16[8,2048]{1,0:T(8,128)(2,1)S(1)} collective-permute-done((bf16[8,2048]{1,0:T(8,128)(2,1)S(1)}, bf16[8,2048]{1,0:T(8,128)(2,1)S(1)}, u32[]{:S(2)}, u32[]{:S(2)}) %collective-permute-start.9) | collective-permute-done | bytes 32800 | tf_op jit(solution)/shard_map/ppermute | solution.py:468
  27.7 0.0 collective-permute-done.8.refs_1_
  27.7 0.2 collective-permute-done.5.forward_ref.refs_0_
  27.9 1.5 %collective-permute-done.11.backward_ref.refs_1_ = bf16[2,128,512]{2,1,0:T(8,128)(2,1)S(1)} collective-permute-done((bf16[2,128,512]{2,1,0:T(8,128)(2,1)S(1)}, bf16[2,128,512]{2,1,0:T(8,128)(2,1)S(1)}, u32[]{:S(2)}, u32[]{:S(2)}) %collective-permute-start.11) | collective-permute-done | bytes 262176 | tf_op jit(solution)/shard_map/ppermute | solution.py:460
  29.4 0.1 collective-permute-start.12
  29.5 2.0 %collective-permute-start.13 = (bf16[1,128,512]{2,1,0:T(8,128)(2,1)S(1)}, bf16[1,128,512]{2,1,0:T(8,128)(2,1)S(1)}, u32[]{:S(2)}, u32[]{:S(2)}) collective-permute-start(bf16[1,128,512]{2,1,0:T(8,128)(2,1)S(1)} %get-tuple-element.38), channel_id=1, source_target_pairs={{1,0},{2,1},{3,2},{19,3},{18,19},{17,18},{16,17},{0,16},{5,4},{6,5... | collective-permute-start | bytes 393224 | tf_op jit(solution)/shard_map/ppermute | solution.py:460
  31.4 0.8 %cross_attend.1.cross_ref = f32[2,2,128,1024]{3,2,1,0:T(8,128)S(1)} custom-call(f32[16,128]{1,0:T(8,128)S(1)} %get-tuple-element.39.factor_ref, bf16[2,128,2048]{2,1,0:T(8,128)(2,1)S(1)} %get-tuple-element.25.q_ref, bf16[8,2048]{1,0:T(8,128)(2,1)S(1)} %pad_maximum_fusion.refs_0_, bf16[8,2048]{1,0:T(8,128)(2,1)S(1)} %collective-permute-done.8.refs_1_, ...), custom_call_target="tpu_custom_call" | custom-call | flops 268435456 | bytes 1048576 | tf_op jit(solution)/shard_map/cross_attend/pallas_call | solution.py:340
  32.3 2.1 %collective-permute-done.12.block0 = bf16[1,128,512]{2,1,0:T(8,128)(2,1)S(1)} collective-permute-done((bf16[1,128,512]{2,1,0:T(8,128)(2,1)S(1)}, bf16[1,128,512]{2,1,0:T(8,128)(2,1)S(1)}, u32[]{:S(2)}, u32[]{:S(2)}) %collective-permute-start.12) | collective-permute-done | bytes 131104 | tf_op jit(solution)/shard_map/ppermute | solution.py:455
  34.4 0.4 collective-permute-done.13.block1
  34.7 2.6 %finish_rows.1 = bf16[2,128,2048]{2,1,0:T(8,128)(2,1)} custom-call(s32[2,128]{1,0:T(2,128)S(1)} %get-tuple-element.24.length_ref, bf16[2,128,2048]{2,1,0:T(8,128)(2,1)S(1)} %get-tuple-element.25.q_ref, bf16[1,128,512]{2,1,0:T(8,128)(2,1)S(1)} %collective-permute-done.12.block0, bf16[1,128,512]{2,1,0:T(8,128)(2,1)S(1)} %collective-permute-done.13.block1, ...), custom_call_target="tpu_custom_call" | custom-call | flops 268435456 | bytes 1048576 | tf_op jit(solution)/shard_map/finish_rows/pallas_call | solution.py:383
  (7 shorter events, 0.2 us)
Async XLA Ops:
  0.0 1.2 %copy-start = (bf16[2,128,2048]{2,1,0:T(8,128)(2,1)S(1)}, bf16[2,128,2048]{2,1,0:T(8,128)(2,1)}, u32[]{:S(2)}) copy-start(bf16[2,128,2048]{2,1,0:T(8,128)(2,1)} %param.6) | copy-start | bytes 3145732
  1.2 12.4 %collective-permute-start.3 = (bf16[2,128,512]{2,1,0:T(8,128)(2,1)S(1)}, bf16[2,128,512]{2,1,0:T(8,128)(2,1)S(1)}, u32[]{:S(2)}, u32[]{:S(2)}) collective-permute-start(bf16[2,128,512]{2,1,0:T(8,128)(2,1)S(1)} %constant_dynamic-slice_fusion.refs_0_), channel_id=1, source_target_pairs={{1,0},{2,1},{3,2},{19,3},{18,19},{17,18},{16,17},{0,16},{5,4},{6,5... | collective-permute-start | bytes 786440 | tf_op jit(solution)/shard_map/ppermute | solution.py:460
  4.3 9.4 %collective-permute-start = (bf16[2,128,512]{2,1,0:T(8,128)(2,1)S(1)}, bf16[2,128,512]{2,1,0:T(8,128)(2,1)S(1)}, u32[]{:S(2)}, u32[]{:S(2)}) collective-permute-start(bf16[2,128,512]{2,1,0:T(8,128)(2,1)S(1)} %constant_dynamic-slice_fusion.refs_0_), channel_id=1, source_target_pairs={{0,1},{1,2},{2,3},{3,19},{19,18},{18,17},{17,16},{16,0},{4,5},{5,6... | collective-permute-start | bytes 786440 | tf_op jit(solution)/shard_map/ppermute | solution.py:455
  4.4 7.7 %collective-permute-start.1 = (bf16[1,2048]{1,0:T(2,128)(2,1)}, bf16[1,2048]{1,0:T(2,128)(2,1)S(1)}, u32[]{:S(2)}, u32[]{:S(2)}) collective-permute-start(bf16[1,2048]{1,0:T(2,128)(2,1)} %image_ref.1), channel_id=1, source_target_pairs={{0,2},{1,3},{2,0},{3,1},{4,6},{5,7},{6,4},{7,5},{8,10},{9,11},{10,... | collective-permute-start | bytes 12296 | tf_op jit(solution)/shard_map/ppermute | solution.py:468
  12.1 4.4 %collective-permute-start.4 = (bf16[2,2048]{1,0:T(2,128)(2,1)S(1)}, bf16[2,2048]{1,0:T(2,128)(2,1)S(1)}, u32[]{:S(2)}, u32[]{:S(2)}) collective-permute-start(bf16[2,2048]{1,0:T(2,128)(2,1)S(1)} %pad_maximum_fusion.2), channel_id=1, source_target_pairs={{0,1},{1,0},{2,3},{3,2},{4,5},{5,4},{6,7},{7,6},{8,9},{9,8},{10,11... | collective-permute-start | bytes 24584 | tf_op jit(solution)/shard_map/ppermute | solution.py:468
  13.7 7.8 %collective-permute-start.2 = (bf16[2,128,512]{2,1,0:T(8,128)(2,1)S(1)}, bf16[2,128,512]{2,1,0:T(8,128)(2,1)S(1)}, u32[]{:S(2)}, u32[]{:S(2)}) collective-permute-start(bf16[2,128,512]{2,1,0:T(8,128)(2,1)S(1)} %collective-permute-done.refs_1_), channel_id=1, source_target_pairs={{0,1},{1,2},{2,3},{3,19},{19,18},{18,17},{17,16},{16,0},{4,5},{5,6... | collective-permute-start | bytes 786440 | tf_op jit(solution)/shard_map/ppermute | solution.py:455
  14.2 7.2 %collective-permute-start.6 = (bf16[2,128,512]{2,1,0:T(8,128)(2,1)S(1)}, bf16[2,128,512]{2,1,0:T(8,128)(2,1)S(1)}, u32[]{:S(2)}, u32[]{:S(2)}) collective-permute-start(bf16[2,128,512]{2,1,0:T(8,128)(2,1)S(1)} %collective-permute-done.3.refs_2_), channel_id=1, source_target_pairs={{1,0},{2,1},{3,2},{19,3},{18,19},{17,18},{16,17},{0,16},{5,4},{6,5... | collective-permute-start | bytes 786440 | tf_op jit(solution)/shard_map/ppermute | solution.py:460
  16.6 7.0 %collective-permute-start.7 = (bf16[4,2048]{1,0:T(4,128)(2,1)S(1)}, bf16[4,2048]{1,0:T(4,128)(2,1)S(1)}, u32[]{:S(2)}, u32[]{:S(2)}) collective-permute-start(bf16[4,2048]{1,0:T(4,128)(2,1)S(1)} %pad_maximum_fusion.1), channel_id=1, source_target_pairs={{0,16},{16,0},{1,17},{17,1},{2,18},{18,2},{3,19},{19,3},{4,20},{20... | collective-permute-start | bytes 49160 | tf_op jit(solution)/shard_map/ppermute | solution.py:468
  21.5 6.4 %collective-permute-start.5 = (bf16[2,128,512]{2,1,0:T(8,128)(2,1)S(1)}, bf16[2,128,512]{2,1,0:T(8,128)(2,1)S(1)}, u32[]{:S(2)}, u32[]{:S(2)}) collective-permute-start(bf16[2,128,512]{2,1,0:T(8,128)(2,1)S(1)} %collective-permute-done.2.refs_0_), channel_id=1, source_target_pairs={{0,1},{1,2},{2,3},{3,19},{19,18},{18,17},{17,16},{16,0},{4,5},{5,6... | collective-permute-start | bytes 786440 | tf_op jit(solution)/shard_map/ppermute | solution.py:455
  23.0 6.4 %collective-permute-start.11 = (bf16[2,128,512]{2,1,0:T(8,128)(2,1)S(1)}, bf16[2,128,512]{2,1,0:T(8,128)(2,1)S(1)}, u32[]{:S(2)}, u32[]{:S(2)}) collective-permute-start(bf16[2,128,512]{2,1,0:T(8,128)(2,1)S(1)} %collective-permute-done.6.refs_1_), channel_id=1, source_target_pairs={{1,0},{2,1},{3,2},{19,3},{18,19},{17,18},{16,17},{0,16},{5,4},{6,5... | collective-permute-start | bytes 786440 | tf_op jit(solution)/shard_map/ppermute | solution.py:460
  23.6 3.7 %collective-permute-start.10 = (bf16[8,2048]{1,0:T(8,128)(2,1)S(1)}, bf16[8,2048]{1,0:T(8,128)(2,1)S(1)}, u32[]{:S(2)}, u32[]{:S(2)}) collective-permute-start(bf16[8,2048]{1,0:T(8,128)(2,1)S(1)} %pad_maximum_fusion.refs_0_), channel_id=1, source_target_pairs={{0,12},{4,8},{8,4},{12,0},{1,13},{5,9},{9,5},{13,1},{2,14},{6,10},... | collective-permute-start | bytes 98312 | tf_op jit(solution)/shard_map/ppermute | solution.py:468
  23.7 4.0 %collective-permute-start.9 = (bf16[8,2048]{1,0:T(8,128)(2,1)S(1)}, bf16[8,2048]{1,0:T(8,128)(2,1)S(1)}, u32[]{:S(2)}, u32[]{:S(2)}) collective-permute-start(bf16[8,2048]{1,0:T(8,128)(2,1)S(1)} %pad_maximum_fusion.refs_0_), channel_id=1, source_target_pairs={{0,8},{4,12},{8,0},{12,4},{1,9},{5,13},{9,1},{13,5},{2,10},{6,14},... | collective-permute-start | bytes 98312 | tf_op jit(solution)/shard_map/ppermute | solution.py:468
  25.2 2.5 %collective-permute-start.8 = (bf16[8,2048]{1,0:T(8,128)(2,1)S(1)}, bf16[8,2048]{1,0:T(8,128)(2,1)S(1)}, u32[]{:S(2)}, u32[]{:S(2)}) collective-permute-start(bf16[8,2048]{1,0:T(8,128)(2,1)S(1)} %pad_maximum_fusion.refs_0_), channel_id=1, source_target_pairs={{0,4},{4,0},{8,12},{12,8},{1,5},{5,1},{9,13},{13,9},{2,6},{6,2},{1... | collective-permute-start | bytes 98312 | tf_op jit(solution)/shard_map/ppermute | solution.py:468
  29.4 5.0 %collective-permute-start.12 = (bf16[1,128,512]{2,1,0:T(8,128)(2,1)S(1)}, bf16[1,128,512]{2,1,0:T(8,128)(2,1)S(1)}, u32[]{:S(2)}, u32[]{:S(2)}) collective-permute-start(bf16[1,128,512]{2,1,0:T(8,128)(2,1)S(1)} %get-tuple-element.37), channel_id=1, source_target_pairs={{0,1},{1,2},{2,3},{3,19},{19,18},{18,17},{17,16},{16,0},{4,5},{5,6... | collective-permute-start | bytes 393224 | tf_op jit(solution)/shard_map/ppermute | solution.py:455
  29.5 5.3 %collective-permute-start.13 = (bf16[1,128,512]{2,1,0:T(8,128)(2,1)S(1)}, bf16[1,128,512]{2,1,0:T(8,128)(2,1)S(1)}, u32[]{:S(2)}, u32[]{:S(2)}) collective-permute-start(bf16[1,128,512]{2,1,0:T(8,128)(2,1)S(1)} %get-tuple-element.38), channel_id=1, source_target_pairs={{1,0},{2,1},{3,2},{19,3},{18,19},{17,18},{16,17},{0,16},{5,4},{6,5... | collective-permute-start | bytes 393224 | tf_op jit(solution)/shard_map/ppermute | solution.py:460

commit v3 on v2

--- a/solution.py
+++ b/solution.py
@@ -348,47 +348,121 @@
     )(*in_vmem(factors, q, *images))
 
 
-def finish_kernel(shift, groups, length_ref, q_ref, block0, block1, cross_ref, stat_ref, sum_ref, out_ref):
+class Results:
+    def __init__(self, heads, out_ref, held_ref, sems):
+        self.heads, self.out_ref, self.held_ref, self.sems = heads, out_ref, held_ref, sems
+        self.copies = []
+
+    def put(self, sequence, group, h, out):
+        heads = self.heads
+        rows = heads.rows
+        for j in range(heads.chunk):
+            first = (group * heads.heads + h + j) * HEAD_SIZE
+            turned = out[:, j * rows : (j + 1) * rows].T.astype(jnp.bfloat16)
+            self.held_ref[sequence, :, first : first + HEAD_SIZE] = turned
+        if h + heads.chunk == heads.heads:
+            width = heads.heads * HEAD_SIZE
+            at = (sequence, slice(None), pl.ds(group * width, width))
+            copy = pltpu.make_async_copy(self.held_ref.at[at], self.out_ref.at[at], self.sems.at[sequence, group])
+            copy.start()
+            self.copies.append(copy)
+
+    def wait(self):
+        for copy in self.copies:
+            copy.wait()
+
+
+def result_scratch(q, groups):
+    return [pltpu.VMEM(q.shape, q.dtype), pltpu.SemaphoreType.DMA((q.shape[0], groups))]
+
+
+def fold_or_finish_kernel(shifts, last_shift, groups, length_ref, q_ref, *refs):
+    blocks = refs[: len(shifts)]
+    cross_ref = refs[len(shifts)]
+    out_ref, stat_ref, sum_ref, held_ref, sems = refs[-5:]
+    numbers, own = ring_blocks(shifts)
+    (last,), _ = ring_blocks([last_shift])
+    heads = Heads(q_ref, groups)
+    useful = functools.reduce(jnp.logical_or, [number < own for number in numbers])
+    state = (stat_ref, sum_ref)
+    pl.when(useful)(lambda: fold(heads, length_ref, blocks, numbers, own, state, state))
+
+    def write():
+        results = Results(heads, out_ref, held_ref, sems)
+        for sequence, group, h in heads.units:
+            part = heads.part(h)
+            over = 1.0 / stat_ref[sequence, group, 1:2, part]
+            results.put(
+                sequence, group, h, sum_ref[sequence, group, :, part] * over + cross_ref[sequence, group, :, part]
+            )
+        results.wait()
+
+    pl.when(last > own)(write)
+
+
+def fold_or_finish(lengths, q, blocks, shifts, last_shift, cross, state):
+    groups = blocks[0].shape[2] // (2 * HEAD_SIZE)
+    args = in_vmem(lengths, q, *blocks, cross, *state)
+    return pl.pallas_call(
+        functools.partial(fold_or_finish_kernel, shifts, last_shift, groups),
+        in_specs=[VMEM_SPEC] * len(args),
+        out_specs=[ANY_SPEC] + [VMEM_SPEC] * 2,
+        out_shape=[pltpu.HBM(q.shape, q.dtype)] + state_shapes(q, groups),
+        scratch_shapes=result_scratch(q, groups),
+        input_output_aliases={len(args) - 2: 1, len(args) - 1: 2},
+        compiler_params=KERNEL,
+        cost_estimate=cost(q, q.shape[1] * len(blocks)),
+        name="fold_or_finish",
+    )(*args)
+
+
+def finish_kernel(shift, groups, length_ref, q_ref, block0, block1, cross_ref, stat_ref, sum_ref, _, out_ref, held_ref, sems):
     heads = Heads(q_ref, groups)
     rows = heads.rows
     (number,), own = ring_blocks([shift])
     blocks = (block0, block1)
-    biases = [[position_bias(number, own, length_ref[i : i + 1], rows, False)] for i in range(heads.sequences)]
-
-    def score(sequence, group, h):
-        return rows_by_rows(blocks[sequence][0, :, key_columns(group)], heads.queries(sequence, group, h))
-
-    def weigh_unit(sequence, group, h, scores):
-        part = heads.part(h)
-        old = stat_ref[sequence, group, 0:1, part]
-        best, total, weights = weigh_heads(scores, biases[sequence], rows, heads.chunk, old)
-        shrink = jnp.exp2((old - best) * EXP2_SCALE)
-        over = 1.0 / (stat_ref[sequence, group, 1:2, part] * shrink + total)
-        return shrink * over, over, weights
-
-    def collect(sequence, group, h, old_factor, factor, weights):
-        part = heads.part(h)
-        added = columns_by_columns(blocks[sequence][0, :, value_columns(group)], weights)
-        out = sum_ref[sequence, group, :, part] * old_factor + added * factor + cross_ref[sequence, group, :, part]
-        for j in range(heads.chunk):
-            first = (group * heads.heads + h + j) * HEAD_SIZE
-            out_ref[sequence, :, first : first + HEAD_SIZE] = out[:, j * rows : (j + 1) * rows].T.astype(jnp.bfloat16)
-
-    in_turn(heads.units, score, weigh_unit, collect)
-
-
-def finish_rows(lengths, q, shift, blocks, cross, state):
+
+    def work():
+        biases = [[position_bias(number, own, length_ref[i : i + 1], rows, False)] for i in range(heads.sequences)]
+        results = Results(heads, out_ref, held_ref, sems)
+
+        def score(sequence, group, h):
+            return rows_by_rows(blocks[sequence][0, :, key_columns(group)], heads.queries(sequence, group, h))
+
+        def weigh_unit(sequence, group, h, scores):
+            part = heads.part(h)
+            old = stat_ref[sequence, group, 0:1, part]
+            best, total, weights = weigh_heads(scores, biases[sequence], rows, heads.chunk, old)
+            shrink = jnp.exp2((old - best) * EXP2_SCALE)
+            over = 1.0 / (stat_ref[sequence, group, 1:2, part] * shrink + total)
+            return shrink * over, over, weights
+
+        def collect(sequence, group, h, old_factor, factor, weights):
+            part = heads.part(h)
+            added = columns_by_columns(blocks[sequence][0, :, value_columns(group)], weights)
+            out = sum_ref[sequence, group, :, part] * old_factor + added * factor + cross_ref[sequence, group, :, part]
+            results.put(sequence, group, h, out)
+
+        in_turn(heads.units, score, weigh_unit, collect)
+        results.wait()
+
+    pl.when(number < own)(work)
+
+
+def finish_rows(lengths, q, shift, blocks, cross, state, result):
     groups = blocks[0].shape[2] // (2 * HEAD_SIZE)
     args = in_vmem(lengths, q, *blocks, cross, *state)
     return pl.pallas_call(
         functools.partial(finish_kernel, shift, groups),
-        in_specs=[VMEM_SPEC] * len(args),
-        out_specs=VMEM_SPEC,
-        out_shape=jax.ShapeDtypeStruct(q.shape, q.dtype),
+        in_specs=[VMEM_SPEC] * len(args) + [ANY_SPEC],
+        out_specs=ANY_SPEC,
+        out_shape=pltpu.HBM(q.shape, q.dtype),
+        scratch_shapes=result_scratch(q, groups),
+        input_output_aliases={len(args): 0},
         compiler_params=KERNEL,
         cost_estimate=cost(q, q.shape[1]),
         name="finish_rows",
-    )(*args)
+    )(*args, result)
 
 
 def load_kernel(lengths, gate, q_ref, image_ref, limit_ref, factor_ref, q_out, image_out, counts, gates, sems):
@@ -492,8 +566,8 @@
     f4, b4 = half_of_each(after(f3, state[0], *images), b3)
     f4, b4 = ring_forward(f4), ring_backward(b4)
     cross = cross_attend(factors, q, images, groups)
-    state = fold_blocks(limits, q, [f3, b3], (-3, 3), state)
-    return finish_rows(limits, q, 4, [f4, b4], cross, state)
+    result, *state = fold_or_finish(limits, q, [f3, b3], (-3, 3), 4, cross, state)
+    return finish_rows(limits, q, 4, [f4, b4], cross, state, result)
 
 
 def solution(mesh):

time: 37.5 us -> 36.3 us (0.968)
  the two profiles are of different devices: /device:TPU:0 before, /device:TPU:4 now
where the time goes in v3:
time: 36.3 us; the launch traced here: 36.1 us
  starting transfers between devices  16.4 us (45%)
  Pallas kernels  11.5 us (32%)
  waiting for transfers between devices  6.8 us (19%)
  local copies, waits for them, and re-layouts  1.24 us (3%)
    ppermute x6, starting transfers between devices, swapped(): lax.ppermute(rows, name, [(i, i ^ bits) for i in range(lax.axis_size(name...  8.23 us
    ppermute x4, starting transfers between devices, ring_backward(): return lax.ppermute(block, ('ctx', 'section'), pairs)  5.35 us
    ppermute x6, waiting for transfers between devices, swapped(): lax.ppermute(rows, name, [(i, i ^ bits) for i in range(lax.axis_size(name...  4.85 us
    pallas_call x2, Pallas kernels, fold_blocks(): pl.pallas_call(functools.partial(fold_kernel, first, shifts, groups), in_...  4.71 us
    ppermute x4, starting transfers between devices, ring_forward(): return lax.ppermute(block, ('ctx', 'section'), pairs)  2.86 us
    pallas_call x1, Pallas kernels, finish_rows(): pl.pallas_call(functools.partial(finish_kernel, shift, groups), in_specs=...  2.43 us
    pallas_call x1, Pallas kernels, fold_or_finish(): pl.pallas_call(functools.partial(fold_or_finish_kernel, shifts, last_shif...  2.21 us
    ppermute x4, waiting for transfers between devices, ring_backward(): return lax.ppermute(block, ('ctx', 'section'), pairs)  1.94 us
  transfers between devices with their start and end apart: 14, of which 5 were waited for; matrix products, arithmetic and copies ran while one was open for 0% of the time, Pallas kernels for 25%

profile of v3, /device:TPU:4, one launch (start us, length us, event | category | flops | bytes accessed | tf_op | source)
XLA Modules:
  0.0 36.1 jit_solution(3591485358087283881)
XLA Ops:
  0.0 0.0 copy-start
  0.0 1.2 %copy-done = bf16[2,128,2048]{2,1,0:T(8,128)(2,1)S(1)} copy-done((bf16[2,128,2048]{2,1,0:T(8,128)(2,1)S(1)}, bf16[2,128,2048]{2,1,0:T(8,128)(2,1)}, u32[]{:S(2)}) %copy-start) | copy-done | bytes 1048600
  1.2 0.1 collective-permute-start
  1.3 2.0 %collective-permute-start.3 = (bf16[2,128,512]{2,1,0:T(8,128)(2,1)S(1)}, bf16[2,128,512]{2,1,0:T(8,128)(2,1)S(1)}, u32[]{:S(2)}, u32[]{:S(2)}) collective-permute-start(bf16[2,128,512]{2,1,0:T(8,128)(2,1)S(1)} %constant_dynamic-slice_fusion.refs_0_), channel_id=1, source_target_pairs={{1,0},{2,1},{3,2},{19,3},{18,19},{17,18},{16,17},{0,16},{5,4},{6,5... | collective-permute-start | bytes 786440 | tf_op jit(solution)/shard_map/ppermute | solution.py:534
  3.3 2.6 %collective-permute-start.1 = (bf16[1,2048]{1,0:T(2,128)(2,1)}, bf16[1,2048]{1,0:T(2,128)(2,1)S(1)}, u32[]{:S(2)}, u32[]{:S(2)}) collective-permute-start(bf16[1,2048]{1,0:T(2,128)(2,1)} %image_ref.1), channel_id=1, source_target_pairs={{0,2},{1,3},{2,0},{3,1},{4,6},{5,7},{6,4},{7,5},{8,10},{9,11},{10,... | collective-permute-start | bytes 12296 | tf_op jit(solution)/shard_map/ppermute | solution.py:542
  5.9 1.3 %load_inputs.1 = (s32[2,128]{1,0:T(2,128)S(1)}, f32[16,128]{1,0:T(8,128)S(1)}, bf16[2,128,2048]{2,1,0:T(8,128)(2,1)S(1)}, bf16[1,2048]{1,0:T(2,128)(2,1)S(1)}) custom-call(s32[2]{0:T(128)} %lengths.1, f32[16]{0:T(128)} %gate.1, bf16[2,128,2048]{2,1,0:T(8,128)(2,1)} %q_ref.1, bf16[1,2048]{1,0:T(2,128)(2,1)} %image_ref.1), custom_call_target="tpu_custom_call" | custom-call | tf_op jit(solution)/shard_map/load_inputs/pallas_call | solution.py:487
  7.2 3.4 %collective-permute-done.1 = bf16[1,2048]{1,0:T(2,128)(2,1)S(1)} collective-permute-done((bf16[1,2048]{1,0:T(2,128)(2,1)}, bf16[1,2048]{1,0:T(2,128)(2,1)S(1)}, u32[]{:S(2)}, u32[]{:S(2)}) %collective-permute-start.1) | collective-permute-done | bytes 4128 | tf_op jit(solution)/shard_map/ppermute | solution.py:542
  10.6 1.6 %collective-permute-start.4 = (bf16[2,2048]{1,0:T(2,128)(2,1)S(1)}, bf16[2,2048]{1,0:T(2,128)(2,1)S(1)}, u32[]{:S(2)}, u32[]{:S(2)}) collective-permute-start(bf16[2,2048]{1,0:T(2,128)(2,1)S(1)} %pad_maximum_fusion.2), channel_id=1, source_target_pairs={{0,1},{1,0},{2,3},{3,2},{4,5},{5,4},{6,7},{7,6},{8,9},{9,8},{10,11... | collective-permute-start | bytes 24584 | tf_op jit(solution)/shard_map/ppermute | solution.py:542
  12.2 0.0 collective-permute-done.refs_1_
  12.2 1.8 %collective-permute-start.2 = (bf16[2,128,512]{2,1,0:T(8,128)(2,1)S(1)}, bf16[2,128,512]{2,1,0:T(8,128)(2,1)S(1)}, u32[]{:S(2)}, u32[]{:S(2)}) collective-permute-start(bf16[2,128,512]{2,1,0:T(8,128)(2,1)S(1)} %collective-permute-done.refs_1_), channel_id=1, source_target_pairs={{0,1},{1,2},{2,3},{3,19},{19,18},{18,17},{17,16},{16,0},{4,5},{5,6... | collective-permute-start | bytes 786440 | tf_op jit(solution)/shard_map/ppermute | solution.py:529
  14.0 0.0 collective-permute-done.3.refs_2_
  14.0 0.2 collective-permute-start.6
  14.2 0.2 collective-permute-done.4
  14.5 1.9 %collective-permute-start.7 = (bf16[4,2048]{1,0:T(4,128)(2,1)S(1)}, bf16[4,2048]{1,0:T(4,128)(2,1)S(1)}, u32[]{:S(2)}, u32[]{:S(2)}) collective-permute-start(bf16[4,2048]{1,0:T(4,128)(2,1)S(1)} %pad_maximum_fusion.1), channel_id=1, source_target_pairs={{0,16},{16,0},{1,17},{17,1},{2,18},{18,2},{3,19},{19,3},{4,20},{20... | collective-permute-start | bytes 49160 | tf_op jit(solution)/shard_map/ppermute | solution.py:542
  16.4 2.5 %fold_blocks.2 = (f32[2,2,2,1024]{3,2,1,0:T(2,128)S(1)}, f32[2,2,128,1024]{3,2,1,0:T(8,128)S(1)}) custom-call(s32[2,128]{1,0:T(2,128)S(1)} %get-tuple-element.25.length_ref, bf16[2,128,2048]{2,1,0:T(8,128)(2,1)S(1)} %get-tuple-element.26.q_ref, bf16[2,128,512]{2,1,0:T(8,128)(2,1)S(1)} %constant_dynamic-slice_fusion.refs_0_, ...), custom_call_target="tpu_custom_call" | custom-call | flops 805306368 | bytes 1048576 | tf_op jit(solution)/shard_map/fold_blocks/pallas_call | solution.py:304
  18.9 0.0 collective-permute-done.2.refs_0_
  18.9 1.6 %collective-permute-done.6.refs_1_ = bf16[2,128,512]{2,1,0:T(8,128)(2,1)S(1)} collective-permute-done((bf16[2,128,512]{2,1,0:T(8,128)(2,1)S(1)}, bf16[2,128,512]{2,1,0:T(8,128)(2,1)S(1)}, u32[]{:S(2)}, u32[]{:S(2)}) %collective-permute-start.6) | collective-permute-done | bytes 262176 | tf_op jit(solution)/shard_map/ppermute | solution.py:534
  20.5 0.5 %collective-permute-start.5 = (bf16[2,128,512]{2,1,0:T(8,128)(2,1)S(1)}, bf16[2,128,512]{2,1,0:T(8,128)(2,1)S(1)}, u32[]{:S(2)}, u32[]{:S(2)}) collective-permute-start(bf16[2,128,512]{2,1,0:T(8,128)(2,1)S(1)} %collective-permute-done.2.refs_0_), channel_id=1, source_target_pairs={{0,1},{1,2},{2,3},{3,19},{19,18},{18,17},{17,16},{16,0},{4,5},{5,6... | collective-permute-start | bytes 786440 | tf_op jit(solution)/shard_map/ppermute | solution.py:529
  21.0 1.6 %collective-permute-start.11 = (bf16[2,128,512]{2,1,0:T(8,128)(2,1)S(1)}, bf16[2,128,512]{2,1,0:T(8,128)(2,1)S(1)}, u32[]{:S(2)}, u32[]{:S(2)}) collective-permute-start(bf16[2,128,512]{2,1,0:T(8,128)(2,1)S(1)} %collective-permute-done.6.refs_1_), channel_id=1, source_target_pairs={{1,0},{2,1},{3,2},{19,3},{18,19},{17,18},{16,17},{0,16},{5,4},{6,5... | collective-permute-start | bytes 786440 | tf_op jit(solution)/shard_map/ppermute | solution.py:534
  22.6 0.0 collective-permute-done.7
  22.6 0.1 collective-permute-start.10
  22.7 1.6 %collective-permute-start.8 = (bf16[8,2048]{1,0:T(8,128)(2,1)S(1)}, bf16[8,2048]{1,0:T(8,128)(2,1)S(1)}, u32[]{:S(2)}, u32[]{:S(2)}) collective-permute-start(bf16[8,2048]{1,0:T(8,128)(2,1)S(1)} %pad_maximum_fusion.refs_0_), channel_id=1, source_target_pairs={{0,4},{4,0},{8,12},{12,8},{1,5},{5,1},{9,13},{13,9},{2,6},{6,2},{1... | collective-permute-start | bytes 98312 | tf_op jit(solution)/shard_map/ppermute | solution.py:542
  24.3 0.5 %collective-permute-start.9 = (bf16[8,2048]{1,0:T(8,128)(2,1)S(1)}, bf16[8,2048]{1,0:T(8,128)(2,1)S(1)}, u32[]{:S(2)}, u32[]{:S(2)}) collective-permute-start(bf16[8,2048]{1,0:T(8,128)(2,1)S(1)} %pad_maximum_fusion.refs_0_), channel_id=1, source_target_pairs={{0,8},{4,12},{8,0},{12,4},{1,9},{5,13},{9,1},{13,5},{2,10},{6,14},... | collective-permute-start | bytes 98312 | tf_op jit(solution)/shard_map/ppermute | solution.py:542
  24.8 2.2 %fold_blocks.3 = (f32[2,2,2,1024]{3,2,1,0:T(2,128)S(1)}, f32[2,2,128,1024]{3,2,1,0:T(8,128)S(1)}) custom-call(s32[2,128]{1,0:T(2,128)S(1)} %get-tuple-element.25.length_ref, bf16[2,128,2048]{2,1,0:T(8,128)(2,1)S(1)} %get-tuple-element.26.q_ref, ...), custom_call_target="tpu_custom_call", output_to_operand_aliasing={{0}: (4, {}), {1}: (5, {})} | custom-call | flops 536870912 | bytes 1048576 | tf_op jit(solution)/shard_map/fold_blocks/pallas_call | solution.py:304
  27.0 0.0 collective-permute-done.10.refs_3_
  27.0 0.0 collective-permute-done.8.refs_1_
  27.0 1.2 %collective-permute-done.9.refs_2_ = bf16[8,2048]{1,0:T(8,128)(2,1)S(1)} collective-permute-done((bf16[8,2048]{1,0:T(8,128)(2,1)S(1)}, bf16[8,2048]{1,0:T(8,128)(2,1)S(1)}, u32[]{:S(2)}, u32[]{:S(2)}) %collective-permute-start.9) | collective-permute-done | bytes 32800 | tf_op jit(solution)/shard_map/ppermute | solution.py:542
  28.2 0.0 collective-permute-done.5.forward_ref.refs_0_
  28.2 0.0 collective-permute-done.11.backward_ref.refs_1_
  28.2 0.5 %collective-permute-start.12 = (bf16[1,128,512]{2,1,0:T(8,128)(2,1)S(1)}, bf16[1,128,512]{2,1,0:T(8,128)(2,1)S(1)}, u32[]{:S(2)}, u32[]{:S(2)}) collective-permute-start(bf16[1,128,512]{2,1,0:T(8,128)(2,1)S(1)} %get-tuple-element.38), channel_id=1, source_target_pairs={{0,1},{1,2},{2,3},{3,19},{19,18},{18,17},{17,16},{16,0},{4,5},{5,6... | collective-permute-start | bytes 393224 | tf_op jit(solution)/shard_map/ppermute | solution.py:529
  28.7 1.6 %collective-permute-start.13 = (bf16[1,128,512]{2,1,0:T(8,128)(2,1)S(1)}, bf16[1,128,512]{2,1,0:T(8,128)(2,1)S(1)}, u32[]{:S(2)}, u32[]{:S(2)}) collective-permute-start(bf16[1,128,512]{2,1,0:T(8,128)(2,1)S(1)} %get-tuple-element.39), channel_id=1, source_target_pairs={{1,0},{2,1},{3,2},{19,3},{18,19},{17,18},{16,17},{0,16},{5,4},{6,5... | collective-permute-start | bytes 393224 | tf_op jit(solution)/shard_map/ppermute | solution.py:534
  30.3 0.8 %cross_attend.1.refs_2_.cross_ref = f32[2,2,128,1024]{3,2,1,0:T(8,128)S(1)} custom-call(f32[16,128]{1,0:T(8,128)S(1)} %get-tuple-element.40.factor_ref, bf16[2,128,2048]{2,1,0:T(8,128)(2,1)S(1)} %get-tuple-element.26.q_ref, bf16[8,2048]{1,0:T(8,128)(2,1)S(1)} %pad_maximum_fusion.refs_0_, bf16[8,2048]{1,0:T(8,128)(2,1)S(1)} %collective-permute-done.8.refs_1_, ...), custom_call_target="tpu_custom_call" | custom-call | flops 268435456 | bytes 1048576 | tf_op jit(solution)/shard_map/cross_attend/pallas_call | solution.py:340
  31.1 2.2 %fold_or_finish.1 = (bf16[2,128,2048]{2,1,0:T(8,128)(2,1)}, f32[2,2,2,1024]{3,2,1,0:T(2,128)S(1)}, f32[2,2,128,1024]{3,2,1,0:T(8,128)S(1)}) custom-call(s32[2,128]{1,0:T(2,128)S(1)} %get-tuple-element.25.length_ref, bf16[2,128,2048]{2,1,0:T(8,128)(2,1)S(1)} %get-tuple-element.26.q_ref, ...), custom_call_target="tpu_custom_call", output_to_operand_aliasing={{1}: (5, {}), {2}: (6, {})} | custom-call | flops 536870912 | bytes 1048576 | tf_op jit(solution)/shard_map/fold_or_finish/pallas_call | solution.py:406
  33.4 0.0 collective-permute-done.12.block0
  33.4 0.3 collective-permute-done.13.block1
  33.7 2.4 %finish_rows.1 = bf16[2,128,2048]{2,1,0:T(8,128)(2,1)} custom-call(s32[2,128]{1,0:T(2,128)S(1)} %get-tuple-element.25.length_ref, bf16[2,128,2048]{2,1,0:T(8,128)(2,1)S(1)} %get-tuple-element.26.q_ref, bf16[1,128,512]{2,1,0:T(8,128)(2,1)S(1)} %collective-permute-done.12.block0, ...), custom_call_target="tpu_custom_call", output_to_operand_aliasing={{}: (7, {})} | custom-call | flops 268435456 | bytes 1048576 | tf_op jit(solution)/shard_map/finish_rows/pallas_call | solution.py:455
  (5 shorter events, 0.1 us)
Async XLA Ops:
  0.0 1.2 %copy-start = (bf16[2,128,2048]{2,1,0:T(8,128)(2,1)S(1)}, bf16[2,128,2048]{2,1,0:T(8,128)(2,1)}, u32[]{:S(2)}) copy-start(bf16[2,128,2048]{2,1,0:T(8,128)(2,1)} %param.6) | copy-start | bytes 3145732
  1.2 11.0 %collective-permute-start = (bf16[2,128,512]{2,1,0:T(8,128)(2,1)S(1)}, bf16[2,128,512]{2,1,0:T(8,128)(2,1)S(1)}, u32[]{:S(2)}, u32[]{:S(2)}) collective-permute-start(bf16[2,128,512]{2,1,0:T(8,128)(2,1)S(1)} %constant_dynamic-slice_fusion.refs_0_), channel_id=1, source_target_pairs={{0,1},{1,2},{2,3},{3,19},{19,18},{18,17},{17,16},{16,0},{4,5},{5,6... | collective-permute-start | bytes 786440 | tf_op jit(solution)/shard_map/ppermute | solution.py:529
  1.3 12.7 %collective-permute-start.3 = (bf16[2,128,512]{2,1,0:T(8,128)(2,1)S(1)}, bf16[2,128,512]{2,1,0:T(8,128)(2,1)S(1)}, u32[]{:S(2)}, u32[]{:S(2)}) collective-permute-start(bf16[2,128,512]{2,1,0:T(8,128)(2,1)S(1)} %constant_dynamic-slice_fusion.refs_0_), channel_id=1, source_target_pairs={{1,0},{2,1},{3,2},{19,3},{18,19},{17,18},{16,17},{0,16},{5,4},{6,5... | collective-permute-start | bytes 786440 | tf_op jit(solution)/shard_map/ppermute | solution.py:534
  3.3 7.3 %collective-permute-start.1 = (bf16[1,2048]{1,0:T(2,128)(2,1)}, bf16[1,2048]{1,0:T(2,128)(2,1)S(1)}, u32[]{:S(2)}, u32[]{:S(2)}) collective-permute-start(bf16[1,2048]{1,0:T(2,128)(2,1)} %image_ref.1), channel_id=1, source_target_pairs={{0,2},{1,3},{2,0},{3,1},{4,6},{5,7},{6,4},{7,5},{8,10},{9,11},{10,... | collective-permute-start | bytes 12296 | tf_op jit(solution)/shard_map/ppermute | solution.py:542
  10.6 3.8 %collective-permute-start.4 = (bf16[2,2048]{1,0:T(2,128)(2,1)S(1)}, bf16[2,2048]{1,0:T(2,128)(2,1)S(1)}, u32[]{:S(2)}, u32[]{:S(2)}) collective-permute-start(bf16[2,2048]{1,0:T(2,128)(2,1)S(1)} %pad_maximum_fusion.2), channel_id=1, source_target_pairs={{0,1},{1,0},{2,3},{3,2},{4,5},{5,4},{6,7},{7,6},{8,9},{9,8},{10,11... | collective-permute-start | bytes 24584 | tf_op jit(solution)/shard_map/ppermute | solution.py:542
  12.2 6.7 %collective-permute-start.2 = (bf16[2,128,512]{2,1,0:T(8,128)(2,1)S(1)}, bf16[2,128,512]{2,1,0:T(8,128)(2,1)S(1)}, u32[]{:S(2)}, u32[]{:S(2)}) collective-permute-start(bf16[2,128,512]{2,1,0:T(8,128)(2,1)S(1)} %collective-permute-done.refs_1_), channel_id=1, source_target_pairs={{0,1},{1,2},{2,3},{3,19},{19,18},{18,17},{17,16},{16,0},{4,5},{5,6... | collective-permute-start | bytes 786440 | tf_op jit(solution)/shard_map/ppermute | solution.py:529
  14.0 6.5 %collective-permute-start.6 = (bf16[2,128,512]{2,1,0:T(8,128)(2,1)S(1)}, bf16[2,128,512]{2,1,0:T(8,128)(2,1)S(1)}, u32[]{:S(2)}, u32[]{:S(2)}) collective-permute-start(bf16[2,128,512]{2,1,0:T(8,128)(2,1)S(1)} %collective-permute-done.3.refs_2_), channel_id=1, source_target_pairs={{1,0},{2,1},{3,2},{19,3},{18,19},{17,18},{16,17},{0,16},{5,4},{6,5... | collective-permute-start | bytes 786440 | tf_op jit(solution)/shard_map/ppermute | solution.py:534
  14.5 8.1 %collective-permute-start.7 = (bf16[4,2048]{1,0:T(4,128)(2,1)S(1)}, bf16[4,2048]{1,0:T(4,128)(2,1)S(1)}, u32[]{:S(2)}, u32[]{:S(2)}) collective-permute-start(bf16[4,2048]{1,0:T(4,128)(2,1)S(1)} %pad_maximum_fusion.1), channel_id=1, source_target_pairs={{0,16},{16,0},{1,17},{17,1},{2,18},{18,2},{3,19},{19,3},{4,20},{20... | collective-permute-start | bytes 49160 | tf_op jit(solution)/shard_map/ppermute | solution.py:542
  20.5 7.7 %collective-permute-start.5 = (bf16[2,128,512]{2,1,0:T(8,128)(2,1)S(1)}, bf16[2,128,512]{2,1,0:T(8,128)(2,1)S(1)}, u32[]{:S(2)}, u32[]{:S(2)}) collective-permute-start(bf16[2,128,512]{2,1,0:T(8,128)(2,1)S(1)} %collective-permute-done.2.refs_0_), channel_id=1, source_target_pairs={{0,1},{1,2},{2,3},{3,19},{19,18},{18,17},{17,16},{16,0},{4,5},{5,6... | collective-permute-start | bytes 786440 | tf_op jit(solution)/shard_map/ppermute | solution.py:529
  21.0 7.2 %collective-permute-start.11 = (bf16[2,128,512]{2,1,0:T(8,128)(2,1)S(1)}, bf16[2,128,512]{2,1,0:T(8,128)(2,1)S(1)}, u32[]{:S(2)}, u32[]{:S(2)}) collective-permute-start(bf16[2,128,512]{2,1,0:T(8,128)(2,1)S(1)} %collective-permute-done.6.refs_1_), channel_id=1, source_target_pairs={{1,0},{2,1},{3,2},{19,3},{18,19},{17,18},{16,17},{0,16},{5,4},{6,5... | collective-permute-start | bytes 786440 | tf_op jit(solution)/shard_map/ppermute | solution.py:534
  22.6 4.4 %collective-permute-start.10 = (bf16[8,2048]{1,0:T(8,128)(2,1)S(1)}, bf16[8,2048]{1,0:T(8,128)(2,1)S(1)}, u32[]{:S(2)}, u32[]{:S(2)}) collective-permute-start(bf16[8,2048]{1,0:T(8,128)(2,1)S(1)} %pad_maximum_fusion.refs_0_), channel_id=1, source_target_pairs={{0,12},{4,8},{8,4},{12,0},{1,13},{5,9},{9,5},{13,1},{2,14},{6,10},... | collective-permute-start | bytes 98312 | tf_op jit(solution)/shard_map/ppermute | solution.py:542
  22.7 4.3 %collective-permute-start.8 = (bf16[8,2048]{1,0:T(8,128)(2,1)S(1)}, bf16[8,2048]{1,0:T(8,128)(2,1)S(1)}, u32[]{:S(2)}, u32[]{:S(2)}) collective-permute-start(bf16[8,2048]{1,0:T(8,128)(2,1)S(1)} %pad_maximum_fusion.refs_0_), channel_id=1, source_target_pairs={{0,4},{4,0},{8,12},{12,8},{1,5},{5,1},{9,13},{13,9},{2,6},{6,2},{1... | collective-permute-start | bytes 98312 | tf_op jit(solution)/shard_map/ppermute | solution.py:542
  24.3 3.9 %collective-permute-start.9 = (bf16[8,2048]{1,0:T(8,128)(2,1)S(1)}, bf16[8,2048]{1,0:T(8,128)(2,1)S(1)}, u32[]{:S(2)}, u32[]{:S(2)}) collective-permute-start(bf16[8,2048]{1,0:T(8,128)(2,1)S(1)} %pad_maximum_fusion.refs_0_), channel_id=1, source_target_pairs={{0,8},{4,12},{8,0},{12,4},{1,9},{5,13},{9,1},{13,5},{2,10},{6,14},... | collective-permute-start | bytes 98312 | tf_op jit(solution)/shard_map/ppermute | solution.py:542
  28.2 5.1 %collective-permute-start.12 = (bf16[1,128,512]{2,1,0:T(8,128)(2,1)S(1)}, bf16[1,128,512]{2,1,0:T(8,128)(2,1)S(1)}, u32[]{:S(2)}, u32[]{:S(2)}) collective-permute-start(bf16[1,128,512]{2,1,0:T(8,128)(2,1)S(1)} %get-tuple-element.38), channel_id=1, source_target_pairs={{0,1},{1,2},{2,3},{3,19},{19,18},{18,17},{17,16},{16,0},{4,5},{5,6... | collective-permute-start | bytes 393224 | tf_op jit(solution)/shard_map/ppermute | solution.py:529
  28.7 5.0 %collective-permute-start.13 = (bf16[1,128,512]{2,1,0:T(8,128)(2,1)S(1)}, bf16[1,128,512]{2,1,0:T(8,128)(2,1)S(1)}, u32[]{:S(2)}, u32[]{:S(2)}) collective-permute-start(bf16[1,128,512]{2,1,0:T(8,128)(2,1)S(1)} %get-tuple-element.39), channel_id=1, source_target_pairs={{1,0},{2,1},{3,2},{19,3},{18,19},{17,18},{16,17},{0,16},{5,4},{6,5... | collective-permute-start | bytes 393224 | tf_op jit(solution)/shard_map/ppermute | solution.py:534

commit v4 on v2

--- a/solution.py
+++ b/solution.py
@@ -271,15 +271,25 @@
     in_turn(heads.units, score, weigh_unit, collect)
 
 
+def fold_useful(heads, length_ref, blocks, numbers, own, old_state, state):
+    ahead = len(blocks) - 2
+    useful = [number < own for number in numbers[ahead:]]
+
+    def work(*chosen):
+        chosen = [*range(ahead), *(ahead + i for i in chosen)]
+        fold(heads, length_ref, [blocks[i] for i in chosen], [numbers[i] for i in chosen], own, old_state, state)
+
+    pl.when(useful[0] & useful[1])(lambda: work(0, 1))
+    pl.when(useful[1] & ~useful[0])(lambda: work(1))
+    one = useful[0] | ~useful[1] if ahead else useful[0]
+    pl.when(one & ~useful[1])(lambda: work(0))
+
+
 def fold_kernel(first, shifts, groups, length_ref, q_ref, *refs):
     blocks = refs[: len(shifts)]
     numbers, own = ring_blocks(shifts)
     heads = Heads(q_ref, groups)
-    if first:
-        fold(heads, length_ref, blocks, numbers, own, None, refs[-2:])
-    else:
-        useful = functools.reduce(jnp.logical_or, [number < own for number in numbers])
-        pl.when(useful)(lambda: fold(heads, length_ref, blocks, numbers, own, refs[-4:-2], refs[-2:]))
+    fold_useful(heads, length_ref, blocks, numbers, own, None if first else refs[-4:-2], refs[-2:])
 
 
 def state_shapes(q, groups):
@@ -348,47 +358,151 @@
     )(*in_vmem(factors, q, *images))
 
 
-def finish_kernel(shift, groups, length_ref, q_ref, block0, block1, cross_ref, stat_ref, sum_ref, out_ref):
+def turned(out, rows):
+    heads = [out[:, first : first + rows].T for first in range(0, out.shape[1], rows)]
+    return jnp.concatenate(heads, 1).astype(jnp.bfloat16)
+
+
+class Results:
+    def __init__(self, heads, out_ref, held_ref, sems):
+        self.heads, self.out_ref, self.held_ref, self.sems = heads, out_ref, held_ref, sems
+        self.copies = []
+
+    def put(self, sequence, group, h, out):
+        heads = self.heads
+        first = (group * heads.heads + h) * HEAD_SIZE
+        self.held_ref[sequence, :, first : first + heads.chunk * HEAD_SIZE] = turned(out, heads.rows)
+        if h + heads.chunk == heads.heads:
+            width = heads.heads * HEAD_SIZE
+            at = (sequence, slice(None), pl.ds(group * width, width))
+            self.send(self.held_ref.at[at], at, self.sems.at[sequence, group])
+
+    def send(self, source, at, sem):
+        copy = pltpu.make_async_copy(source, self.out_ref.at[at], sem)
+        copy.start()
+        self.copies.append(copy)
+
+    def wait(self):
+        for copy in self.copies:
+            copy.wait()
+
+
+def result_scratch(q, groups):
+    return [pltpu.VMEM(q.shape, q.dtype), pltpu.SemaphoreType.DMA((q.shape[0], groups))]
+
+
+def early_kernel(last_shift, groups, q_ref, cross_ref, stat_ref, sum_ref, out_ref, held_ref, sems):
+    (last,), own = ring_blocks([last_shift])
     heads = Heads(q_ref, groups)
+
+    def write():
+        results = Results(heads, out_ref, held_ref, sems)
+        for sequence, group, h in heads.units:
+            part = heads.part(h)
+            over = 1.0 / stat_ref[sequence, group, 1:2, part]
+            results.put(
+                sequence, group, h, sum_ref[sequence, group, :, part] * over + cross_ref[sequence, group, :, part]
+            )
+        results.wait()
+
+    pl.when(last > own)(write)
+
+
+def early_rows(q, last_shift, groups, cross, state):
+    args = in_vmem(q, cross, *state)
+    return pl.pallas_call(
+        functools.partial(early_kernel, last_shift, groups),
+        in_specs=[VMEM_SPEC] * len(args),
+        out_specs=ANY_SPEC,
+        out_shape=pltpu.HBM(q.shape, q.dtype),
+        scratch_shapes=result_scratch(q, groups),
+        compiler_params=KERNEL,
+        cost_estimate=cost(q, q.shape[1] // 4),
+        name="early_rows",
+    )(*args)
+
+
+def last_block(heads, sequence, shift, length_ref, block, cross_ref, stat_ref, sum_ref, put):
     rows = heads.rows
     (number,), own = ring_blocks([shift])
-    blocks = (block0, block1)
-    biases = [[position_bias(number, own, length_ref[i : i + 1], rows, False)] for i in range(heads.sequences)]
+    biases = [position_bias(number, own, length_ref[sequence : sequence + 1], rows, False)]
 
     def score(sequence, group, h):
-        return rows_by_rows(blocks[sequence][0, :, key_columns(group)], heads.queries(sequence, group, h))
+        return rows_by_rows(block[0, :, key_columns(group)], heads.queries(sequence, group, h))
 
     def weigh_unit(sequence, group, h, scores):
         part = heads.part(h)
         old = stat_ref[sequence, group, 0:1, part]
-        best, total, weights = weigh_heads(scores, biases[sequence], rows, heads.chunk, old)
+        best, total, weights = weigh_heads(scores, biases, rows, heads.chunk, old)
         shrink = jnp.exp2((old - best) * EXP2_SCALE)
         over = 1.0 / (stat_ref[sequence, group, 1:2, part] * shrink + total)
         return shrink * over, over, weights
 
     def collect(sequence, group, h, old_factor, factor, weights):
         part = heads.part(h)
-        added = columns_by_columns(blocks[sequence][0, :, value_columns(group)], weights)
+        added = columns_by_columns(block[0, :, value_columns(group)], weights)
         out = sum_ref[sequence, group, :, part] * old_factor + added * factor + cross_ref[sequence, group, :, part]
-        for j in range(heads.chunk):
-            first = (group * heads.heads + h + j) * HEAD_SIZE
-            out_ref[sequence, :, first : first + HEAD_SIZE] = out[:, j * rows : (j + 1) * rows].T.astype(jnp.bfloat16)
-
-    in_turn(heads.units, score, weigh_unit, collect)
-
-
-def finish_rows(lengths, q, shift, blocks, cross, state):
-    groups = blocks[0].shape[2] // (2 * HEAD_SIZE)
-    args = in_vmem(lengths, q, *blocks, cross, *state)
-    return pl.pallas_call(
-        functools.partial(finish_kernel, shift, groups),
+        put(sequence, group, h, out)
+
+    in_turn([unit for unit in heads.units if unit[0] == sequence], score, weigh_unit, collect)
+
+
+def first_finish_kernel(shift, groups, length_ref, q_ref, block, cross_ref, stat_ref, sum_ref, rows_ref):
+    heads = Heads(q_ref, groups)
+    (number,), own = ring_blocks([shift])
+
+    def put(sequence, group, h, out):
+        first = (group * heads.heads + h) * HEAD_SIZE
+        rows_ref[:, first : first + heads.chunk * HEAD_SIZE] = turned(out, heads.rows)
+
+    pl.when(number < own)(
+        lambda: last_block(heads, 0, shift, length_ref, block, cross_ref, stat_ref, sum_ref, put)
+    )
+
+
+def first_finish(lengths, q, shift, block, cross, state):
+    groups = block.shape[2] // (2 * HEAD_SIZE)
+    args = in_vmem(lengths, q, block, cross, *state)
+    return pl.pallas_call(
+        functools.partial(first_finish_kernel, shift, groups),
         in_specs=[VMEM_SPEC] * len(args),
         out_specs=VMEM_SPEC,
-        out_shape=jax.ShapeDtypeStruct(q.shape, q.dtype),
-        compiler_params=KERNEL,
-        cost_estimate=cost(q, q.shape[1]),
-        name="finish_rows",
+        out_shape=pltpu.VMEM(q.shape[1:], q.dtype),
+        compiler_params=KERNEL,
+        cost_estimate=cost(q, q.shape[1] // 2),
+        name="first_finish",
     )(*args)
+
+
+def second_finish_kernel(
+    shift, groups, length_ref, q_ref, block, cross_ref, stat_ref, sum_ref, rows_ref, _, out_ref, held_ref, sems
+):
+    heads = Heads(q_ref, groups)
+    (number,), own = ring_blocks([shift])
+
+    def work():
+        results = Results(heads, out_ref, held_ref, sems)
+        results.send(rows_ref, 0, sems.at[0, 0])
+        last_block(heads, 1, shift, length_ref, block, cross_ref, stat_ref, sum_ref, results.put)
+        results.wait()
+
+    pl.when(number < own)(work)
+
+
+def second_finish(lengths, q, shift, block, cross, state, first_rows, result):
+    groups = block.shape[2] // (2 * HEAD_SIZE)
+    args = in_vmem(lengths, q, block, cross, *state, first_rows)
+    return pl.pallas_call(
+        functools.partial(second_finish_kernel, shift, groups),
+        in_specs=[VMEM_SPEC] * len(args) + [ANY_SPEC],
+        out_specs=ANY_SPEC,
+        out_shape=pltpu.HBM(q.shape, q.dtype),
+        scratch_shapes=result_scratch(q, groups),
+        input_output_aliases={len(args): 0},
+        compiler_params=KERNEL,
+        cost_estimate=cost(q, q.shape[1] // 2),
+        name="second_finish",
+    )(*args, result)
 
 
 def load_kernel(lengths, gate, q_ref, image_ref, limit_ref, factor_ref, q_out, image_out, counts, gates, sems):
@@ -430,21 +544,35 @@
     )(*[pltpu.with_memory_space_constraint(array, pltpu.HBM) for array in arrays])
 
 
-def halve_kernel(forward_ref, backward_ref, first_ref, second_ref):
-    first_ref[...] = forward_ref[0:1]
-    second_ref[...] = backward_ref[1:2]
-
-
-def half_of_each(forward, backward):
-    shape = pltpu.VMEM((1,) + forward.shape[1:], forward.dtype)
-    return pl.pallas_call(
-        halve_kernel,
+def join_kernel(first_ref, second_ref, joined_ref):
+    rows = [r[...].astype(jnp.float32) for r in (first_ref, second_ref)]
+    joined_ref[...] = jnp.concatenate(rows, 0).astype(joined_ref.dtype)
+
+
+def joined(first, second):
+    return pl.pallas_call(
+        join_kernel,
         in_specs=[VMEM_SPEC] * 2,
-        out_specs=[VMEM_SPEC] * 2,
-        out_shape=[shape] * 2,
-        compiler_params=KERNEL,
-        name="half_of_each",
-    )(*in_vmem(forward, backward))
+        out_specs=VMEM_SPEC,
+        out_shape=pltpu.VMEM((first.shape[0] + second.shape[0], first.shape[1]), first.dtype),
+        compiler_params=KERNEL,
+        name="joined",
+    )(*in_vmem(first, second))
+
+
+def half_kernel(sequence, block_ref, half_ref):
+    half_ref[...] = block_ref[sequence : sequence + 1]
+
+
+def half_of(block, sequence):
+    return pl.pallas_call(
+        functools.partial(half_kernel, sequence),
+        in_specs=[VMEM_SPEC],
+        out_specs=VMEM_SPEC,
+        out_shape=pltpu.VMEM((1,) + block.shape[1:], block.dtype),
+        compiler_params=KERNEL,
+        name="half_of",
+    )(*in_vmem(block))
 
 
 RING = (0, 1, 2, 3, 7, 6, 5, 4)
@@ -474,26 +602,29 @@
     kv_cols = groups * 2 * HEAD_SIZE
     own = lax.dynamic_slice_in_dim(self_kv, lax.axis_index("tp") * kv_cols, kv_cols, 2)
     f1, b1 = ring_forward(own), ring_backward(own)
-    i1 = swapped(image_kv, "section", 2)
+    sections = lax.axis_size("section")
+    n1 = swapped(image_kv, "section", 2)
+    n2 = swapped(image_kv, "ctx", 1)
+    n3 = swapped(image_kv, ("ctx", "section"), sections + 2)
     limits, factors, q, image1 = load_inputs(lengths, cross_gate, queries, image_kv)
-    image2 = jnp.concatenate([image1, i1], 0)
-    i2 = swapped(image2, "section", 1)
-
-    f2, b2 = ring_forward(after(f1, image2)), ring_backward(after(b1, image2))
-    image4 = jnp.concatenate([image2, i2], 0)
-    i3 = swapped(image4, "ctx", 1)
+
+    f2, b2 = ring_forward(f1), ring_backward(b1)
+    image4 = jnp.concatenate([image1, n1, n2, n3], 0)
+    far = swapped(image4, "section", 1)
     state = fold_blocks(limits, q, [own, f1, after(b1, image4)], (0, -1, 1), None)
 
-    f3, b3 = ring_forward(after(f2, state[0])), ring_backward(after(b2, state[0]))
-    image8 = jnp.concatenate([image4, i3], 0)
+    f3, b3 = ring_forward(after(f2, state[0], far)), ring_backward(after(b2, state[0], far))
+    image8 = joined(image4, far)
     images = [image8] + [swapped(image8, "tp", bits) for bits in range(1, tp_count)]
     state = fold_blocks(limits, q, [f2, after(b2, image8)], (-2, 2), state)
 
-    f4, b4 = half_of_each(after(f3, state[0], *images), b3)
-    f4, b4 = ring_forward(f4), ring_backward(b4)
+    f4 = ring_forward(half_of(after(f3, state[0]), 0))
+    b4 = ring_backward(half_of(after(b3, state[0], *images), 1))
     cross = cross_attend(factors, q, images, groups)
     state = fold_blocks(limits, q, [f3, b3], (-3, 3), state)
-    return finish_rows(limits, q, 4, [f4, b4], cross, state)
+    result = early_rows(q, 4, groups, cross, state)
+    first_rows = first_finish(limits, q, 4, f4, cross, state)
+    return second_finish(limits, q, 4, b4, cross, state, first_rows, result)
 
 
 def solution(mesh):

time: 37.5 us -> 32.6 us (0.87)
  starting transfers between devices: 18.9 us -> 16.8 us
  Pallas kernels: 7.34 us -> 5.37 us
  waiting for transfers between devices: 9.7 us -> 8.72 us
    ppermute x4, starting transfers between devices: 7.89 us -> 2.94 us  [ring_backward(): return lax.ppermute(block, ('ctx', 'section'), pairs)]
    ppermute x4, starting transfers between devices: 2.28 us -> 5.96 us  [ring_forward(): return lax.ppermute(block, ('ctx', 'section'), pairs)]
    ppermute x6 -> x7, waiting for transfers between devices: 5.62 us -> 3.59 us  [swapped(): lax.ppermute(rows, name, [(i, i ^ bits) for i in range(lax.axis_size(name...]
    pallas_call x2 -> x6, Pallas kernels: 2.66 us -> 1.23 us  [the longest x1 1.16 us: early_rows(): pl.pallas_call(functools.partial(early_kernel, last_shift, groups), in_sp...]
    ppermute x4, waiting for transfers between devices: 2.27 us -> 3.51 us  [ring_forward(): return lax.ppermute(block, ('ctx', 'section'), pairs)]
    ppermute x6 -> x7, starting transfers between devices: 8.74 us -> 7.94 us  [swapped(): lax.ppermute(rows, name, [(i, i ^ bits) for i in range(lax.axis_size(name...]
    pallas_call x3, Pallas kernels: 2.59 us -> 2.04 us  [fold_blocks(): pl.pallas_call(functools.partial(fold_kernel, first, shifts, groups), in_...]
  transfers between devices with their start and end apart: 14 -> 15, of which waited for: 7 -> 7; matrix products, arithmetic and copies ran while one was open for 0% -> 0% of each run, Pallas kernels for 13% -> 16%
where the time goes in v4:
time: 32.6 us; the launch traced here: 32.5 us
  starting transfers between devices  16.8 us (52%)
  waiting for transfers between devices  8.72 us (27%)
  Pallas kernels  5.37 us (16%)
  local copies, waits for them, and re-layouts  1.24 us (4%)
    ppermute x7, starting transfers between devices, swapped(): lax.ppermute(rows, name, [(i, i ^ bits) for i in range(lax.axis_size(name...  7.94 us
    ppermute x4, starting transfers between devices, ring_forward(): return lax.ppermute(block, ('ctx', 'section'), pairs)  5.96 us
    ppermute x7, waiting for transfers between devices, swapped(): lax.ppermute(rows, name, [(i, i ^ bits) for i in range(lax.axis_size(name...  3.59 us
    ppermute x4, waiting for transfers between devices, ring_forward(): return lax.ppermute(block, ('ctx', 'section'), pairs)  3.51 us
    ppermute x4, starting transfers between devices, ring_backward(): return lax.ppermute(block, ('ctx', 'section'), pairs)  2.94 us
    pallas_call x3, Pallas kernels, fold_blocks(): pl.pallas_call(functools.partial(fold_kernel, first, shifts, groups), in_...  2.04 us
    ppermute x4, waiting for transfers between devices, ring_backward(): return lax.ppermute(block, ('ctx', 'section'), pairs)  1.62 us
    pallas_call x1, Pallas kernels, load_inputs(): pl.pallas_call(load_kernel, in_specs=[ANY_SPEC] * 4, out_specs=[VMEM_SPEC...  1.26 us
  transfers between devices with their start and end apart: 15, of which 7 were waited for; matrix products, arithmetic and copies ran while one was open for 0% of the time, Pallas kernels for 16%

profile of v4, /device:TPU:0, one launch (start us, length us, event | category | flops | bytes accessed | tf_op | source)
XLA Modules:
  0.0 32.5 jit_solution(11093381164723719168)
XLA Ops:
  0.0 0.0 copy-start
  0.0 1.2 %copy-done = bf16[2,128,2048]{2,1,0:T(8,128)(2,1)S(1)} copy-done((bf16[2,128,2048]{2,1,0:T(8,128)(2,1)S(1)}, bf16[2,128,2048]{2,1,0:T(8,128)(2,1)}, u32[]{:S(2)}) %copy-start) | copy-done | bytes 1048600
  1.2 3.1 %collective-permute-start.2 = (bf16[2,128,512]{2,1,0:T(8,128)(2,1)S(1)}, bf16[2,128,512]{2,1,0:T(8,128)(2,1)S(1)}, u32[]{:S(2)}, u32[]{:S(2)}) collective-permute-start(bf16[2,128,512]{2,1,0:T(8,128)(2,1)S(1)} %constant_dynamic-slice_fusion.refs_0_), channel_id=1, source_target_pairs={{0,1},{1,2},{2,3},{3,19},{19,18},{18,17},{17,16},{16,0},{4,5},{5,6... | collective-permute-start | bytes 786440 | tf_op jit(solution)/shard_map/ppermute | solution.py:583
  4.3 0.0 collective-permute-start
  4.3 3.0 %collective-permute-start.3 = (bf16[1,2048]{1,0:T(2,128)(2,1)}, bf16[1,2048]{1,0:T(2,128)(2,1)S(1)}, u32[]{:S(2)}, u32[]{:S(2)}) collective-permute-start(bf16[1,2048]{1,0:T(2,128)(2,1)} %image_ref.1), channel_id=1, source_target_pairs={{0,2},{1,3},{2,0},{3,1},{4,6},{5,7},{6,4},{7,5},{8,10},{9,11},{10,... | collective-permute-start | bytes 12296 | tf_op jit(solution)/shard_map/ppermute | solution.py:596
  7.4 1.3 %collective-permute-start.5 = (bf16[1,2048]{1,0:T(2,128)(2,1)}, bf16[1,2048]{1,0:T(2,128)(2,1)S(1)}, u32[]{:S(2)}, u32[]{:S(2)}) collective-permute-start(bf16[1,2048]{1,0:T(2,128)(2,1)} %image_ref.1), channel_id=1, source_target_pairs={{0,18},{1,19},{2,16},{3,17},{16,2},{17,3},{18,0},{19,1},{4,22},{5,... | collective-permute-start | bytes 12296 | tf_op jit(solution)/shard_map/ppermute | solution.py:596
  8.7 0.2 collective-permute-start.4
  8.9 1.3 %load_inputs.1 = (s32[2,128]{1,0:T(2,128)S(1)}, f32[16,128]{1,0:T(8,128)S(1)}, bf16[2,128,2048]{2,1,0:T(8,128)(2,1)S(1)}, bf16[1,2048]{1,0:T(2,128)(2,1)S(1)}) custom-call(s32[2]{0:T(128)} %lengths.1, f32[16]{0:T(128)} %gate.1, bf16[2,128,2048]{2,1,0:T(8,128)(2,1)} %q_ref.1, bf16[1,2048]{1,0:T(2,128)(2,1)} %image_ref.1), custom_call_target="tpu_custom_call" | custom-call | tf_op jit(solution)/shard_map/load_inputs/pallas_call | solution.py:527
  10.2 0.5 %collective-permute-done.2.refs_1_ = bf16[2,128,512]{2,1,0:T(8,128)(2,1)S(1)} collective-permute-done((bf16[2,128,512]{2,1,0:T(8,128)(2,1)S(1)}, bf16[2,128,512]{2,1,0:T(8,128)(2,1)S(1)}, u32[]{:S(2)}, u32[]{:S(2)}) %collective-permute-start.2) | collective-permute-done | bytes 262176 | tf_op jit(solution)/shard_map/ppermute | solution.py:583
  10.7 1.9 %collective-permute-start.8 = (bf16[2,128,512]{2,1,0:T(8,128)(2,1)S(1)}, bf16[2,128,512]{2,1,0:T(8,128)(2,1)S(1)}, u32[]{:S(2)}, u32[]{:S(2)}) collective-permute-start(bf16[2,128,512]{2,1,0:T(8,128)(2,1)S(1)} %collective-permute-done.2.refs_1_), channel_id=1, source_target_pairs={{0,1},{1,2},{2,3},{3,19},{19,18},{18,17},{17,16},{16,0},{4,5},{5,6... | collective-permute-start | bytes 786440 | tf_op jit(solution)/shard_map/ppermute | solution.py:583
  12.5 0.0 collective-permute-done.refs_2_
  12.5 0.1 collective-permute-start.1
  12.7 0.9 %collective-permute-done.3 = bf16[1,2048]{1,0:T(2,128)(2,1)S(1)} collective-permute-done((bf16[1,2048]{1,0:T(2,128)(2,1)}, bf16[1,2048]{1,0:T(2,128)(2,1)S(1)}, u32[]{:S(2)}, u32[]{:S(2)}) %collective-permute-start.3) | collective-permute-done | bytes 4128 | tf_op jit(solution)/shard_map/ppermute | solution.py:596
  13.5 0.0 collective-permute-done.5
  13.5 0.0 collective-permute-done.4
  13.6 1.5 %collective-permute-start.6 = (bf16[4,2048]{1,0:T(4,128)(2,1)S(1)}, bf16[4,2048]{1,0:T(4,128)(2,1)S(1)}, u32[]{:S(2)}, u32[]{:S(2)}) collective-permute-start(bf16[4,2048]{1,0:T(4,128)(2,1)S(1)} %pad_maximum_fusion.first_ref), channel_id=1, source_target_pairs={{0,1},{1,0},{2,3},{3,2},{4,5},{5,4},{6,7},{7,6},{8,9},{9,8},{10,11... | collective-permute-start | bytes 49160 | tf_op jit(solution)/shard_map/ppermute | solution.py:596
  15.1 1.8 %fold_blocks.3 = (f32[2,2,2,1024]{3,2,1,0:T(2,128)S(1)}, f32[2,2,128,1024]{3,2,1,0:T(8,128)S(1)}) custom-call(s32[2,128]{1,0:T(2,128)S(1)} %get-tuple-element.21.length_ref, bf16[2,128,2048]{2,1,0:T(8,128)(2,1)S(1)} %get-tuple-element.22.q_ref, bf16[2,128,512]{2,1,0:T(8,128)(2,1)S(1)} %constant_dynamic-slice_fusion.refs_0_, ...), custom_call_target="tpu_custom_call" | custom-call | flops 805306368 | bytes 1048576 | tf_op jit(solution)/shard_map/fold_blocks/pallas_call | solution.py:314
  16.9 2.7 %collective-permute-done.6.second_ref = bf16[4,2048]{1,0:T(4,128)(2,1)S(1)} collective-permute-done((bf16[4,2048]{1,0:T(4,128)(2,1)S(1)}, bf16[4,2048]{1,0:T(4,128)(2,1)S(1)}, u32[]{:S(2)}, u32[]{:S(2)}) %collective-permute-start.6) | collective-permute-done | bytes 16416 | tf_op jit(solution)/shard_map/ppermute | solution.py:596
  19.6 0.0 collective-permute-done.8.refs_0_
  19.6 0.3 collective-permute-start.13
  19.9 0.0 collective-permute-done.1.refs_1_
  19.9 1.8 %collective-permute-start.7 = (bf16[2,128,512]{2,1,0:T(8,128)(2,1)S(1)}, bf16[2,128,512]{2,1,0:T(8,128)(2,1)S(1)}, u32[]{:S(2)}, u32[]{:S(2)}) collective-permute-start(bf16[2,128,512]{2,1,0:T(8,128)(2,1)S(1)} %collective-permute-done.1.refs_1_), channel_id=1, source_target_pairs={{1,0},{2,1},{3,2},{19,3},{18,19},{17,18},{16,17},{0,16},{5,4},{6,5... | collective-permute-start | bytes 786440 | tf_op jit(solution)/shard_map/ppermute | solution.py:588
  21.7 0.1 collective-permute-start.11
  21.7 1.6 %collective-permute-start.10 = (bf16[8,2048]{1,0:T(8,128)(2,1)S(1)}, bf16[8,2048]{1,0:T(8,128)(2,1)S(1)}, u32[]{:S(2)}, u32[]{:S(2)}) collective-permute-start(bf16[8,2048]{1,0:T(8,128)(2,1)S(1)} %joined.1.refs_0_), channel_id=1, source_target_pairs={{0,8},{4,12},{8,0},{12,4},{1,9},{5,13},{9,1},{13,5},{2,10},{6,14},... | collective-permute-start | bytes 98312 | tf_op jit(solution)/shard_map/ppermute | solution.py:596
  23.3 0.3 collective-permute-start.9
  23.6 2.4 %collective-permute-done.13.refs_0_.block_ref = bf16[2,128,512]{2,1,0:T(8,128)(2,1)S(1)} collective-permute-done((bf16[2,128,512]{2,1,0:T(8,128)(2,1)S(1)}, bf16[2,128,512]{2,1,0:T(8,128)(2,1)S(1)}, u32[]{:S(2)}, u32[]{:S(2)}) %collective-permute-start.13) | collective-permute-done | bytes 262176 | tf_op jit(solution)/shard_map/ppermute | solution.py:583
  26.0 0.7 %collective-permute-start.14 = (bf16[1,128,512]{2,1,0:T(8,128)(2,1)S(1)}, bf16[1,128,512]{2,1,0:T(8,128)(2,1)S(1)}, u32[]{:S(2)}, u32[]{:S(2)}) collective-permute-start(bf16[1,128,512]{2,1,0:T(8,128)(2,1)S(1)} %half_of.3), channel_id=1, source_target_pairs={{0,1},{1,2},{2,3},{3,19},{19,18},{18,17},{17,16},{16,0},{4,5},{5,6... | collective-permute-start | bytes 393224 | tf_op jit(solution)/shard_map/ppermute | solution.py:583
  26.7 0.0 collective-permute-done.11.refs_3_
  26.7 0.0 collective-permute-done.10.refs_2_
  26.7 0.0 collective-permute-done.9.refs_1_
  26.7 0.4 %collective-permute-done.7.block_ref.refs_1_ = bf16[2,128,512]{2,1,0:T(8,128)(2,1)S(1)} collective-permute-done((bf16[2,128,512]{2,1,0:T(8,128)(2,1)S(1)}, bf16[2,128,512]{2,1,0:T(8,128)(2,1)S(1)}, u32[]{:S(2)}, u32[]{:S(2)}) %collective-permute-start.7) | collective-permute-done | bytes 262176 | tf_op jit(solution)/shard_map/ppermute | solution.py:588
  27.1 1.0 %collective-permute-start.12 = (bf16[1,128,512]{2,1,0:T(8,128)(2,1)S(1)}, bf16[1,128,512]{2,1,0:T(8,128)(2,1)S(1)}, u32[]{:S(2)}, u32[]{:S(2)}) collective-permute-start(bf16[1,128,512]{2,1,0:T(8,128)(2,1)S(1)} %half_of.2), channel_id=1, source_target_pairs={{1,0},{2,1},{3,2},{19,3},{18,19},{17,18},{16,17},{0,16},{5,4},{6,5... | collective-permute-start | bytes 393224 | tf_op jit(solution)/shard_map/ppermute | solution.py:588
  28.2 0.8 %cross_attend.1.cross_ref = f32[2,2,128,1024]{3,2,1,0:T(8,128)S(1)} custom-call(f32[16,128]{1,0:T(8,128)S(1)} %get-tuple-element.31.factor_ref, bf16[2,128,2048]{2,1,0:T(8,128)(2,1)S(1)} %get-tuple-element.22.q_ref, bf16[8,2048]{1,0:T(8,128)(2,1)S(1)} %joined.1.refs_0_, bf16[8,2048]{1,0:T(8,128)(2,1)S(1)} %collective-permute-done.9.refs_1_, ...), custom_call_target="tpu_custom_call" | custom-call | flops 268435456 | bytes 1048576 | tf_op jit(solution)/shard_map/cross_attend/pallas_call | solution.py:350
  29.0 0.2 fold_blocks.5
  29.2 1.2 %early_rows.1._ = bf16[2,128,2048]{2,1,0:T(8,128)(2,1)} custom-call(bf16[2,128,2048]{2,1,0:T(8,128)(2,1)S(1)} %get-tuple-element.22.q_ref, f32[2,2,128,1024]{3,2,1,0:T(8,128)S(1)} %cross_attend.1.cross_ref, f32[2,2,2,1024]{3,2,1,0:T(2,128)S(1)} %get-tuple-element.34.stat_ref, f32[2,2,128,1024]{3,2,1,0:T(8,128)S(1)} %get-tuple-element.35.sum_ref), custom_call_target="tpu_custom_call" | custom-call | flops 67108864 | bytes 1048576 | tf_op jit(solution)/shard_map/early_rows/pallas_call | solution.py:413
  30.4 0.6 %collective-permute-done.14.block = bf16[1,128,512]{2,1,0:T(8,128)(2,1)S(1)} collective-permute-done((bf16[1,128,512]{2,1,0:T(8,128)(2,1)S(1)}, bf16[1,128,512]{2,1,0:T(8,128)(2,1)S(1)}, u32[]{:S(2)}, u32[]{:S(2)}) %collective-permute-start.14) | collective-permute-done | bytes 131104 | tf_op jit(solution)/shard_map/ppermute | solution.py:583
  31.0 1.2 %collective-permute-done.12.block = bf16[1,128,512]{2,1,0:T(8,128)(2,1)S(1)} collective-permute-done((bf16[1,128,512]{2,1,0:T(8,128)(2,1)S(1)}, bf16[1,128,512]{2,1,0:T(8,128)(2,1)S(1)}, u32[]{:S(2)}, u32[]{:S(2)}) %collective-permute-start.12) | collective-permute-done | bytes 131104 | tf_op jit(solution)/shard_map/ppermute | solution.py:588
  (8 shorter events, 0.1 us)
Async XLA Ops:
  0.0 1.2 %copy-start = (bf16[2,128,2048]{2,1,0:T(8,128)(2,1)S(1)}, bf16[2,128,2048]{2,1,0:T(8,128)(2,1)}, u32[]{:S(2)}) copy-start(bf16[2,128,2048]{2,1,0:T(8,128)(2,1)} %param.6) | copy-start | bytes 3145732
  1.2 9.4 %collective-permute-start.2 = (bf16[2,128,512]{2,1,0:T(8,128)(2,1)S(1)}, bf16[2,128,512]{2,1,0:T(8,128)(2,1)S(1)}, u32[]{:S(2)}, u32[]{:S(2)}) collective-permute-start(bf16[2,128,512]{2,1,0:T(8,128)(2,1)S(1)} %constant_dynamic-slice_fusion.refs_0_), channel_id=1, source_target_pairs={{0,1},{1,2},{2,3},{3,19},{19,18},{18,17},{17,16},{16,0},{4,5},{5,6... | collective-permute-start | bytes 786440 | tf_op jit(solution)/shard_map/ppermute | solution.py:583
  4.3 8.2 %collective-permute-start = (bf16[2,128,512]{2,1,0:T(8,128)(2,1)S(1)}, bf16[2,128,512]{2,1,0:T(8,128)(2,1)S(1)}, u32[]{:S(2)}, u32[]{:S(2)}) collective-permute-start(bf16[2,128,512]{2,1,0:T(8,128)(2,1)S(1)} %constant_dynamic-slice_fusion.refs_0_), channel_id=1, source_target_pairs={{1,0},{2,1},{3,2},{19,3},{18,19},{17,18},{16,17},{0,16},{5,4},{6,5... | collective-permute-start | bytes 786440 | tf_op jit(solution)/shard_map/ppermute | solution.py:588
  4.3 9.2 %collective-permute-start.3 = (bf16[1,2048]{1,0:T(2,128)(2,1)}, bf16[1,2048]{1,0:T(2,128)(2,1)S(1)}, u32[]{:S(2)}, u32[]{:S(2)}) collective-permute-start(bf16[1,2048]{1,0:T(2,128)(2,1)} %image_ref.1), channel_id=1, source_target_pairs={{0,2},{1,3},{2,0},{3,1},{4,6},{5,7},{6,4},{7,5},{8,10},{9,11},{10,... | collective-permute-start | bytes 12296 | tf_op jit(solution)/shard_map/ppermute | solution.py:596
  7.4 6.2 %collective-permute-start.5 = (bf16[1,2048]{1,0:T(2,128)(2,1)}, bf16[1,2048]{1,0:T(2,128)(2,1)S(1)}, u32[]{:S(2)}, u32[]{:S(2)}) collective-permute-start(bf16[1,2048]{1,0:T(2,128)(2,1)} %image_ref.1), channel_id=1, source_target_pairs={{0,18},{1,19},{2,16},{3,17},{16,2},{17,3},{18,0},{19,1},{4,22},{5,... | collective-permute-start | bytes 12296 | tf_op jit(solution)/shard_map/ppermute | solution.py:596
  8.7 4.9 %collective-permute-start.4 = (bf16[1,2048]{1,0:T(2,128)(2,1)}, bf16[1,2048]{1,0:T(2,128)(2,1)S(1)}, u32[]{:S(2)}, u32[]{:S(2)}) collective-permute-start(bf16[1,2048]{1,0:T(2,128)(2,1)} %image_ref.1), channel_id=1, source_target_pairs={{0,16},{16,0},{1,17},{17,1},{2,18},{18,2},{3,19},{19,3},{4,20},{20... | collective-permute-start | bytes 12296 | tf_op jit(solution)/shard_map/ppermute | solution.py:596
  10.7 9.0 %collective-permute-start.8 = (bf16[2,128,512]{2,1,0:T(8,128)(2,1)S(1)}, bf16[2,128,512]{2,1,0:T(8,128)(2,1)S(1)}, u32[]{:S(2)}, u32[]{:S(2)}) collective-permute-start(bf16[2,128,512]{2,1,0:T(8,128)(2,1)S(1)} %collective-permute-done.2.refs_1_), channel_id=1, source_target_pairs={{0,1},{1,2},{2,3},{3,19},{19,18},{18,17},{17,16},{16,0},{4,5},{5,6... | collective-permute-start | bytes 786440 | tf_op jit(solution)/shard_map/ppermute | solution.py:583
  12.5 7.4 %collective-permute-start.1 = (bf16[2,128,512]{2,1,0:T(8,128)(2,1)S(1)}, bf16[2,128,512]{2,1,0:T(8,128)(2,1)S(1)}, u32[]{:S(2)}, u32[]{:S(2)}) collective-permute-start(bf16[2,128,512]{2,1,0:T(8,128)(2,1)S(1)} %collective-permute-done.refs_2_), channel_id=1, source_target_pairs={{1,0},{2,1},{3,2},{19,3},{18,19},{17,18},{16,17},{0,16},{5,4},{6,5... | collective-permute-start | bytes 786440 | tf_op jit(solution)/shard_map/ppermute | solution.py:588
  13.6 6.0 %collective-permute-start.6 = (bf16[4,2048]{1,0:T(4,128)(2,1)S(1)}, bf16[4,2048]{1,0:T(4,128)(2,1)S(1)}, u32[]{:S(2)}, u32[]{:S(2)}) collective-permute-start(bf16[4,2048]{1,0:T(4,128)(2,1)S(1)} %pad_maximum_fusion.first_ref), channel_id=1, source_target_pairs={{0,1},{1,0},{2,3},{3,2},{4,5},{5,4},{6,7},{7,6},{8,9},{9,8},{10,11... | collective-permute-start | bytes 49160 | tf_op jit(solution)/shard_map/ppermute | solution.py:596
  19.6 6.4 %collective-permute-start.13 = (bf16[2,128,512]{2,1,0:T(8,128)(2,1)S(1)}, bf16[2,128,512]{2,1,0:T(8,128)(2,1)S(1)}, u32[]{:S(2)}, u32[]{:S(2)}) collective-permute-start(bf16[2,128,512]{2,1,0:T(8,128)(2,1)S(1)} %collective-permute-done.8.refs_0_), channel_id=1, source_target_pairs={{0,1},{1,2},{2,3},{3,19},{19,18},{18,17},{17,16},{16,0},{4,5},{5,6... | collective-permute-start | bytes 786440 | tf_op jit(solution)/shard_map/ppermute | solution.py:583
  19.9 7.2 %collective-permute-start.7 = (bf16[2,128,512]{2,1,0:T(8,128)(2,1)S(1)}, bf16[2,128,512]{2,1,0:T(8,128)(2,1)S(1)}, u32[]{:S(2)}, u32[]{:S(2)}) collective-permute-start(bf16[2,128,512]{2,1,0:T(8,128)(2,1)S(1)} %collective-permute-done.1.refs_1_), channel_id=1, source_target_pairs={{1,0},{2,1},{3,2},{19,3},{18,19},{17,18},{16,17},{0,16},{5,4},{6,5... | collective-permute-start | bytes 786440 | tf_op jit(solution)/shard_map/ppermute | solution.py:588
  21.7 5.1 %collective-permute-start.11 = (bf16[8,2048]{1,0:T(8,128)(2,1)S(1)}, bf16[8,2048]{1,0:T(8,128)(2,1)S(1)}, u32[]{:S(2)}, u32[]{:S(2)}) collective-permute-start(bf16[8,2048]{1,0:T(8,128)(2,1)S(1)} %joined.1.refs_0_), channel_id=1, source_target_pairs={{0,12},{4,8},{8,4},{12,0},{1,13},{5,9},{9,5},{13,1},{2,14},{6,10},... | collective-permute-start | bytes 98312 | tf_op jit(solution)/shard_map/ppermute | solution.py:596
  21.7 5.0 %collective-permute-start.10 = (bf16[8,2048]{1,0:T(8,128)(2,1)S(1)}, bf16[8,2048]{1,0:T(8,128)(2,1)S(1)}, u32[]{:S(2)}, u32[]{:S(2)}) collective-permute-start(bf16[8,2048]{1,0:T(8,128)(2,1)S(1)} %joined.1.refs_0_), channel_id=1, source_target_pairs={{0,8},{4,12},{8,0},{12,4},{1,9},{5,13},{9,1},{13,5},{2,10},{6,14},... | collective-permute-start | bytes 98312 | tf_op jit(solution)/shard_map/ppermute | solution.py:596
  23.3 3.4 %collective-permute-start.9 = (bf16[8,2048]{1,0:T(8,128)(2,1)S(1)}, bf16[8,2048]{1,0:T(8,128)(2,1)S(1)}, u32[]{:S(2)}, u32[]{:S(2)}) collective-permute-start(bf16[8,2048]{1,0:T(8,128)(2,1)S(1)} %joined.1.refs_0_), channel_id=1, source_target_pairs={{0,4},{4,0},{8,12},{12,8},{1,5},{5,1},{9,13},{13,9},{2,6},{6,2},{1... | collective-permute-start | bytes 98312 | tf_op jit(solution)/shard_map/ppermute | solution.py:596
  26.0 5.0 %collective-permute-start.14 = (bf16[1,128,512]{2,1,0:T(8,128)(2,1)S(1)}, bf16[1,128,512]{2,1,0:T(8,128)(2,1)S(1)}, u32[]{:S(2)}, u32[]{:S(2)}) collective-permute-start(bf16[1,128,512]{2,1,0:T(8,128)(2,1)S(1)} %half_of.3), channel_id=1, source_target_pairs={{0,1},{1,2},{2,3},{3,19},{19,18},{18,17},{17,16},{16,0},{4,5},{5,6... | collective-permute-start | bytes 393224 | tf_op jit(solution)/shard_map/ppermute | solution.py:583
  27.1 5.1 %collective-permute-start.12 = (bf16[1,128,512]{2,1,0:T(8,128)(2,1)S(1)}, bf16[1,128,512]{2,1,0:T(8,128)(2,1)S(1)}, u32[]{:S(2)}, u32[]{:S(2)}) collective-permute-start(bf16[1,128,512]{2,1,0:T(8,128)(2,1)S(1)} %half_of.2), channel_id=1, source_target_pairs={{1,0},{2,1},{3,2},{19,3},{18,19},{17,18},{16,17},{0,16},{5,4},{6,5... | collective-permute-start | bytes 393224 | tf_op jit(solution)/shard_map/ppermute | solution.py:588

commit v5 on v4

--- a/solution.py
+++ b/solution.py
@@ -133,7 +133,7 @@
 VMEM_SPEC = pl.BlockSpec(memory_space=pltpu.VMEM)
 ANY_SPEC = pl.BlockSpec(memory_space=pl.ANY)
 BLOCKS = 8
-CHUNK = 4
+CHUNK = 8
 KERNEL = pltpu.CompilerParams(vmem_limit_bytes=12 << 20)
 
 
@@ -505,28 +505,33 @@
     )(*args, result)
 
 
-def load_kernel(lengths, gate, q_ref, image_ref, limit_ref, factor_ref, q_out, image_out, counts, gates, sems):
-    pairs = ((lengths, counts), (gate, gates), (q_ref, q_out), (image_ref, image_out))
-    copies = [pltpu.make_async_copy(source, target, sems.at[i]) for i, (source, target) in enumerate(pairs)]
-    for copy in copies:
-        copy.start()
-    copies[0].wait()
-    for i in range(limit_ref.shape[0]):
-        limit_ref[i : i + 1] = jnp.full((1, limit_ref.shape[1]), counts[i], jnp.int32)
-    copies[1].wait()
-    for i in range(factor_ref.shape[0]):
-        factor_ref[i : i + 1] = jnp.full((1, factor_ref.shape[1]), gates[i], jnp.float32)
-    factor_ref[...] = jnp.tanh(factor_ref[...])
-    copies[2].wait()
-    copies[3].wait()
-
-
-def load_inputs(*arrays):
+def load_kernel(parity, lengths, gate, q_ref, image_ref, *refs):
+    limit_ref, factor_ref, q_out, image_out, counts, gates, sems = refs[-7:]
+
+    def work():
+        pairs = ((lengths, counts), (gate, gates), (q_ref, q_out), (image_ref, image_out))
+        copies = [pltpu.make_async_copy(source, target, sems.at[i]) for i, (source, target) in enumerate(pairs)]
+        for copy in copies:
+            copy.start()
+        copies[0].wait()
+        for i in range(limit_ref.shape[0]):
+            limit_ref[i : i + 1] = jnp.full((1, limit_ref.shape[1]), counts[i], jnp.int32)
+        copies[1].wait()
+        for i in range(factor_ref.shape[0]):
+            factor_ref[i : i + 1] = jnp.full((1, factor_ref.shape[1]), gates[i], jnp.float32)
+        factor_ref[...] = jnp.tanh(factor_ref[...])
+        copies[2].wait()
+        copies[3].wait()
+
+    pl.when((lax.axis_index("tp") & 1) == parity)(work)
+
+
+def load_inputs(parity, loaded, *arrays):
     lengths, gate, q, image = arrays
     rows = q.shape[1]
     return pl.pallas_call(
-        load_kernel,
-        in_specs=[ANY_SPEC] * 4,
+        functools.partial(load_kernel, parity),
+        in_specs=[ANY_SPEC] * 4 + [VMEM_SPEC] * len(loaded),
         out_specs=[VMEM_SPEC] * 4,
         out_shape=[
             pltpu.VMEM((lengths.shape[0], rows), jnp.int32),
@@ -539,9 +544,10 @@
             pltpu.SMEM(gate.shape, gate.dtype),
             pltpu.SemaphoreType.DMA((4,)),
         ],
+        input_output_aliases={4 + i: i for i in range(len(loaded))},
         compiler_params=KERNEL,
         name="load_inputs",
-    )(*[pltpu.with_memory_space_constraint(array, pltpu.HBM) for array in arrays])
+    )(*[pltpu.with_memory_space_constraint(array, pltpu.HBM) for array in arrays], *in_vmem(*loaded))
 
 
 def join_kernel(first_ref, second_ref, joined_ref):
@@ -601,19 +607,21 @@
     groups = KVH // tp_count
     kv_cols = groups * 2 * HEAD_SIZE
     own = lax.dynamic_slice_in_dim(self_kv, lax.axis_index("tp") * kv_cols, kv_cols, 2)
+    loaded = load_inputs(0, (), lengths, cross_gate, queries, image_kv)
+    own = after(own, loaded[0])
     f1, b1 = ring_forward(own), ring_backward(own)
     sections = lax.axis_size("section")
     n1 = swapped(image_kv, "section", 2)
     n2 = swapped(image_kv, "ctx", 1)
     n3 = swapped(image_kv, ("ctx", "section"), sections + 2)
-    limits, factors, q, image1 = load_inputs(lengths, cross_gate, queries, image_kv)
+    limits, factors, q, image1 = load_inputs(1, tuple(loaded), lengths, cross_gate, queries, image_kv)
 
     f2, b2 = ring_forward(f1), ring_backward(b1)
     image4 = jnp.concatenate([image1, n1, n2, n3], 0)
     far = swapped(image4, "section", 1)
     state = fold_blocks(limits, q, [own, f1, after(b1, image4)], (0, -1, 1), None)
 
-    f3, b3 = ring_forward(after(f2, state[0], far)), ring_backward(after(b2, state[0], far))
+    f3, b3 = ring_forward(after(f2, state[0])), ring_backward(after(b2, state[0], far))
     image8 = joined(image4, far)
     images = [image8] + [swapped(image8, "tp", bits) for bits in range(1, tp_count)]
     state = fold_blocks(limits, q, [f2, after(b2, image8)], (-2, 2), state)

time: 32.6 us -> 31.3 us (0.960)
  waiting for transfers between devices: 8.72 us -> 6.94 us
  starting transfers between devices: 16.8 us -> 17.3 us
    ppermute x4, starting transfers between devices: 5.96 us -> 7.94 us  [ring_forward(): return lax.ppermute(block, ('ctx', 'section'), pairs)]
    ppermute x7, waiting for transfers between devices: 3.59 us -> 1.77 us  [swapped(): lax.ppermute(rows, name, [(i, i ^ bits) for i in range(lax.axis_size(name...]
    ppermute x4, starting transfers between devices: 2.94 us -> 1.29 us  [ring_backward(): return lax.ppermute(block, ('ctx', 'section'), pairs)]
    pallas_call x1 -> x2, Pallas kernels: 1.26 us -> 1.31 us  [load_inputs(): pl.pallas_call(functools.partial(load_kernel, parity), in_specs=[ANY_SPEC...]
  transfers between devices with their start and end apart: 15 -> 15, of which waited for: 7 -> 7; matrix products, arithmetic and copies ran while one was open for 0% -> 0% of each run, Pallas kernels for 16% -> 13%
where the time goes in v5:
time: 31.3 us; the launch traced here: 31.1 us
  starting transfers between devices  17.3 us (55%)
  waiting for transfers between devices  6.94 us (22%)
  Pallas kernels  5.29 us (17%)
  local copies, waits for them, and re-layouts  1.24 us (4%)
    ppermute x7, starting transfers between devices, swapped(): lax.ppermute(rows, name, [(i, i ^ bits) for i in range(lax.axis_size(name...  8.11 us
    ppermute x4, starting transfers between devices, ring_forward(): return lax.ppermute(block, ('ctx', 'section'), pairs)  7.94 us
    ppermute x4, waiting for transfers between devices, ring_forward(): return lax.ppermute(block, ('ctx', 'section'), pairs)  3.6 us
    pallas_call x3, Pallas kernels, fold_blocks(): pl.pallas_call(functools.partial(fold_kernel, first, shifts, groups), in_...  1.99 us
    ppermute x7, waiting for transfers between devices, swapped(): lax.ppermute(rows, name, [(i, i ^ bits) for i in range(lax.axis_size(name...  1.77 us
    ppermute x4, waiting for transfers between devices, ring_backward(): return lax.ppermute(block, ('ctx', 'section'), pairs)  1.57 us
    pallas_call x2, Pallas kernels, load_inputs(): pl.pallas_call(functools.partial(load_kernel, parity), in_specs=[ANY_SPEC...  1.31 us
    ppermute x4, starting transfers between devices, ring_backward(): return lax.ppermute(block, ('ctx', 'section'), pairs)  1.29 us
  transfers between devices with their start and end apart: 15, of which 7 were waited for; matrix products, arithmetic and copies ran while one was open for 0% of the time, Pallas kernels for 13%

profile of v5, /device:TPU:0, one launch (start us, length us, event | category | flops | bytes accessed | tf_op | source)
XLA Modules:
  0.0 31.1 jit_solution(8534454975437009178)
XLA Ops:
  0.0 0.0 copy-start
  0.0 1.2 %copy-done = bf16[2,128,2048]{2,1,0:T(8,128)(2,1)S(1)} copy-done((bf16[2,128,2048]{2,1,0:T(8,128)(2,1)S(1)}, bf16[2,128,2048]{2,1,0:T(8,128)(2,1)}, u32[]{:S(2)}) %copy-start) | copy-done | bytes 1048600
  1.2 1.3 %load_inputs.2 = (s32[2,128]{1,0:T(2,128)S(1)}, f32[16,128]{1,0:T(8,128)S(1)}, bf16[2,128,2048]{2,1,0:T(8,128)(2,1)S(1)}, bf16[1,2048]{1,0:T(2,128)(2,1)S(1)}) custom-call(s32[2]{0:T(128)} %lengths.3, f32[16]{0:T(128)} %gate.3, bf16[2,128,2048]{2,1,0:T(8,128)(2,1)} %q_ref.3, bf16[1,2048]{1,0:T(2,128)(2,1)} %image_ref.3), custom_call_target="tpu_custom_call" | custom-call | tf_op jit(solution)/shard_map/load_inputs/pallas_call | solution.py:532
  2.5 3.1 %collective-permute-start.2 = (bf16[2,128,512]{2,1,0:T(8,128)(2,1)S(1)}, bf16[2,128,512]{2,1,0:T(8,128)(2,1)S(1)}, u32[]{:S(2)}, u32[]{:S(2)}) collective-permute-start(bf16[2,128,512]{2,1,0:T(8,128)(2,1)S(1)} %constant_dynamic-slice_fusion.refs_0_), channel_id=1, source_target_pairs={{0,1},{1,2},{2,3},{3,19},{19,18},{18,17},{17,16},{16,0},{4,5},{5,6... | collective-permute-start | bytes 786440 | tf_op jit(solution)/shard_map/ppermute | solution.py:589
  5.6 0.0 collective-permute-start
  5.6 3.0 %collective-permute-start.3 = (bf16[1,2048]{1,0:T(2,128)(2,1)}, bf16[1,2048]{1,0:T(2,128)(2,1)S(1)}, u32[]{:S(2)}, u32[]{:S(2)}) collective-permute-start(bf16[1,2048]{1,0:T(2,128)(2,1)} %image_ref.3), channel_id=1, source_target_pairs={{0,2},{1,3},{2,0},{3,1},{4,6},{5,7},{6,4},{7,5},{8,10},{9,11},{10,... | collective-permute-start | bytes 12296 | tf_op jit(solution)/shard_map/ppermute | solution.py:602
  8.6 1.3 %collective-permute-start.5 = (bf16[1,2048]{1,0:T(2,128)(2,1)}, bf16[1,2048]{1,0:T(2,128)(2,1)S(1)}, u32[]{:S(2)}, u32[]{:S(2)}) collective-permute-start(bf16[1,2048]{1,0:T(2,128)(2,1)} %image_ref.3), channel_id=1, source_target_pairs={{0,18},{1,19},{2,16},{3,17},{16,2},{17,3},{18,0},{19,1},{4,22},{5,... | collective-permute-start | bytes 12296 | tf_op jit(solution)/shard_map/ppermute | solution.py:602
  9.9 0.2 collective-permute-start.4
  10.2 0.5 %collective-permute-done.2.refs_1_ = bf16[2,128,512]{2,1,0:T(8,128)(2,1)S(1)} collective-permute-done((bf16[2,128,512]{2,1,0:T(8,128)(2,1)S(1)}, bf16[2,128,512]{2,1,0:T(8,128)(2,1)S(1)}, u32[]{:S(2)}, u32[]{:S(2)}) %collective-permute-start.2) | collective-permute-done | bytes 262176 | tf_op jit(solution)/shard_map/ppermute | solution.py:589
  10.7 1.9 %collective-permute-start.8 = (bf16[2,128,512]{2,1,0:T(8,128)(2,1)S(1)}, bf16[2,128,512]{2,1,0:T(8,128)(2,1)S(1)}, u32[]{:S(2)}, u32[]{:S(2)}) collective-permute-start(bf16[2,128,512]{2,1,0:T(8,128)(2,1)S(1)} %collective-permute-done.2.refs_1_), channel_id=1, source_target_pairs={{0,1},{1,2},{2,3},{3,19},{19,18},{18,17},{17,16},{16,0},{4,5},{5,6... | collective-permute-start | bytes 786440 | tf_op jit(solution)/shard_map/ppermute | solution.py:589
  12.6 0.0 collective-permute-done.refs_2_
  12.6 0.1 collective-permute-start.1
  12.8 1.0 %collective-permute-done.3 = bf16[1,2048]{1,0:T(2,128)(2,1)S(1)} collective-permute-done((bf16[1,2048]{1,0:T(2,128)(2,1)}, bf16[1,2048]{1,0:T(2,128)(2,1)S(1)}, u32[]{:S(2)}, u32[]{:S(2)}) %collective-permute-start.3) | collective-permute-done | bytes 4128 | tf_op jit(solution)/shard_map/ppermute | solution.py:602
  13.7 0.7 %collective-permute-done.5 = bf16[1,2048]{1,0:T(2,128)(2,1)S(1)} collective-permute-done((bf16[1,2048]{1,0:T(2,128)(2,1)}, bf16[1,2048]{1,0:T(2,128)(2,1)S(1)}, u32[]{:S(2)}, u32[]{:S(2)}) %collective-permute-start.5) | collective-permute-done | bytes 4128 | tf_op jit(solution)/shard_map/ppermute | solution.py:602
  14.4 0.0 collective-permute-done.4
  14.5 1.6 %collective-permute-start.6 = (bf16[4,2048]{1,0:T(4,128)(2,1)S(1)}, bf16[4,2048]{1,0:T(4,128)(2,1)S(1)}, u32[]{:S(2)}, u32[]{:S(2)}) collective-permute-start(bf16[4,2048]{1,0:T(4,128)(2,1)S(1)} %pad_maximum_fusion.first_ref), channel_id=1, source_target_pairs={{0,1},{1,0},{2,3},{3,2},{4,5},{5,4},{6,7},{7,6},{8,9},{9,8},{10,11... | collective-permute-start | bytes 49160 | tf_op jit(solution)/shard_map/ppermute | solution.py:602
  16.1 1.8 %fold_blocks.3 = (f32[2,2,2,1024]{3,2,1,0:T(2,128)S(1)}, f32[2,2,128,1024]{3,2,1,0:T(8,128)S(1)}) custom-call(s32[2,128]{1,0:T(2,128)S(1)} %get-tuple-element.30.length_ref, bf16[2,128,2048]{2,1,0:T(8,128)(2,1)S(1)} %get-tuple-element.31.q_ref, bf16[2,128,512]{2,1,0:T(8,128)(2,1)S(1)} %constant_dynamic-slice_fusion.refs_0_, ...), custom_call_target="tpu_custom_call" | custom-call | flops 805306368 | bytes 1048576 | tf_op jit(solution)/shard_map/fold_blocks/pallas_call | solution.py:314
  17.9 0.0 collective-permute-done.8.refs_0_
  17.9 1.5 %collective-permute-start.13 = (bf16[2,128,512]{2,1,0:T(8,128)(2,1)S(1)}, bf16[2,128,512]{2,1,0:T(8,128)(2,1)S(1)}, u32[]{:S(2)}, u32[]{:S(2)}) collective-permute-start(bf16[2,128,512]{2,1,0:T(8,128)(2,1)S(1)} %collective-permute-done.8.refs_0_), channel_id=1, source_target_pairs={{0,1},{1,2},{2,3},{3,19},{19,18},{18,17},{17,16},{16,0},{4,5},{5,6... | collective-permute-start | bytes 786440 | tf_op jit(solution)/shard_map/ppermute | solution.py:589
  19.4 0.1 collective-permute-done.6.second_ref
  19.5 0.0 collective-permute-done.1.refs_1_
  19.5 0.5 %collective-permute-start.7 = (bf16[2,128,512]{2,1,0:T(8,128)(2,1)S(1)}, bf16[2,128,512]{2,1,0:T(8,128)(2,1)S(1)}, u32[]{:S(2)}, u32[]{:S(2)}) collective-permute-start(bf16[2,128,512]{2,1,0:T(8,128)(2,1)S(1)} %collective-permute-done.1.refs_1_), channel_id=1, source_target_pairs={{1,0},{2,1},{3,2},{19,3},{18,19},{17,18},{16,17},{0,16},{5,4},{6,5... | collective-permute-start | bytes 786440 | tf_op jit(solution)/shard_map/ppermute | solution.py:594
  20.0 0.1 collective-permute-start.11
  20.1 1.6 %collective-permute-start.10 = (bf16[8,2048]{1,0:T(8,128)(2,1)S(1)}, bf16[8,2048]{1,0:T(8,128)(2,1)S(1)}, u32[]{:S(2)}, u32[]{:S(2)}) collective-permute-start(bf16[8,2048]{1,0:T(8,128)(2,1)S(1)} %joined.1.refs_0_), channel_id=1, source_target_pairs={{0,8},{4,12},{8,0},{12,4},{1,9},{5,13},{9,1},{13,5},{2,10},{6,14},... | collective-permute-start | bytes 98312 | tf_op jit(solution)/shard_map/ppermute | solution.py:602
  21.6 0.3 collective-permute-start.9
  21.9 2.4 %collective-permute-done.13.refs_0_.block_ref = bf16[2,128,512]{2,1,0:T(8,128)(2,1)S(1)} collective-permute-done((bf16[2,128,512]{2,1,0:T(8,128)(2,1)S(1)}, bf16[2,128,512]{2,1,0:T(8,128)(2,1)S(1)}, u32[]{:S(2)}, u32[]{:S(2)}) %collective-permute-start.13) | collective-permute-done | bytes 262176 | tf_op jit(solution)/shard_map/ppermute | solution.py:589
  24.3 1.5 %collective-permute-start.14 = (bf16[1,128,512]{2,1,0:T(8,128)(2,1)S(1)}, bf16[1,128,512]{2,1,0:T(8,128)(2,1)S(1)}, u32[]{:S(2)}, u32[]{:S(2)}) collective-permute-start(bf16[1,128,512]{2,1,0:T(8,128)(2,1)S(1)} %half_of.3), channel_id=1, source_target_pairs={{0,1},{1,2},{2,3},{3,19},{19,18},{18,17},{17,16},{16,0},{4,5},{5,6... | collective-permute-start | bytes 393224 | tf_op jit(solution)/shard_map/ppermute | solution.py:589
  25.8 0.0 collective-permute-done.11.refs_3_
  25.8 0.0 collective-permute-done.10.refs_2_
  25.8 0.0 collective-permute-done.9.refs_1_
  25.8 0.0 collective-permute-done.7.block_ref.refs_1_
  25.9 0.6 %collective-permute-start.12 = (bf16[1,128,512]{2,1,0:T(8,128)(2,1)S(1)}, bf16[1,128,512]{2,1,0:T(8,128)(2,1)S(1)}, u32[]{:S(2)}, u32[]{:S(2)}) collective-permute-start(bf16[1,128,512]{2,1,0:T(8,128)(2,1)S(1)} %half_of.2), channel_id=1, source_target_pairs={{1,0},{2,1},{3,2},{19,3},{18,19},{17,18},{16,17},{0,16},{5,4},{6,5... | collective-permute-start | bytes 393224 | tf_op jit(solution)/shard_map/ppermute | solution.py:594
  26.5 0.7 %cross_attend.1.cross_ref = f32[2,2,128,1024]{3,2,1,0:T(8,128)S(1)} custom-call(f32[16,128]{1,0:T(8,128)S(1)} %get-tuple-element.41.factor_ref, bf16[2,128,2048]{2,1,0:T(8,128)(2,1)S(1)} %get-tuple-element.31.q_ref, bf16[8,2048]{1,0:T(8,128)(2,1)S(1)} %joined.1.refs_0_, bf16[8,2048]{1,0:T(8,128)(2,1)S(1)} %collective-permute-done.9.refs_1_, ...), custom_call_target="tpu_custom_call" | custom-call | flops 268435456 | bytes 1048576 | tf_op jit(solution)/shard_map/cross_attend/pallas_call | solution.py:350
  27.3 0.2 fold_blocks.5
  27.5 1.2 %early_rows.1._ = bf16[2,128,2048]{2,1,0:T(8,128)(2,1)} custom-call(bf16[2,128,2048]{2,1,0:T(8,128)(2,1)S(1)} %get-tuple-element.31.q_ref, f32[2,2,128,1024]{3,2,1,0:T(8,128)S(1)} %cross_attend.1.cross_ref, f32[2,2,2,1024]{3,2,1,0:T(2,128)S(1)} %get-tuple-element.44.stat_ref, f32[2,2,128,1024]{3,2,1,0:T(8,128)S(1)} %get-tuple-element.45.sum_ref), custom_call_target="tpu_custom_call" | custom-call | flops 67108864 | bytes 1048576 | tf_op jit(solution)/shard_map/early_rows/pallas_call | solution.py:413
  28.7 0.7 %collective-permute-done.14.block = bf16[1,128,512]{2,1,0:T(8,128)(2,1)S(1)} collective-permute-done((bf16[1,128,512]{2,1,0:T(8,128)(2,1)S(1)}, bf16[1,128,512]{2,1,0:T(8,128)(2,1)S(1)}, u32[]{:S(2)}, u32[]{:S(2)}) %collective-permute-start.14) | collective-permute-done | bytes 131104 | tf_op jit(solution)/shard_map/ppermute | solution.py:589
  29.4 1.5 %collective-permute-done.12.block = bf16[1,128,512]{2,1,0:T(8,128)(2,1)S(1)} collective-permute-done((bf16[1,128,512]{2,1,0:T(8,128)(2,1)S(1)}, bf16[1,128,512]{2,1,0:T(8,128)(2,1)S(1)}, u32[]{:S(2)}, u32[]{:S(2)}) %collective-permute-start.12) | collective-permute-done | bytes 131104 | tf_op jit(solution)/shard_map/ppermute | solution.py:594
  (9 shorter events, 0.2 us)
Async XLA Ops:
  0.0 1.2 %copy-start = (bf16[2,128,2048]{2,1,0:T(8,128)(2,1)S(1)}, bf16[2,128,2048]{2,1,0:T(8,128)(2,1)}, u32[]{:S(2)}) copy-start(bf16[2,128,2048]{2,1,0:T(8,128)(2,1)} %param.6) | copy-start | bytes 3145732
  2.5 8.2 %collective-permute-start.2 = (bf16[2,128,512]{2,1,0:T(8,128)(2,1)S(1)}, bf16[2,128,512]{2,1,0:T(8,128)(2,1)S(1)}, u32[]{:S(2)}, u32[]{:S(2)}) collective-permute-start(bf16[2,128,512]{2,1,0:T(8,128)(2,1)S(1)} %constant_dynamic-slice_fusion.refs_0_), channel_id=1, source_target_pairs={{0,1},{1,2},{2,3},{3,19},{19,18},{18,17},{17,16},{16,0},{4,5},{5,6... | collective-permute-start | bytes 786440 | tf_op jit(solution)/shard_map/ppermute | solution.py:589
  5.6 7.0 %collective-permute-start = (bf16[2,128,512]{2,1,0:T(8,128)(2,1)S(1)}, bf16[2,128,512]{2,1,0:T(8,128)(2,1)S(1)}, u32[]{:S(2)}, u32[]{:S(2)}) collective-permute-start(bf16[2,128,512]{2,1,0:T(8,128)(2,1)S(1)} %constant_dynamic-slice_fusion.refs_0_), channel_id=1, source_target_pairs={{1,0},{2,1},{3,2},{19,3},{18,19},{17,18},{16,17},{0,16},{5,4},{6,5... | collective-permute-start | bytes 786440 | tf_op jit(solution)/shard_map/ppermute | solution.py:594
  5.6 8.1 %collective-permute-start.3 = (bf16[1,2048]{1,0:T(2,128)(2,1)}, bf16[1,2048]{1,0:T(2,128)(2,1)S(1)}, u32[]{:S(2)}, u32[]{:S(2)}) collective-permute-start(bf16[1,2048]{1,0:T(2,128)(2,1)} %image_ref.3), channel_id=1, source_target_pairs={{0,2},{1,3},{2,0},{3,1},{4,6},{5,7},{6,4},{7,5},{8,10},{9,11},{10,... | collective-permute-start | bytes 12296 | tf_op jit(solution)/shard_map/ppermute | solution.py:602
  8.6 5.8 %collective-permute-start.5 = (bf16[1,2048]{1,0:T(2,128)(2,1)}, bf16[1,2048]{1,0:T(2,128)(2,1)S(1)}, u32[]{:S(2)}, u32[]{:S(2)}) collective-permute-start(bf16[1,2048]{1,0:T(2,128)(2,1)} %image_ref.3), channel_id=1, source_target_pairs={{0,18},{1,19},{2,16},{3,17},{16,2},{17,3},{18,0},{19,1},{4,22},{5,... | collective-permute-start | bytes 12296 | tf_op jit(solution)/shard_map/ppermute | solution.py:602
  9.9 4.5 %collective-permute-start.4 = (bf16[1,2048]{1,0:T(2,128)(2,1)}, bf16[1,2048]{1,0:T(2,128)(2,1)S(1)}, u32[]{:S(2)}, u32[]{:S(2)}) collective-permute-start(bf16[1,2048]{1,0:T(2,128)(2,1)} %image_ref.3), channel_id=1, source_target_pairs={{0,16},{16,0},{1,17},{17,1},{2,18},{18,2},{3,19},{19,3},{4,20},{20... | collective-permute-start | bytes 12296 | tf_op jit(solution)/shard_map/ppermute | solution.py:602
  10.7 7.2 %collective-permute-start.8 = (bf16[2,128,512]{2,1,0:T(8,128)(2,1)S(1)}, bf16[2,128,512]{2,1,0:T(8,128)(2,1)S(1)}, u32[]{:S(2)}, u32[]{:S(2)}) collective-permute-start(bf16[2,128,512]{2,1,0:T(8,128)(2,1)S(1)} %collective-permute-done.2.refs_1_), channel_id=1, source_target_pairs={{0,1},{1,2},{2,3},{3,19},{19,18},{18,17},{17,16},{16,0},{4,5},{5,6... | collective-permute-start | bytes 786440 | tf_op jit(solution)/shard_map/ppermute | solution.py:589
  12.6 6.9 %collective-permute-start.1 = (bf16[2,128,512]{2,1,0:T(8,128)(2,1)S(1)}, bf16[2,128,512]{2,1,0:T(8,128)(2,1)S(1)}, u32[]{:S(2)}, u32[]{:S(2)}) collective-permute-start(bf16[2,128,512]{2,1,0:T(8,128)(2,1)S(1)} %collective-permute-done.refs_2_), channel_id=1, source_target_pairs={{1,0},{2,1},{3,2},{19,3},{18,19},{17,18},{16,17},{0,16},{5,4},{6,5... | collective-permute-start | bytes 786440 | tf_op jit(solution)/shard_map/ppermute | solution.py:594
  14.5 5.0 %collective-permute-start.6 = (bf16[4,2048]{1,0:T(4,128)(2,1)S(1)}, bf16[4,2048]{1,0:T(4,128)(2,1)S(1)}, u32[]{:S(2)}, u32[]{:S(2)}) collective-permute-start(bf16[4,2048]{1,0:T(4,128)(2,1)S(1)} %pad_maximum_fusion.first_ref), channel_id=1, source_target_pairs={{0,1},{1,0},{2,3},{3,2},{4,5},{5,4},{6,7},{7,6},{8,9},{9,8},{10,11... | collective-permute-start | bytes 49160 | tf_op jit(solution)/shard_map/ppermute | solution.py:602
  17.9 6.4 %collective-permute-start.13 = (bf16[2,128,512]{2,1,0:T(8,128)(2,1)S(1)}, bf16[2,128,512]{2,1,0:T(8,128)(2,1)S(1)}, u32[]{:S(2)}, u32[]{:S(2)}) collective-permute-start(bf16[2,128,512]{2,1,0:T(8,128)(2,1)S(1)} %collective-permute-done.8.refs_0_), channel_id=1, source_target_pairs={{0,1},{1,2},{2,3},{3,19},{19,18},{18,17},{17,16},{16,0},{4,5},{5,6... | collective-permute-start | bytes 786440 | tf_op jit(solution)/shard_map/ppermute | solution.py:589
  19.5 6.4 %collective-permute-start.7 = (bf16[2,128,512]{2,1,0:T(8,128)(2,1)S(1)}, bf16[2,128,512]{2,1,0:T(8,128)(2,1)S(1)}, u32[]{:S(2)}, u32[]{:S(2)}) collective-permute-start(bf16[2,128,512]{2,1,0:T(8,128)(2,1)S(1)} %collective-permute-done.1.refs_1_), channel_id=1, source_target_pairs={{1,0},{2,1},{3,2},{19,3},{18,19},{17,18},{16,17},{0,16},{5,4},{6,5... | collective-permute-start | bytes 786440 | tf_op jit(solution)/shard_map/ppermute | solution.py:594
  20.0 5.8 %collective-permute-start.11 = (bf16[8,2048]{1,0:T(8,128)(2,1)S(1)}, bf16[8,2048]{1,0:T(8,128)(2,1)S(1)}, u32[]{:S(2)}, u32[]{:S(2)}) collective-permute-start(bf16[8,2048]{1,0:T(8,128)(2,1)S(1)} %joined.1.refs_0_), channel_id=1, source_target_pairs={{0,12},{4,8},{8,4},{12,0},{1,13},{5,9},{9,5},{13,1},{2,14},{6,10},... | collective-permute-start | bytes 98312 | tf_op jit(solution)/shard_map/ppermute | solution.py:602
  20.1 5.8 %collective-permute-start.10 = (bf16[8,2048]{1,0:T(8,128)(2,1)S(1)}, bf16[8,2048]{1,0:T(8,128)(2,1)S(1)}, u32[]{:S(2)}, u32[]{:S(2)}) collective-permute-start(bf16[8,2048]{1,0:T(8,128)(2,1)S(1)} %joined.1.refs_0_), channel_id=1, source_target_pairs={{0,8},{4,12},{8,0},{12,4},{1,9},{5,13},{9,1},{13,5},{2,10},{6,14},... | collective-permute-start | bytes 98312 | tf_op jit(solution)/shard_map/ppermute | solution.py:602
  21.6 4.2 %collective-permute-start.9 = (bf16[8,2048]{1,0:T(8,128)(2,1)S(1)}, bf16[8,2048]{1,0:T(8,128)(2,1)S(1)}, u32[]{:S(2)}, u32[]{:S(2)}) collective-permute-start(bf16[8,2048]{1,0:T(8,128)(2,1)S(1)} %joined.1.refs_0_), channel_id=1, source_target_pairs={{0,4},{4,0},{8,12},{12,8},{1,5},{5,1},{9,13},{13,9},{2,6},{6,2},{1... | collective-permute-start | bytes 98312 | tf_op jit(solution)/shard_map/ppermute | solution.py:602
  24.3 5.0 %collective-permute-start.14 = (bf16[1,128,512]{2,1,0:T(8,128)(2,1)S(1)}, bf16[1,128,512]{2,1,0:T(8,128)(2,1)S(1)}, u32[]{:S(2)}, u32[]{:S(2)}) collective-permute-start(bf16[1,128,512]{2,1,0:T(8,128)(2,1)S(1)} %half_of.3), channel_id=1, source_target_pairs={{0,1},{1,2},{2,3},{3,19},{19,18},{18,17},{17,16},{16,0},{4,5},{5,6... | collective-permute-start | bytes 393224 | tf_op jit(solution)/shard_map/ppermute | solution.py:589
  25.9 5.0 %collective-permute-start.12 = (bf16[1,128,512]{2,1,0:T(8,128)(2,1)S(1)}, bf16[1,128,512]{2,1,0:T(8,128)(2,1)S(1)}, u32[]{:S(2)}, u32[]{:S(2)}) collective-permute-start(bf16[1,128,512]{2,1,0:T(8,128)(2,1)S(1)} %half_of.2), channel_id=1, source_target_pairs={{1,0},{2,1},{3,2},{19,3},{18,19},{17,18},{16,17},{0,16},{5,4},{6,5... | collective-permute-start | bytes 393224 | tf_op jit(solution)/shard_map/ppermute | solution.py:594

commit v6 on v5

--- a/solution.py
+++ b/solution.py
@@ -505,8 +505,9 @@
     )(*args, result)
 
 
-def load_kernel(parity, lengths, gate, q_ref, image_ref, *refs):
+def load_kernel(parity, *refs):
     limit_ref, factor_ref, q_out, image_out, counts, gates, sems = refs[-7:]
+    lengths, gate, q_ref, image_ref = refs[:4]
 
     def work():
         pairs = ((lengths, counts), (gate, gates), (q_ref, q_out), (image_ref, image_out))
@@ -523,28 +524,41 @@
         copies[2].wait()
         copies[3].wait()
 
+    own = None
+    if parity == 0:
+        kv_ref, own_ref = refs[4:6]
+        width = own_ref.shape[2]
+        columns = pl.ds(pl.multiple_of(lax.axis_index("tp") * width, width), width)
+        own = pltpu.make_async_copy(kv_ref.at[:, :, columns], own_ref, sems.at[4])
+        own.start()
     pl.when((lax.axis_index("tp") & 1) == parity)(work)
+    if own is not None:
+        own.wait()
 
 
 def load_inputs(parity, loaded, *arrays):
-    lengths, gate, q, image = arrays
+    lengths, gate, q, image = arrays[:4]
     rows = q.shape[1]
+    shapes = [
+        pltpu.VMEM((lengths.shape[0], rows), jnp.int32),
+        pltpu.VMEM((gate.shape[0], rows), jnp.float32),
+        pltpu.VMEM(q.shape, q.dtype),
+        pltpu.VMEM(image.shape, image.dtype),
+    ]
+    if parity == 0:
+        kv = arrays[4]
+        shapes = [pltpu.VMEM((*kv.shape[:2], kv.shape[2] // lax.axis_size("tp")), kv.dtype)] + shapes
     return pl.pallas_call(
         functools.partial(load_kernel, parity),
-        in_specs=[ANY_SPEC] * 4 + [VMEM_SPEC] * len(loaded),
-        out_specs=[VMEM_SPEC] * 4,
-        out_shape=[
-            pltpu.VMEM((lengths.shape[0], rows), jnp.int32),
-            pltpu.VMEM((gate.shape[0], rows), jnp.float32),
-            pltpu.VMEM(q.shape, q.dtype),
-            pltpu.VMEM(image.shape, image.dtype),
-        ],
+        in_specs=[ANY_SPEC] * len(arrays) + [VMEM_SPEC] * len(loaded),
+        out_specs=[VMEM_SPEC] * len(shapes),
+        out_shape=shapes,
         scratch_shapes=[
             pltpu.SMEM(lengths.shape, lengths.dtype),
             pltpu.SMEM(gate.shape, gate.dtype),
-            pltpu.SemaphoreType.DMA((4,)),
+            pltpu.SemaphoreType.DMA((5,)),
         ],
-        input_output_aliases={4 + i: i for i in range(len(loaded))},
+        input_output_aliases={len(arrays) + i: i for i in range(len(loaded))},
         compiler_params=KERNEL,
         name="load_inputs",
     )(*[pltpu.with_memory_space_constraint(array, pltpu.HBM) for array in arrays], *in_vmem(*loaded))
@@ -605,14 +619,11 @@
 def ring_device(queries, self_kv, image_kv, cross_gate, lengths):
     tp_count = lax.axis_size("tp")
     groups = KVH // tp_count
-    kv_cols = groups * 2 * HEAD_SIZE
-    own = lax.dynamic_slice_in_dim(self_kv, lax.axis_index("tp") * kv_cols, kv_cols, 2)
-    loaded = load_inputs(0, (), lengths, cross_gate, queries, image_kv)
-    own = after(own, loaded[0])
+    own, *loaded = load_inputs(0, (), lengths, cross_gate, queries, image_kv, self_kv)
     f1, b1 = ring_forward(own), ring_backward(own)
     sections = lax.axis_size("section")
+    n2 = swapped(image_kv, "ctx", 1)
     n1 = swapped(image_kv, "section", 2)
-    n2 = swapped(image_kv, "ctx", 1)
     n3 = swapped(image_kv, ("ctx", "section"), sections + 2)
     limits, factors, q, image1 = load_inputs(1, tuple(loaded), lengths, cross_gate, queries, image_kv)
 

time: 31.3 us -> 31 us (level)
  local copies, waits for them, and re-layouts: 1.24 us -> 0.01 us
  waiting for transfers between devices: 6.94 us -> 8.05 us
    ppermute x4, waiting for transfers between devices: 3.6 us -> 5.44 us  [ring_forward(): return lax.ppermute(block, ('ctx', 'section'), pairs)]
    unnamed x2, local copies, waits for them, and re-layouts: 1.22 us -> 0.01 us
    ppermute x7, waiting for transfers between devices: 1.77 us -> 0.98 us  [swapped(): lax.ppermute(rows, name, [(i, i ^ bits) for i in range(lax.axis_size(name...]
  transfers between devices with their start and end apart: 15 -> 15, of which waited for: 7 -> 6; matrix products, arithmetic and copies ran while one was open for 0% -> 0% of each run, Pallas kernels for 13% -> 13%
where the time goes in v6:
time: 31 us; the launch traced here: 30.8 us
  starting transfers between devices  17.1 us (55%)
  waiting for transfers between devices  8.05 us (26%)
  Pallas kernels  5.38 us (17%)
    ppermute x4, starting transfers between devices, ring_forward(): return lax.ppermute(block, ('ctx', 'section'), pairs)  8.07 us
    ppermute x7, starting transfers between devices, swapped(): lax.ppermute(rows, name, [(i, i ^ bits) for i in range(lax.axis_size(name...  7.83 us
    ppermute x4, waiting for transfers between devices, ring_forward(): return lax.ppermute(block, ('ctx', 'section'), pairs)  5.44 us
    pallas_call x3, Pallas kernels, fold_blocks(): pl.pallas_call(functools.partial(fold_kernel, first, shifts, groups), in_...  1.99 us
    ppermute x4, waiting for transfers between devices, ring_backward(): return lax.ppermute(block, ('ctx', 'section'), pairs)  1.63 us
    pallas_call x2, Pallas kernels, load_inputs(): pl.pallas_call(functools.partial(load_kernel, parity), in_specs=[ANY_SPEC...  1.42 us
    ppermute x4, starting transfers between devices, ring_backward(): return lax.ppermute(block, ('ctx', 'section'), pairs)  1.19 us
    pallas_call x1, Pallas kernels, early_rows(): pl.pallas_call(functools.partial(early_kernel, last_shift, groups), in_sp...  1.17 us
  transfers between devices with their start and end apart: 15, of which 6 were waited for; matrix products, arithmetic and copies ran while one was open for 0% of the time, Pallas kernels for 13%

profile of v6, /device:TPU:0, one launch (start us, length us, event | category | flops | bytes accessed | tf_op | source)
XLA Modules:
  0.0 30.8 jit_solution(3967535044308217720)
XLA Ops:
  0.0 0.0 copy-start
  0.0 1.4 %load_inputs.2 = (bf16[2,128,512]{2,1,0:T(8,128)(2,1)S(1)}, s32[2,128]{1,0:T(2,128)S(1)}, f32[16,128]{1,0:T(8,128)S(1)}, bf16[2,128,2048]{2,1,0:T(8,128)(2,1)S(1)}, bf16[1,2048]{1,0:T(2,128)(2,1)S(1)}) custom-call(s32[2]{0:T(128)} %refs_0_.3, f32[16]{0:T(128)} %refs_1_.3, bf16[2,128,2048]{2,1,0:T(8,128)(2,1)} %refs_2_.3, bf16[1,2048]{1,0:T(2,128)(2,1)} %refs_3_.3, ...), custom_call_target="tpu_custom_call" | custom-call | tf_op jit(solution)/shard_map/load_inputs/pallas_call | solution.py:551
  1.4 3.1 %collective-permute-start.2 = (bf16[2,128,512]{2,1,0:T(8,128)(2,1)S(1)}, bf16[2,128,512]{2,1,0:T(8,128)(2,1)S(1)}, u32[]{:S(2)}, u32[]{:S(2)}) collective-permute-start(bf16[2,128,512]{2,1,0:T(8,128)(2,1)S(1)} %get-tuple-element.32.refs_0_), channel_id=1, source_target_pairs={{0,1},{1,2},{2,3},{3,19},{19,18},{18,17},{17,16},{16,0},{4,5},{5,6... | collective-permute-start | bytes 786440 | tf_op jit(solution)/shard_map/ppermute | solution.py:603
  4.5 0.0 collective-permute-start
  4.5 0.0 copy-done
  4.5 3.0 %collective-permute-start.3 = (bf16[1,2048]{1,0:T(2,128)(2,1)S(1)}, bf16[1,2048]{1,0:T(2,128)(2,1)S(1)}, u32[]{:S(2)}, u32[]{:S(2)}) collective-permute-start(bf16[1,2048]{1,0:T(2,128)(2,1)S(1)} %copy-done), channel_id=1, source_target_pairs={{0,2},{1,3},{2,0},{3,1},{4,6},{5,7},{6,4},{7,5},{8,10},{9,11},{10,... | collective-permute-start | bytes 12296 | tf_op jit(solution)/shard_map/ppermute | solution.py:616
  7.5 1.3 %collective-permute-start.5 = (bf16[1,2048]{1,0:T(2,128)(2,1)S(1)}, bf16[1,2048]{1,0:T(2,128)(2,1)S(1)}, u32[]{:S(2)}, u32[]{:S(2)}) collective-permute-start(bf16[1,2048]{1,0:T(2,128)(2,1)S(1)} %copy-done), channel_id=1, source_target_pairs={{0,18},{1,19},{2,16},{3,17},{16,2},{17,3},{18,0},{19,1},{4,22},{5,... | collective-permute-start | bytes 12296 | tf_op jit(solution)/shard_map/ppermute | solution.py:616
  8.8 0.2 collective-permute-start.4
  9.1 1.4 %collective-permute-done.2.refs_1_ = bf16[2,128,512]{2,1,0:T(8,128)(2,1)S(1)} collective-permute-done((bf16[2,128,512]{2,1,0:T(8,128)(2,1)S(1)}, bf16[2,128,512]{2,1,0:T(8,128)(2,1)S(1)}, u32[]{:S(2)}, u32[]{:S(2)}) %collective-permute-start.2) | collective-permute-done | bytes 262176 | tf_op jit(solution)/shard_map/ppermute | solution.py:603
  10.4 1.9 %collective-permute-start.8 = (bf16[2,128,512]{2,1,0:T(8,128)(2,1)S(1)}, bf16[2,128,512]{2,1,0:T(8,128)(2,1)S(1)}, u32[]{:S(2)}, u32[]{:S(2)}) collective-permute-start(bf16[2,128,512]{2,1,0:T(8,128)(2,1)S(1)} %collective-permute-done.2.refs_1_), channel_id=1, source_target_pairs={{0,1},{1,2},{2,3},{3,19},{19,18},{18,17},{17,16},{16,0},{4,5},{5,6... | collective-permute-start | bytes 786440 | tf_op jit(solution)/shard_map/ppermute | solution.py:603
  12.3 0.0 collective-permute-done.refs_2_
  12.3 0.1 collective-permute-start.1
  12.5 1.0 %collective-permute-done.3 = bf16[1,2048]{1,0:T(2,128)(2,1)S(1)} collective-permute-done((bf16[1,2048]{1,0:T(2,128)(2,1)S(1)}, bf16[1,2048]{1,0:T(2,128)(2,1)S(1)}, u32[]{:S(2)}, u32[]{:S(2)}) %collective-permute-start.3) | collective-permute-done | bytes 4128 | tf_op jit(solution)/shard_map/ppermute | solution.py:616
  13.4 0.0 collective-permute-done.5
  13.4 0.0 collective-permute-done.4
  13.5 1.4 %collective-permute-start.6 = (bf16[4,2048]{1,0:T(4,128)(2,1)S(1)}, bf16[4,2048]{1,0:T(4,128)(2,1)S(1)}, u32[]{:S(2)}, u32[]{:S(2)}) collective-permute-start(bf16[4,2048]{1,0:T(4,128)(2,1)S(1)} %pad_maximum_fusion.first_ref), channel_id=1, source_target_pairs={{0,1},{1,0},{2,3},{3,2},{4,5},{5,4},{6,7},{7,6},{8,9},{9,8},{10,11... | collective-permute-start | bytes 49160 | tf_op jit(solution)/shard_map/ppermute | solution.py:616
  14.8 1.8 %fold_blocks.3 = (f32[2,2,2,1024]{3,2,1,0:T(2,128)S(1)}, f32[2,2,128,1024]{3,2,1,0:T(8,128)S(1)}) custom-call(s32[2,128]{1,0:T(2,128)S(1)} %get-tuple-element.30.length_ref, bf16[2,128,2048]{2,1,0:T(8,128)(2,1)S(1)} %get-tuple-element.31.q_ref, bf16[2,128,512]{2,1,0:T(8,128)(2,1)S(1)} %get-tuple-element.32.refs_0_, ...), custom_call_target="tpu_custom_call" | custom-call | flops 805306368 | bytes 1048576 | tf_op jit(solution)/shard_map/fold_blocks/pallas_call | solution.py:314
  16.6 1.0 %collective-permute-done.8.refs_0_ = bf16[2,128,512]{2,1,0:T(8,128)(2,1)S(1)} collective-permute-done((bf16[2,128,512]{2,1,0:T(8,128)(2,1)S(1)}, bf16[2,128,512]{2,1,0:T(8,128)(2,1)S(1)}, u32[]{:S(2)}, u32[]{:S(2)}) %collective-permute-start.8) | collective-permute-done | bytes 262176 | tf_op jit(solution)/shard_map/ppermute | solution.py:603
  17.6 1.5 %collective-permute-start.13 = (bf16[2,128,512]{2,1,0:T(8,128)(2,1)S(1)}, bf16[2,128,512]{2,1,0:T(8,128)(2,1)S(1)}, u32[]{:S(2)}, u32[]{:S(2)}) collective-permute-start(bf16[2,128,512]{2,1,0:T(8,128)(2,1)S(1)} %collective-permute-done.8.refs_0_), channel_id=1, source_target_pairs={{0,1},{1,2},{2,3},{3,19},{19,18},{18,17},{17,16},{16,0},{4,5},{5,6... | collective-permute-start | bytes 786440 | tf_op jit(solution)/shard_map/ppermute | solution.py:603
  19.1 0.0 collective-permute-done.6.second_ref
  19.1 0.0 collective-permute-done.1.refs_1_
  19.2 0.5 %collective-permute-start.7 = (bf16[2,128,512]{2,1,0:T(8,128)(2,1)S(1)}, bf16[2,128,512]{2,1,0:T(8,128)(2,1)S(1)}, u32[]{:S(2)}, u32[]{:S(2)}) collective-permute-start(bf16[2,128,512]{2,1,0:T(8,128)(2,1)S(1)} %collective-permute-done.1.refs_1_), channel_id=1, source_target_pairs={{1,0},{2,1},{3,2},{19,3},{18,19},{17,18},{16,17},{0,16},{5,4},{6,5... | collective-permute-start | bytes 786440 | tf_op jit(solution)/shard_map/ppermute | solution.py:608
  19.7 0.1 collective-permute-start.11
  19.7 1.4 %collective-permute-start.10 = (bf16[8,2048]{1,0:T(8,128)(2,1)S(1)}, bf16[8,2048]{1,0:T(8,128)(2,1)S(1)}, u32[]{:S(2)}, u32[]{:S(2)}) collective-permute-start(bf16[8,2048]{1,0:T(8,128)(2,1)S(1)} %joined.1.refs_0_), channel_id=1, source_target_pairs={{0,8},{4,12},{8,0},{12,4},{1,9},{5,13},{9,1},{13,5},{2,10},{6,14},... | collective-permute-start | bytes 98312 | tf_op jit(solution)/shard_map/ppermute | solution.py:616
  21.2 0.4 %collective-permute-start.9 = (bf16[8,2048]{1,0:T(8,128)(2,1)S(1)}, bf16[8,2048]{1,0:T(8,128)(2,1)S(1)}, u32[]{:S(2)}, u32[]{:S(2)}) collective-permute-start(bf16[8,2048]{1,0:T(8,128)(2,1)S(1)} %joined.1.refs_0_), channel_id=1, source_target_pairs={{0,4},{4,0},{8,12},{12,8},{1,5},{5,1},{9,13},{13,9},{2,6},{6,2},{1... | collective-permute-start | bytes 98312 | tf_op jit(solution)/shard_map/ppermute | solution.py:616
  21.6 2.4 %collective-permute-done.13.refs_0_.block_ref = bf16[2,128,512]{2,1,0:T(8,128)(2,1)S(1)} collective-permute-done((bf16[2,128,512]{2,1,0:T(8,128)(2,1)S(1)}, bf16[2,128,512]{2,1,0:T(8,128)(2,1)S(1)}, u32[]{:S(2)}, u32[]{:S(2)}) %collective-permute-start.13) | collective-permute-done | bytes 262176 | tf_op jit(solution)/shard_map/ppermute | solution.py:603
  24.0 1.6 %collective-permute-start.14 = (bf16[1,128,512]{2,1,0:T(8,128)(2,1)S(1)}, bf16[1,128,512]{2,1,0:T(8,128)(2,1)S(1)}, u32[]{:S(2)}, u32[]{:S(2)}) collective-permute-start(bf16[1,128,512]{2,1,0:T(8,128)(2,1)S(1)} %half_of.3), channel_id=1, source_target_pairs={{0,1},{1,2},{2,3},{3,19},{19,18},{18,17},{17,16},{16,0},{4,5},{5,6... | collective-permute-start | bytes 393224 | tf_op jit(solution)/shard_map/ppermute | solution.py:603
  25.6 0.0 collective-permute-done.11.refs_3_
  25.6 0.0 collective-permute-done.10.refs_2_
  25.6 0.0 collective-permute-done.9.refs_1_
  25.6 0.0 collective-permute-done.7.block_ref.refs_1_
  25.6 0.5 %collective-permute-start.12 = (bf16[1,128,512]{2,1,0:T(8,128)(2,1)S(1)}, bf16[1,128,512]{2,1,0:T(8,128)(2,1)S(1)}, u32[]{:S(2)}, u32[]{:S(2)}) collective-permute-start(bf16[1,128,512]{2,1,0:T(8,128)(2,1)S(1)} %half_of.2), channel_id=1, source_target_pairs={{1,0},{2,1},{3,2},{19,3},{18,19},{17,18},{16,17},{0,16},{5,4},{6,5... | collective-permute-start | bytes 393224 | tf_op jit(solution)/shard_map/ppermute | solution.py:608
  26.2 0.7 %cross_attend.1.cross_ref = f32[2,2,128,1024]{3,2,1,0:T(8,128)S(1)} custom-call(f32[16,128]{1,0:T(8,128)S(1)} %get-tuple-element.41.factor_ref, bf16[2,128,2048]{2,1,0:T(8,128)(2,1)S(1)} %get-tuple-element.31.q_ref, bf16[8,2048]{1,0:T(8,128)(2,1)S(1)} %joined.1.refs_0_, bf16[8,2048]{1,0:T(8,128)(2,1)S(1)} %collective-permute-done.9.refs_1_, ...), custom_call_target="tpu_custom_call" | custom-call | flops 268435456 | bytes 1048576 | tf_op jit(solution)/shard_map/cross_attend/pallas_call | solution.py:350
  26.9 0.2 fold_blocks.5
  27.1 1.2 %early_rows.1._ = bf16[2,128,2048]{2,1,0:T(8,128)(2,1)} custom-call(bf16[2,128,2048]{2,1,0:T(8,128)(2,1)S(1)} %get-tuple-element.31.q_ref, f32[2,2,128,1024]{3,2,1,0:T(8,128)S(1)} %cross_attend.1.cross_ref, f32[2,2,2,1024]{3,2,1,0:T(2,128)S(1)} %get-tuple-element.44.stat_ref, f32[2,2,128,1024]{3,2,1,0:T(8,128)S(1)} %get-tuple-element.45.sum_ref), custom_call_target="tpu_custom_call" | custom-call | flops 67108864 | bytes 1048576 | tf_op jit(solution)/shard_map/early_rows/pallas_call | solution.py:413
  28.3 0.7 %collective-permute-done.14.block = bf16[1,128,512]{2,1,0:T(8,128)(2,1)S(1)} collective-permute-done((bf16[1,128,512]{2,1,0:T(8,128)(2,1)S(1)}, bf16[1,128,512]{2,1,0:T(8,128)(2,1)S(1)}, u32[]{:S(2)}, u32[]{:S(2)}) %collective-permute-start.14) | collective-permute-done | bytes 131104 | tf_op jit(solution)/shard_map/ppermute | solution.py:603
  29.0 1.6 %collective-permute-done.12.block = bf16[1,128,512]{2,1,0:T(8,128)(2,1)S(1)} collective-permute-done((bf16[1,128,512]{2,1,0:T(8,128)(2,1)S(1)}, bf16[1,128,512]{2,1,0:T(8,128)(2,1)S(1)}, u32[]{:S(2)}, u32[]{:S(2)}) %collective-permute-start.12) | collective-permute-done | bytes 131104 | tf_op jit(solution)/shard_map/ppermute | solution.py:608
  (8 shorter events, 0.2 us)
Async XLA Ops:
  0.0 4.5 %copy-start = (bf16[1,2048]{1,0:T(2,128)(2,1)S(1)}, bf16[1,2048]{1,0:T(2,128)(2,1)}, u32[]{:S(2)}) copy-start(bf16[1,2048]{1,0:T(2,128)(2,1)} %refs_3_.3) | copy-start | bytes 12292
  1.4 9.0 %collective-permute-start.2 = (bf16[2,128,512]{2,1,0:T(8,128)(2,1)S(1)}, bf16[2,128,512]{2,1,0:T(8,128)(2,1)S(1)}, u32[]{:S(2)}, u32[]{:S(2)}) collective-permute-start(bf16[2,128,512]{2,1,0:T(8,128)(2,1)S(1)} %get-tuple-element.32.refs_0_), channel_id=1, source_target_pairs={{0,1},{1,2},{2,3},{3,19},{19,18},{18,17},{17,16},{16,0},{4,5},{5,6... | collective-permute-start | bytes 786440 | tf_op jit(solution)/shard_map/ppermute | solution.py:603
  4.5 7.9 %collective-permute-start = (bf16[2,128,512]{2,1,0:T(8,128)(2,1)S(1)}, bf16[2,128,512]{2,1,0:T(8,128)(2,1)S(1)}, u32[]{:S(2)}, u32[]{:S(2)}) collective-permute-start(bf16[2,128,512]{2,1,0:T(8,128)(2,1)S(1)} %get-tuple-element.32.refs_0_), channel_id=1, source_target_pairs={{1,0},{2,1},{3,2},{19,3},{18,19},{17,18},{16,17},{0,16},{5,4},{6,5... | collective-permute-start | bytes 786440 | tf_op jit(solution)/shard_map/ppermute | solution.py:608
  4.5 8.9 %collective-permute-start.3 = (bf16[1,2048]{1,0:T(2,128)(2,1)S(1)}, bf16[1,2048]{1,0:T(2,128)(2,1)S(1)}, u32[]{:S(2)}, u32[]{:S(2)}) collective-permute-start(bf16[1,2048]{1,0:T(2,128)(2,1)S(1)} %copy-done), channel_id=1, source_target_pairs={{0,2},{1,3},{2,0},{3,1},{4,6},{5,7},{6,4},{7,5},{8,10},{9,11},{10,... | collective-permute-start | bytes 12296 | tf_op jit(solution)/shard_map/ppermute | solution.py:616
  7.5 5.9 %collective-permute-start.5 = (bf16[1,2048]{1,0:T(2,128)(2,1)S(1)}, bf16[1,2048]{1,0:T(2,128)(2,1)S(1)}, u32[]{:S(2)}, u32[]{:S(2)}) collective-permute-start(bf16[1,2048]{1,0:T(2,128)(2,1)S(1)} %copy-done), channel_id=1, source_target_pairs={{0,18},{1,19},{2,16},{3,17},{16,2},{17,3},{18,0},{19,1},{4,22},{5,... | collective-permute-start | bytes 12296 | tf_op jit(solution)/shard_map/ppermute | solution.py:616
  8.8 4.6 %collective-permute-start.4 = (bf16[1,2048]{1,0:T(2,128)(2,1)S(1)}, bf16[1,2048]{1,0:T(2,128)(2,1)S(1)}, u32[]{:S(2)}, u32[]{:S(2)}) collective-permute-start(bf16[1,2048]{1,0:T(2,128)(2,1)S(1)} %copy-done), channel_id=1, source_target_pairs={{0,16},{16,0},{1,17},{17,1},{2,18},{18,2},{3,19},{19,3},{4,20},{20... | collective-permute-start | bytes 12296 | tf_op jit(solution)/shard_map/ppermute | solution.py:616
  10.4 7.2 %collective-permute-start.8 = (bf16[2,128,512]{2,1,0:T(8,128)(2,1)S(1)}, bf16[2,128,512]{2,1,0:T(8,128)(2,1)S(1)}, u32[]{:S(2)}, u32[]{:S(2)}) collective-permute-start(bf16[2,128,512]{2,1,0:T(8,128)(2,1)S(1)} %collective-permute-done.2.refs_1_), channel_id=1, source_target_pairs={{0,1},{1,2},{2,3},{3,19},{19,18},{18,17},{17,16},{16,0},{4,5},{5,6... | collective-permute-start | bytes 786440 | tf_op jit(solution)/shard_map/ppermute | solution.py:603
  12.3 6.8 %collective-permute-start.1 = (bf16[2,128,512]{2,1,0:T(8,128)(2,1)S(1)}, bf16[2,128,512]{2,1,0:T(8,128)(2,1)S(1)}, u32[]{:S(2)}, u32[]{:S(2)}) collective-permute-start(bf16[2,128,512]{2,1,0:T(8,128)(2,1)S(1)} %collective-permute-done.refs_2_), channel_id=1, source_target_pairs={{1,0},{2,1},{3,2},{19,3},{18,19},{17,18},{16,17},{0,16},{5,4},{6,5... | collective-permute-start | bytes 786440 | tf_op jit(solution)/shard_map/ppermute | solution.py:608
  13.5 5.7 %collective-permute-start.6 = (bf16[4,2048]{1,0:T(4,128)(2,1)S(1)}, bf16[4,2048]{1,0:T(4,128)(2,1)S(1)}, u32[]{:S(2)}, u32[]{:S(2)}) collective-permute-start(bf16[4,2048]{1,0:T(4,128)(2,1)S(1)} %pad_maximum_fusion.first_ref), channel_id=1, source_target_pairs={{0,1},{1,0},{2,3},{3,2},{4,5},{5,4},{6,7},{7,6},{8,9},{9,8},{10,11... | collective-permute-start | bytes 49160 | tf_op jit(solution)/shard_map/ppermute | solution.py:616
  17.6 6.4 %collective-permute-start.13 = (bf16[2,128,512]{2,1,0:T(8,128)(2,1)S(1)}, bf16[2,128,512]{2,1,0:T(8,128)(2,1)S(1)}, u32[]{:S(2)}, u32[]{:S(2)}) collective-permute-start(bf16[2,128,512]{2,1,0:T(8,128)(2,1)S(1)} %collective-permute-done.8.refs_0_), channel_id=1, source_target_pairs={{0,1},{1,2},{2,3},{3,19},{19,18},{18,17},{17,16},{16,0},{4,5},{5,6... | collective-permute-start | bytes 786440 | tf_op jit(solution)/shard_map/ppermute | solution.py:603
  19.2 6.4 %collective-permute-start.7 = (bf16[2,128,512]{2,1,0:T(8,128)(2,1)S(1)}, bf16[2,128,512]{2,1,0:T(8,128)(2,1)S(1)}, u32[]{:S(2)}, u32[]{:S(2)}) collective-permute-start(bf16[2,128,512]{2,1,0:T(8,128)(2,1)S(1)} %collective-permute-done.1.refs_1_), channel_id=1, source_target_pairs={{1,0},{2,1},{3,2},{19,3},{18,19},{17,18},{16,17},{0,16},{5,4},{6,5... | collective-permute-start | bytes 786440 | tf_op jit(solution)/shard_map/ppermute | solution.py:608
  19.7 5.9 %collective-permute-start.11 = (bf16[8,2048]{1,0:T(8,128)(2,1)S(1)}, bf16[8,2048]{1,0:T(8,128)(2,1)S(1)}, u32[]{:S(2)}, u32[]{:S(2)}) collective-permute-start(bf16[8,2048]{1,0:T(8,128)(2,1)S(1)} %joined.1.refs_0_), channel_id=1, source_target_pairs={{0,12},{4,8},{8,4},{12,0},{1,13},{5,9},{9,5},{13,1},{2,14},{6,10},... | collective-permute-start | bytes 98312 | tf_op jit(solution)/shard_map/ppermute | solution.py:616
  19.7 5.8 %collective-permute-start.10 = (bf16[8,2048]{1,0:T(8,128)(2,1)S(1)}, bf16[8,2048]{1,0:T(8,128)(2,1)S(1)}, u32[]{:S(2)}, u32[]{:S(2)}) collective-permute-start(bf16[8,2048]{1,0:T(8,128)(2,1)S(1)} %joined.1.refs_0_), channel_id=1, source_target_pairs={{0,8},{4,12},{8,0},{12,4},{1,9},{5,13},{9,1},{13,5},{2,10},{6,14},... | collective-permute-start | bytes 98312 | tf_op jit(solution)/shard_map/ppermute | solution.py:616
  21.2 4.4 %collective-permute-start.9 = (bf16[8,2048]{1,0:T(8,128)(2,1)S(1)}, bf16[8,2048]{1,0:T(8,128)(2,1)S(1)}, u32[]{:S(2)}, u32[]{:S(2)}) collective-permute-start(bf16[8,2048]{1,0:T(8,128)(2,1)S(1)} %joined.1.refs_0_), channel_id=1, source_target_pairs={{0,4},{4,0},{8,12},{12,8},{1,5},{5,1},{9,13},{13,9},{2,6},{6,2},{1... | collective-permute-start | bytes 98312 | tf_op jit(solution)/shard_map/ppermute | solution.py:616
  24.0 5.0 %collective-permute-start.14 = (bf16[1,128,512]{2,1,0:T(8,128)(2,1)S(1)}, bf16[1,128,512]{2,1,0:T(8,128)(2,1)S(1)}, u32[]{:S(2)}, u32[]{:S(2)}) collective-permute-start(bf16[1,128,512]{2,1,0:T(8,128)(2,1)S(1)} %half_of.3), channel_id=1, source_target_pairs={{0,1},{1,2},{2,3},{3,19},{19,18},{18,17},{17,16},{16,0},{4,5},{5,6... | collective-permute-start | bytes 393224 | tf_op jit(solution)/shard_map/ppermute | solution.py:603
  25.6 5.0 %collective-permute-start.12 = (bf16[1,128,512]{2,1,0:T(8,128)(2,1)S(1)}, bf16[1,128,512]{2,1,0:T(8,128)(2,1)S(1)}, u32[]{:S(2)}, u32[]{:S(2)}) collective-permute-start(bf16[1,128,512]{2,1,0:T(8,128)(2,1)S(1)} %half_of.2), channel_id=1, source_target_pairs={{1,0},{2,1},{3,2},{19,3},{18,19},{17,18},{16,17},{0,16},{5,4},{6,5... | collective-permute-start | bytes 393224 | tf_op jit(solution)/shard_map/ppermute | solution.py:608

commit v7 on v6

--- a/solution.py
+++ b/solution.py
@@ -635,7 +635,7 @@
     f3, b3 = ring_forward(after(f2, state[0])), ring_backward(after(b2, state[0], far))
     image8 = joined(image4, far)
     images = [image8] + [swapped(image8, "tp", bits) for bits in range(1, tp_count)]
-    state = fold_blocks(limits, q, [f2, after(b2, image8)], (-2, 2), state)
+    state = fold_blocks(limits, q, [f2, b2], (-2, 2), state)
 
     f4 = ring_forward(half_of(after(f3, state[0]), 0))
     b4 = ring_backward(half_of(after(b3, state[0], *images), 1))

time: 31 us -> 31 us (level)
  no operation moved by 1% of the time
where the time goes in v7:
time: 31 us; the launch traced here: 30.8 us
  starting transfers between devices  17.1 us (55%)
  waiting for transfers between devices  8.05 us (26%)
  Pallas kernels  5.38 us (17%)
    ppermute x4, starting transfers between devices, ring_forward(): return lax.ppermute(block, ('ctx', 'section'), pairs)  8.07 us
    ppermute x7, starting transfers between devices, swapped(): lax.ppermute(rows, name, [(i, i ^ bits) for i in range(lax.axis_size(name...  7.83 us
    ppermute x4, waiting for transfers between devices, ring_forward(): return lax.ppermute(block, ('ctx', 'section'), pairs)  5.44 us
    pallas_call x3, Pallas kernels, fold_blocks(): pl.pallas_call(functools.partial(fold_kernel, first, shifts, groups), in_...  1.99 us
    ppermute x4, waiting for transfers between devices, ring_backward(): return lax.ppermute(block, ('ctx', 'section'), pairs)  1.63 us
    pallas_call x2, Pallas kernels, load_inputs(): pl.pallas_call(functools.partial(load_kernel, parity), in_specs=[ANY_SPEC...  1.42 us
    ppermute x4, starting transfers between devices, ring_backward(): return lax.ppermute(block, ('ctx', 'section'), pairs)  1.19 us
    pallas_call x1, Pallas kernels, early_rows(): pl.pallas_call(functools.partial(early_kernel, last_shift, groups), in_sp...  1.17 us
  transfers between devices with their start and end apart: 15, of which 6 were waited for; matrix products, arithmetic and copies ran while one was open for 0% of the time, Pallas kernels for 13%

profile of v7, /device:TPU:0, one launch (start us, length us, event | category | flops | bytes accessed | tf_op | source)
XLA Modules:
  0.0 30.8 jit_solution(3967535044308217720)
XLA Ops:
  0.0 0.0 copy-start
  0.0 1.4 %load_inputs.2 = (bf16[2,128,512]{2,1,0:T(8,128)(2,1)S(1)}, s32[2,128]{1,0:T(2,128)S(1)}, f32[16,128]{1,0:T(8,128)S(1)}, bf16[2,128,2048]{2,1,0:T(8,128)(2,1)S(1)}, bf16[1,2048]{1,0:T(2,128)(2,1)S(1)}) custom-call(s32[2]{0:T(128)} %refs_0_.3, f32[16]{0:T(128)} %refs_1_.3, bf16[2,128,2048]{2,1,0:T(8,128)(2,1)} %refs_2_.3, bf16[1,2048]{1,0:T(2,128)(2,1)} %refs_3_.3, ...), custom_call_target="tpu_custom_call" | custom-call | tf_op jit(solution)/shard_map/load_inputs/pallas_call | solution.py:551
  1.4 3.1 %collective-permute-start.2 = (bf16[2,128,512]{2,1,0:T(8,128)(2,1)S(1)}, bf16[2,128,512]{2,1,0:T(8,128)(2,1)S(1)}, u32[]{:S(2)}, u32[]{:S(2)}) collective-permute-start(bf16[2,128,512]{2,1,0:T(8,128)(2,1)S(1)} %get-tuple-element.31.refs_0_), channel_id=1, source_target_pairs={{0,1},{1,2},{2,3},{3,19},{19,18},{18,17},{17,16},{16,0},{4,5},{5,6... | collective-permute-start | bytes 786440 | tf_op jit(solution)/shard_map/ppermute | solution.py:603
  4.5 0.0 collective-permute-start
  4.5 0.0 copy-done
  4.5 3.0 %collective-permute-start.3 = (bf16[1,2048]{1,0:T(2,128)(2,1)S(1)}, bf16[1,2048]{1,0:T(2,128)(2,1)S(1)}, u32[]{:S(2)}, u32[]{:S(2)}) collective-permute-start(bf16[1,2048]{1,0:T(2,128)(2,1)S(1)} %copy-done), channel_id=1, source_target_pairs={{0,2},{1,3},{2,0},{3,1},{4,6},{5,7},{6,4},{7,5},{8,10},{9,11},{10,... | collective-permute-start | bytes 12296 | tf_op jit(solution)/shard_map/ppermute | solution.py:616
  7.5 1.3 %collective-permute-start.5 = (bf16[1,2048]{1,0:T(2,128)(2,1)S(1)}, bf16[1,2048]{1,0:T(2,128)(2,1)S(1)}, u32[]{:S(2)}, u32[]{:S(2)}) collective-permute-start(bf16[1,2048]{1,0:T(2,128)(2,1)S(1)} %copy-done), channel_id=1, source_target_pairs={{0,18},{1,19},{2,16},{3,17},{16,2},{17,3},{18,0},{19,1},{4,22},{5,... | collective-permute-start | bytes 12296 | tf_op jit(solution)/shard_map/ppermute | solution.py:616
  8.8 0.2 collective-permute-start.4
  9.1 1.4 %collective-permute-done.2.refs_1_ = bf16[2,128,512]{2,1,0:T(8,128)(2,1)S(1)} collective-permute-done((bf16[2,128,512]{2,1,0:T(8,128)(2,1)S(1)}, bf16[2,128,512]{2,1,0:T(8,128)(2,1)S(1)}, u32[]{:S(2)}, u32[]{:S(2)}) %collective-permute-start.2) | collective-permute-done | bytes 262176 | tf_op jit(solution)/shard_map/ppermute | solution.py:603
  10.4 1.9 %collective-permute-start.8 = (bf16[2,128,512]{2,1,0:T(8,128)(2,1)S(1)}, bf16[2,128,512]{2,1,0:T(8,128)(2,1)S(1)}, u32[]{:S(2)}, u32[]{:S(2)}) collective-permute-start(bf16[2,128,512]{2,1,0:T(8,128)(2,1)S(1)} %collective-permute-done.2.refs_1_), channel_id=1, source_target_pairs={{0,1},{1,2},{2,3},{3,19},{19,18},{18,17},{17,16},{16,0},{4,5},{5,6... | collective-permute-start | bytes 786440 | tf_op jit(solution)/shard_map/ppermute | solution.py:603
  12.3 0.0 collective-permute-done.refs_2_
  12.3 0.1 collective-permute-start.1
  12.5 1.0 %collective-permute-done.3 = bf16[1,2048]{1,0:T(2,128)(2,1)S(1)} collective-permute-done((bf16[1,2048]{1,0:T(2,128)(2,1)S(1)}, bf16[1,2048]{1,0:T(2,128)(2,1)S(1)}, u32[]{:S(2)}, u32[]{:S(2)}) %collective-permute-start.3) | collective-permute-done | bytes 4128 | tf_op jit(solution)/shard_map/ppermute | solution.py:616
  13.4 0.0 collective-permute-done.5
  13.4 0.0 collective-permute-done.4
  13.5 1.4 %collective-permute-start.6 = (bf16[4,2048]{1,0:T(4,128)(2,1)S(1)}, bf16[4,2048]{1,0:T(4,128)(2,1)S(1)}, u32[]{:S(2)}, u32[]{:S(2)}) collective-permute-start(bf16[4,2048]{1,0:T(4,128)(2,1)S(1)} %pad_maximum_fusion.first_ref), channel_id=1, source_target_pairs={{0,1},{1,0},{2,3},{3,2},{4,5},{5,4},{6,7},{7,6},{8,9},{9,8},{10,11... | collective-permute-start | bytes 49160 | tf_op jit(solution)/shard_map/ppermute | solution.py:616
  14.8 1.8 %fold_blocks.3 = (f32[2,2,2,1024]{3,2,1,0:T(2,128)S(1)}, f32[2,2,128,1024]{3,2,1,0:T(8,128)S(1)}) custom-call(s32[2,128]{1,0:T(2,128)S(1)} %get-tuple-element.29.length_ref, bf16[2,128,2048]{2,1,0:T(8,128)(2,1)S(1)} %get-tuple-element.30.q_ref, bf16[2,128,512]{2,1,0:T(8,128)(2,1)S(1)} %get-tuple-element.31.refs_0_, ...), custom_call_target="tpu_custom_call" | custom-call | flops 805306368 | bytes 1048576 | tf_op jit(solution)/shard_map/fold_blocks/pallas_call | solution.py:314
  16.6 1.0 %collective-permute-done.8.refs_0_ = bf16[2,128,512]{2,1,0:T(8,128)(2,1)S(1)} collective-permute-done((bf16[2,128,512]{2,1,0:T(8,128)(2,1)S(1)}, bf16[2,128,512]{2,1,0:T(8,128)(2,1)S(1)}, u32[]{:S(2)}, u32[]{:S(2)}) %collective-permute-start.8) | collective-permute-done | bytes 262176 | tf_op jit(solution)/shard_map/ppermute | solution.py:603
  17.6 1.5 %collective-permute-start.13 = (bf16[2,128,512]{2,1,0:T(8,128)(2,1)S(1)}, bf16[2,128,512]{2,1,0:T(8,128)(2,1)S(1)}, u32[]{:S(2)}, u32[]{:S(2)}) collective-permute-start(bf16[2,128,512]{2,1,0:T(8,128)(2,1)S(1)} %collective-permute-done.8.refs_0_), channel_id=1, source_target_pairs={{0,1},{1,2},{2,3},{3,19},{19,18},{18,17},{17,16},{16,0},{4,5},{5,6... | collective-permute-start | bytes 786440 | tf_op jit(solution)/shard_map/ppermute | solution.py:603
  19.1 0.0 collective-permute-done.6.second_ref
  19.1 0.0 collective-permute-done.1.refs_1_
  19.2 0.5 %collective-permute-start.7 = (bf16[2,128,512]{2,1,0:T(8,128)(2,1)S(1)}, bf16[2,128,512]{2,1,0:T(8,128)(2,1)S(1)}, u32[]{:S(2)}, u32[]{:S(2)}) collective-permute-start(bf16[2,128,512]{2,1,0:T(8,128)(2,1)S(1)} %collective-permute-done.1.refs_1_), channel_id=1, source_target_pairs={{1,0},{2,1},{3,2},{19,3},{18,19},{17,18},{16,17},{0,16},{5,4},{6,5... | collective-permute-start | bytes 786440 | tf_op jit(solution)/shard_map/ppermute | solution.py:608
  19.7 0.1 collective-permute-start.11
  19.7 1.4 %collective-permute-start.10 = (bf16[8,2048]{1,0:T(8,128)(2,1)S(1)}, bf16[8,2048]{1,0:T(8,128)(2,1)S(1)}, u32[]{:S(2)}, u32[]{:S(2)}) collective-permute-start(bf16[8,2048]{1,0:T(8,128)(2,1)S(1)} %joined.1.refs_0_), channel_id=1, source_target_pairs={{0,8},{4,12},{8,0},{12,4},{1,9},{5,13},{9,1},{13,5},{2,10},{6,14},... | collective-permute-start | bytes 98312 | tf_op jit(solution)/shard_map/ppermute | solution.py:616
  21.2 0.4 %collective-permute-start.9 = (bf16[8,2048]{1,0:T(8,128)(2,1)S(1)}, bf16[8,2048]{1,0:T(8,128)(2,1)S(1)}, u32[]{:S(2)}, u32[]{:S(2)}) collective-permute-start(bf16[8,2048]{1,0:T(8,128)(2,1)S(1)} %joined.1.refs_0_), channel_id=1, source_target_pairs={{0,4},{4,0},{8,12},{12,8},{1,5},{5,1},{9,13},{13,9},{2,6},{6,2},{1... | collective-permute-start | bytes 98312 | tf_op jit(solution)/shard_map/ppermute | solution.py:616
  21.6 2.4 %collective-permute-done.13.refs_0_.block_ref = bf16[2,128,512]{2,1,0:T(8,128)(2,1)S(1)} collective-permute-done((bf16[2,128,512]{2,1,0:T(8,128)(2,1)S(1)}, bf16[2,128,512]{2,1,0:T(8,128)(2,1)S(1)}, u32[]{:S(2)}, u32[]{:S(2)}) %collective-permute-start.13) | collective-permute-done | bytes 262176 | tf_op jit(solution)/shard_map/ppermute | solution.py:603
  24.0 1.6 %collective-permute-start.14 = (bf16[1,128,512]{2,1,0:T(8,128)(2,1)S(1)}, bf16[1,128,512]{2,1,0:T(8,128)(2,1)S(1)}, u32[]{:S(2)}, u32[]{:S(2)}) collective-permute-start(bf16[1,128,512]{2,1,0:T(8,128)(2,1)S(1)} %half_of.3), channel_id=1, source_target_pairs={{0,1},{1,2},{2,3},{3,19},{19,18},{18,17},{17,16},{16,0},{4,5},{5,6... | collective-permute-start | bytes 393224 | tf_op jit(solution)/shard_map/ppermute | solution.py:603
  25.6 0.0 collective-permute-done.11.refs_3_
  25.6 0.0 collective-permute-done.10.refs_2_
  25.6 0.0 collective-permute-done.9.refs_1_
  25.6 0.0 collective-permute-done.7.block_ref.refs_1_
  25.6 0.5 %collective-permute-start.12 = (bf16[1,128,512]{2,1,0:T(8,128)(2,1)S(1)}, bf16[1,128,512]{2,1,0:T(8,128)(2,1)S(1)}, u32[]{:S(2)}, u32[]{:S(2)}) collective-permute-start(bf16[1,128,512]{2,1,0:T(8,128)(2,1)S(1)} %half_of.2), channel_id=1, source_target_pairs={{1,0},{2,1},{3,2},{19,3},{18,19},{17,18},{16,17},{0,16},{5,4},{6,5... | collective-permute-start | bytes 393224 | tf_op jit(solution)/shard_map/ppermute | solution.py:608
  26.2 0.7 %cross_attend.1.cross_ref = f32[2,2,128,1024]{3,2,1,0:T(8,128)S(1)} custom-call(f32[16,128]{1,0:T(8,128)S(1)} %get-tuple-element.39.factor_ref, bf16[2,128,2048]{2,1,0:T(8,128)(2,1)S(1)} %get-tuple-element.30.q_ref, bf16[8,2048]{1,0:T(8,128)(2,1)S(1)} %joined.1.refs_0_, bf16[8,2048]{1,0:T(8,128)(2,1)S(1)} %collective-permute-done.9.refs_1_, ...), custom_call_target="tpu_custom_call" | custom-call | flops 268435456 | bytes 1048576 | tf_op jit(solution)/shard_map/cross_attend/pallas_call | solution.py:350
  26.9 0.2 fold_blocks.5
  27.1 1.2 %early_rows.1._ = bf16[2,128,2048]{2,1,0:T(8,128)(2,1)} custom-call(bf16[2,128,2048]{2,1,0:T(8,128)(2,1)S(1)} %get-tuple-element.30.q_ref, f32[2,2,128,1024]{3,2,1,0:T(8,128)S(1)} %cross_attend.1.cross_ref, f32[2,2,2,1024]{3,2,1,0:T(2,128)S(1)} %get-tuple-element.42.stat_ref, f32[2,2,128,1024]{3,2,1,0:T(8,128)S(1)} %get-tuple-element.43.sum_ref), custom_call_target="tpu_custom_call" | custom-call | flops 67108864 | bytes 1048576 | tf_op jit(solution)/shard_map/early_rows/pallas_call | solution.py:413
  28.3 0.7 %collective-permute-done.14.block = bf16[1,128,512]{2,1,0:T(8,128)(2,1)S(1)} collective-permute-done((bf16[1,128,512]{2,1,0:T(8,128)(2,1)S(1)}, bf16[1,128,512]{2,1,0:T(8,128)(2,1)S(1)}, u32[]{:S(2)}, u32[]{:S(2)}) %collective-permute-start.14) | collective-permute-done | bytes 131104 | tf_op jit(solution)/shard_map/ppermute | solution.py:603
  29.0 1.6 %collective-permute-done.12.block = bf16[1,128,512]{2,1,0:T(8,128)(2,1)S(1)} collective-permute-done((bf16[1,128,512]{2,1,0:T(8,128)(2,1)S(1)}, bf16[1,128,512]{2,1,0:T(8,128)(2,1)S(1)}, u32[]{:S(2)}, u32[]{:S(2)}) %collective-permute-start.12) | collective-permute-done | bytes 131104 | tf_op jit(solution)/shard_map/ppermute | solution.py:608
  (8 shorter events, 0.2 us)
Async XLA Ops:
  0.0 4.5 %copy-start = (bf16[1,2048]{1,0:T(2,128)(2,1)S(1)}, bf16[1,2048]{1,0:T(2,128)(2,1)}, u32[]{:S(2)}) copy-start(bf16[1,2048]{1,0:T(2,128)(2,1)} %refs_3_.3) | copy-start | bytes 12292
  1.4 9.0 %collective-permute-start.2 = (bf16[2,128,512]{2,1,0:T(8,128)(2,1)S(1)}, bf16[2,128,512]{2,1,0:T(8,128)(2,1)S(1)}, u32[]{:S(2)}, u32[]{:S(2)}) collective-permute-start(bf16[2,128,512]{2,1,0:T(8,128)(2,1)S(1)} %get-tuple-element.31.refs_0_), channel_id=1, source_target_pairs={{0,1},{1,2},{2,3},{3,19},{19,18},{18,17},{17,16},{16,0},{4,5},{5,6... | collective-permute-start | bytes 786440 | tf_op jit(solution)/shard_map/ppermute | solution.py:603
  4.5 7.9 %collective-permute-start = (bf16[2,128,512]{2,1,0:T(8,128)(2,1)S(1)}, bf16[2,128,512]{2,1,0:T(8,128)(2,1)S(1)}, u32[]{:S(2)}, u32[]{:S(2)}) collective-permute-start(bf16[2,128,512]{2,1,0:T(8,128)(2,1)S(1)} %get-tuple-element.31.refs_0_), channel_id=1, source_target_pairs={{1,0},{2,1},{3,2},{19,3},{18,19},{17,18},{16,17},{0,16},{5,4},{6,5... | collective-permute-start | bytes 786440 | tf_op jit(solution)/shard_map/ppermute | solution.py:608
  4.5 8.9 %collective-permute-start.3 = (bf16[1,2048]{1,0:T(2,128)(2,1)S(1)}, bf16[1,2048]{1,0:T(2,128)(2,1)S(1)}, u32[]{:S(2)}, u32[]{:S(2)}) collective-permute-start(bf16[1,2048]{1,0:T(2,128)(2,1)S(1)} %copy-done), channel_id=1, source_target_pairs={{0,2},{1,3},{2,0},{3,1},{4,6},{5,7},{6,4},{7,5},{8,10},{9,11},{10,... | collective-permute-start | bytes 12296 | tf_op jit(solution)/shard_map/ppermute | solution.py:616
  7.5 5.9 %collective-permute-start.5 = (bf16[1,2048]{1,0:T(2,128)(2,1)S(1)}, bf16[1,2048]{1,0:T(2,128)(2,1)S(1)}, u32[]{:S(2)}, u32[]{:S(2)}) collective-permute-start(bf16[1,2048]{1,0:T(2,128)(2,1)S(1)} %copy-done), channel_id=1, source_target_pairs={{0,18},{1,19},{2,16},{3,17},{16,2},{17,3},{18,0},{19,1},{4,22},{5,... | collective-permute-start | bytes 12296 | tf_op jit(solution)/shard_map/ppermute | solution.py:616
  8.8 4.6 %collective-permute-start.4 = (bf16[1,2048]{1,0:T(2,128)(2,1)S(1)}, bf16[1,2048]{1,0:T(2,128)(2,1)S(1)}, u32[]{:S(2)}, u32[]{:S(2)}) collective-permute-start(bf16[1,2048]{1,0:T(2,128)(2,1)S(1)} %copy-done), channel_id=1, source_target_pairs={{0,16},{16,0},{1,17},{17,1},{2,18},{18,2},{3,19},{19,3},{4,20},{20... | collective-permute-start | bytes 12296 | tf_op jit(solution)/shard_map/ppermute | solution.py:616
  10.4 7.2 %collective-permute-start.8 = (bf16[2,128,512]{2,1,0:T(8,128)(2,1)S(1)}, bf16[2,128,512]{2,1,0:T(8,128)(2,1)S(1)}, u32[]{:S(2)}, u32[]{:S(2)}) collective-permute-start(bf16[2,128,512]{2,1,0:T(8,128)(2,1)S(1)} %collective-permute-done.2.refs_1_), channel_id=1, source_target_pairs={{0,1},{1,2},{2,3},{3,19},{19,18},{18,17},{17,16},{16,0},{4,5},{5,6... | collective-permute-start | bytes 786440 | tf_op jit(solution)/shard_map/ppermute | solution.py:603
  12.3 6.8 %collective-permute-start.1 = (bf16[2,128,512]{2,1,0:T(8,128)(2,1)S(1)}, bf16[2,128,512]{2,1,0:T(8,128)(2,1)S(1)}, u32[]{:S(2)}, u32[]{:S(2)}) collective-permute-start(bf16[2,128,512]{2,1,0:T(8,128)(2,1)S(1)} %collective-permute-done.refs_2_), channel_id=1, source_target_pairs={{1,0},{2,1},{3,2},{19,3},{18,19},{17,18},{16,17},{0,16},{5,4},{6,5... | collective-permute-start | bytes 786440 | tf_op jit(solution)/shard_map/ppermute | solution.py:608
  13.5 5.7 %collective-permute-start.6 = (bf16[4,2048]{1,0:T(4,128)(2,1)S(1)}, bf16[4,2048]{1,0:T(4,128)(2,1)S(1)}, u32[]{:S(2)}, u32[]{:S(2)}) collective-permute-start(bf16[4,2048]{1,0:T(4,128)(2,1)S(1)} %pad_maximum_fusion.first_ref), channel_id=1, source_target_pairs={{0,1},{1,0},{2,3},{3,2},{4,5},{5,4},{6,7},{7,6},{8,9},{9,8},{10,11... | collective-permute-start | bytes 49160 | tf_op jit(solution)/shard_map/ppermute | solution.py:616
  17.6 6.4 %collective-permute-start.13 = (bf16[2,128,512]{2,1,0:T(8,128)(2,1)S(1)}, bf16[2,128,512]{2,1,0:T(8,128)(2,1)S(1)}, u32[]{:S(2)}, u32[]{:S(2)}) collective-permute-start(bf16[2,128,512]{2,1,0:T(8,128)(2,1)S(1)} %collective-permute-done.8.refs_0_), channel_id=1, source_target_pairs={{0,1},{1,2},{2,3},{3,19},{19,18},{18,17},{17,16},{16,0},{4,5},{5,6... | collective-permute-start | bytes 786440 | tf_op jit(solution)/shard_map/ppermute | solution.py:603
  19.2 6.4 %collective-permute-start.7 = (bf16[2,128,512]{2,1,0:T(8,128)(2,1)S(1)}, bf16[2,128,512]{2,1,0:T(8,128)(2,1)S(1)}, u32[]{:S(2)}, u32[]{:S(2)}) collective-permute-start(bf16[2,128,512]{2,1,0:T(8,128)(2,1)S(1)} %collective-permute-done.1.refs_1_), channel_id=1, source_target_pairs={{1,0},{2,1},{3,2},{19,3},{18,19},{17,18},{16,17},{0,16},{5,4},{6,5... | collective-permute-start | bytes 786440 | tf_op jit(solution)/shard_map/ppermute | solution.py:608
  19.7 5.9 %collective-permute-start.11 = (bf16[8,2048]{1,0:T(8,128)(2,1)S(1)}, bf16[8,2048]{1,0:T(8,128)(2,1)S(1)}, u32[]{:S(2)}, u32[]{:S(2)}) collective-permute-start(bf16[8,2048]{1,0:T(8,128)(2,1)S(1)} %joined.1.refs_0_), channel_id=1, source_target_pairs={{0,12},{4,8},{8,4},{12,0},{1,13},{5,9},{9,5},{13,1},{2,14},{6,10},... | collective-permute-start | bytes 98312 | tf_op jit(solution)/shard_map/ppermute | solution.py:616
  19.7 5.8 %collective-permute-start.10 = (bf16[8,2048]{1,0:T(8,128)(2,1)S(1)}, bf16[8,2048]{1,0:T(8,128)(2,1)S(1)}, u32[]{:S(2)}, u32[]{:S(2)}) collective-permute-start(bf16[8,2048]{1,0:T(8,128)(2,1)S(1)} %joined.1.refs_0_), channel_id=1, source_target_pairs={{0,8},{4,12},{8,0},{12,4},{1,9},{5,13},{9,1},{13,5},{2,10},{6,14},... | collective-permute-start | bytes 98312 | tf_op jit(solution)/shard_map/ppermute | solution.py:616
  21.2 4.4 %collective-permute-start.9 = (bf16[8,2048]{1,0:T(8,128)(2,1)S(1)}, bf16[8,2048]{1,0:T(8,128)(2,1)S(1)}, u32[]{:S(2)}, u32[]{:S(2)}) collective-permute-start(bf16[8,2048]{1,0:T(8,128)(2,1)S(1)} %joined.1.refs_0_), channel_id=1, source_target_pairs={{0,4},{4,0},{8,12},{12,8},{1,5},{5,1},{9,13},{13,9},{2,6},{6,2},{1... | collective-permute-start | bytes 98312 | tf_op jit(solution)/shard_map/ppermute | solution.py:616
  24.0 5.0 %collective-permute-start.14 = (bf16[1,128,512]{2,1,0:T(8,128)(2,1)S(1)}, bf16[1,128,512]{2,1,0:T(8,128)(2,1)S(1)}, u32[]{:S(2)}, u32[]{:S(2)}) collective-permute-start(bf16[1,128,512]{2,1,0:T(8,128)(2,1)S(1)} %half_of.3), channel_id=1, source_target_pairs={{0,1},{1,2},{2,3},{3,19},{19,18},{18,17},{17,16},{16,0},{4,5},{5,6... | collective-permute-start | bytes 393224 | tf_op jit(solution)/shard_map/ppermute | solution.py:603
  25.6 5.0 %collective-permute-start.12 = (bf16[1,128,512]{2,1,0:T(8,128)(2,1)S(1)}, bf16[1,128,512]{2,1,0:T(8,128)(2,1)S(1)}, u32[]{:S(2)}, u32[]{:S(2)}) collective-permute-start(bf16[1,128,512]{2,1,0:T(8,128)(2,1)S(1)} %half_of.2), channel_id=1, source_target_pairs={{1,0},{2,1},{3,2},{19,3},{18,19},{17,18},{16,17},{0,16},{5,4},{6,5... | collective-permute-start | bytes 393224 | tf_op jit(solution)/shard_map/ppermute | solution.py:608
